TPU v7x, 32 devices: a whole 2x2x4 slice. The times are simulated.
32 devices in a mesh: row: 4 (over y, x), col: 8 (over z, core).
Axes of the slice: x: 2, y: 2, z: 4, core: 2. Of those that a mesh axis runs over, the one named last changes fastest.
Arguments:
- features: float32 [2, 64, 512, 128], P(None, 'row', 'col'), may hold values from -6 to 6
- cotangent: float32 [2, 64, 512, 128], P(None, 'row', 'col'), may hold values from -6 to 6
- conv_kernel: float32 [7, 7, 128], P(None, None, ('row', 'col')), may hold values from -0.875 to 0.875
- conv_bias: float32 [128], P(('row', 'col')), may hold values from -3 to 3
- norm_gain: float32 [128], P(('row', 'col')), may hold values from 0.1 to 1.9
- norm_shift: float32 [128], P(('row', 'col')), may hold values from -2 to 2
- w_in: float32 [128, 512], P(None, ('row', 'col')), may hold values from -0.5 to 0.5
- in_bias: float32 [512], P(('row', 'col')), may hold values from -3 to 3
- w_out: float32 [512, 128], P(('row', 'col')), may hold values from -0.25 to 0.25
- out_bias: float32 [128], P(('row', 'col')), may hold values from -3 to 3
- layer_scale: float32 [128], P(('row', 'col')), may hold values from 0.5 to 1.5
Outputs:
- features_grad: float32 [2, 64, 512, 128], P(None, 'row', 'col')
- kernel_grad: float32 [7, 7, 128], P(None, None, ('row', 'col'))
- conv_bias_grad: float32 [128], P(('row', 'col'))
- gain_grad: float32 [128], P(('row', 'col'))
- shift_grad: float32 [128], P(('row', 'col'))
- w_in_grad: float32 [128, 512], P(None, ('row', 'col'))
- in_bias_grad: float32 [512], P(('row', 'col'))
- w_out_grad: float32 [512, 128], P(('row', 'col'))
- out_bias_grad: float32 [128], P(('row', 'col'))
- scale_grad: float32 [128], P(('row', 'col'))
All inputs are finite; a program needn't handle non-finite values.
Results may differ from a plain program's by a relative error of at most 0.0003.
Values sent between devices are 32-bit elements; how exact they have to be, the bound alone decides.
No kernel may reach another device: no remote copies, remote signals or barrier semaphores. Data moves between devices by JAX's collectives and lax.ppermute only.
A program may use at most 64 MiB of HBM per device.

v0:
```python
import functools
import math

import jax
import jax.numpy as jnp
from jax import lax
from jax.experimental import pallas as pl
from jax.experimental.pallas import tpu as pltpu
from jax.sharding import PartitionSpec as P

norm_eps = 1e-06
inverse_root_twopi = 0.3989422804014327
half_log2e = 0.7213475204444817
tail_p = 0.275
tail_c = (
    0.1178092510180382,
    0.04211149421929024,
    0.3339322641039753,
    -0.33099338058058636,
    0.45199870802757525,
    -0.11485833206946416,
)
AXES = ("row", "col")
LANES = 128
LEFT = 8
NN = (((1,), (0,)), ((), ()))
NT = (((1,), (1,)), ((), ()))
f32, bf16 = jnp.float32, jnp.bfloat16


def ceil8(n):
    return (n + 7) // 8 * 8


def call(body, outs, scratch=(), flops=0, size=0, limit=8, **more):
    return pl.pallas_call(
        body,
        out_shape=outs,
        scratch_shapes=list(scratch),
        compiler_params=pltpu.CompilerParams(vmem_limit_bytes=limit and limit * 1024 * 1024),
        **more,
        cost_estimate=pl.CostEstimate(flops=flops, bytes_accessed=size, transcendentals=0),
    )


def shape(*dims):
    return jax.ShapeDtypeStruct(dims, f32)


def device_index(mesh_shape):
    return lax.axis_index("row") * mesh_shape["col"] + lax.axis_index("col")


def split(x):
    high = x.astype(bf16)
    return high, (x - high.astype(f32)).astype(bf16)


def dot(a, b, dims):
    return lax.dot_general(a, b, dims, preferred_element_type=f32)


def exchange_order(x, unit, count, me):
    rows = x.shape[0]
    index = lax.broadcasted_iota(jnp.int32, x.shape, 0)
    step = unit
    bit = 1
    while bit < count:
        up = pltpu.roll(x, step, 0)
        down = pltpu.roll(x, rows - step, 0)
        swapped = jnp.where((index & step) != 0, up, down)
        x = jnp.where((me & bit) != 0, swapped, x)
        step *= 2
        bit *= 2
    return x


def pairs(count, second):
    if not second:
        return [(i, i ^ 1) for i in range(count)]
    return [(i, (i + 1 if i % 2 else i - 1) % count) for i in range(count)]


def both_pairs(a, b, axis):
    count = lax.axis_size(axis)
    return lax.ppermute(a, axis, pairs(count, False)), lax.ppermute(b, axis, pairs(count, True))


def even(axis):
    return lax.axis_index(axis) % 2 == 0


def true_neighbour(ms, axis):
    i = lax.axis_index(axis)
    return jnp.where(i % 2 == 0, i > 0, i < ms[axis] - 1)


def start_body(feat, kernel_hbm, cb, ng, ns, ob, ls, win_hbm, ib, wout_hbm, out_ref, row_a, row_b,
               kernel_scr, v0, v1, v2, v3, v4, ib_scr, win_scr, wout_scr, sems):
    batch, rows, cols, C = feat.shape
    taps_i, cs, taps_j = kernel_hbm.shape
    hs = win_hbm.shape[0]
    taps = taps_i * taps_j
    m = taps_i // 2
    even_r = even("row")
    far = jnp.where(even_r, rows - m, 0)
    near = jnp.where(even_r, 0, rows - m)
    vectors = (v0, v1, v2, v3, v4)
    moves = [(kernel_hbm, kernel_scr), (win_hbm, win_scr), (wout_hbm, wout_scr), (ib, ib_scr)]
    moves += list(zip((cb, ng, ns, ob, ls), vectors))
    moves += [(feat.at[:, pl.ds(far, m)], row_a), (feat.at[:, pl.ds(near, m)], row_b)]
    copies = [pltpu.make_async_copy(src, dst, sems.at[n]) for n, (src, dst) in enumerate(moves)]
    for copy in copies:
        copy.start()
    out_ref[...] = jnp.zeros_like(out_ref)
    for copy in copies:
        copy.wait()
    out_ref[0:hs, :] = win_scr[...]
    out_ref[hs : 2 * hs, :] = wout_scr[...]
    base = 2 * hs
    for i in range(taps_i):
        out_ref[base : base + cs, i * taps_j : (i + 1) * taps_j] = kernel_scr[i]
    for n, ref in enumerate(vectors):
        column = jnp.broadcast_to(ref[...], (8, cs)).T
        out_ref[base : base + cs, taps + n : taps + n + 1] = column[:, 0:1]
    out_ref[base + cs : base + cs + 1, 0:hs] = ib_scr[...]


def with_corners(ms, edge_a, edge_b, got_a, got_b, out_a, out_b):
    batch, rows, m, C = edge_a.shape
    cols = got_a.shape[2]
    even_r, even_c = even("row"), even("col")
    out_a[:, m : m + rows, 0:m] = edge_a[...]
    out_b[:, m : m + rows, 0:m] = edge_b[...]
    true_r = true_neighbour(ms, "row")
    for got, end, keep in ((got_a, even_r, None), (got_b, jnp.logical_not(even_r), true_r)):
        at = jnp.where(end, rows + m, 0)
        last, first = got[:, :, cols - m :], got[:, :, 0:m]
        x, y = jnp.where(even_c, last, first), jnp.where(even_c, first, last)
        if keep is not None:
            x, y = jnp.where(keep, x, 0.0), jnp.where(keep, y, 0.0)
        out_a[:, pl.ds(at, m), 0:m] = x
        out_b[:, pl.ds(at, m), 0:m] = y


def first_join_body(ms, inner, got_a, got_b, *refs):
    parts, (slots, out_a, out_b, edge_a, edge_b) = refs[:-5], refs[-5:]
    cols, m = inner.shape[2], got_a.shape[1]
    even_c = even("col")
    first, last = inner[:, :, 0:m], inner[:, :, cols - m :]
    edge_a[...] = jnp.where(even_c, last, first)
    edge_b[...] = jnp.where(even_c, first, last)
    with_corners(ms, edge_a, edge_b, got_a, got_b, out_a, out_b)
    n = 0
    for part in parts:
        slots[n : n + part.shape[0]] = part[...]
        n += part.shape[0]


def message_body(waited, halo, *refs):
    parts, message = refs[:-1], refs[-1]
    n = 0
    for part in parts:
        for k in range(part.shape[0]):
            message[n : n + part.shape[1], :] = part[k]
            n += part.shape[1]
    batch, rows, m, _ = halo.shape
    step = (message.shape[0] - n) // (batch * rows)
    for b in range(batch):
        for r in range(rows):
            message[n : n + m, :] = halo[b, r]
            n += step


def back_join_body(ms, edge_a, edge_b, got_a, got_b, large, large_got, small, small_got, *refs):
    out_a, out_b = refs[-2:]
    rows = large.shape[1]
    n = 0
    for out in refs[:-2]:
        count = out.shape[0]
        out[:, 0:rows] = large[n : n + count] + large_got[n : n + count]
        out[:, rows:] = small[n : n + count] + small_got[n : n + count]
        n += count
    with_corners(ms, edge_a, edge_b, got_a, got_b, out_a, out_b)


def differences(src, out):
    for b in range(src.shape[0]):
        out[b] = src[b, 0 : src.shape[1] - 1] - src[b, 1:]


def pair_sums(weight, taps_i, taps_j, out):
    for a in range((taps_i + 1) // 2):
        for j in range(taps_j):
            w = weight(2 * a, j)
            if 2 * a + 1 < taps_i:
                w = w + weight(2 * a + 1, j)
            out[a * taps_j + j] = w


def depthwise_block(read, diff, weight, sums, rows, taps_i, taps_j, start):
    def add(total, k, term):
        total[k] = term if total[k] is None else total[k] + term

    n, n0, n1 = rows // 2, (taps_i + 1) // 2, taps_i // 2
    both, even_rows, odd_rows = [None] * n, list(start[0::2]), list(start[1::2])
    for j in range(taps_j):
        w0 = [weight(2 * a, j) for a in range(n0)]
        w1 = [weight(2 * a + 1, j) for a in range(n1)]
        ws = [sums(a, j) for a in range(n0)]
        for r in range(n + n0 - 1):
            x, d = read(2 * r + 1, j), diff(2 * r, j)
            for a in range(n0):
                if 0 <= r - a < n:
                    add(both, r - a, ws[a] * x)
                    add(even_rows, r - a, w0[a] * d)
        for r in range(n + n1 - 1):
            d = diff(2 * r + 1, j)
            for a in range(n1):
                if 0 <= r - a < n:
                    odd_rows[r - a] = odd_rows[r - a] - w1[a] * d
    out = []
    for k in range(n):
        out += [both[k] + even_rows[k], both[k] + odd_rows[k]]
    return out


def fill(ms, dst, inner, row_a, row_b, col_a, col_b):
    batch, rows, cols, _ = inner.shape
    m = row_a.shape[1]
    even_r, even_c = even("row"), even("col")
    true_r, true_c = true_neighbour(ms, "row"), true_neighbour(ms, "col")
    at_a = jnp.where(even_r, rows + m, 0)
    at_b = jnp.where(even_r, 0, rows + m)
    for b in range(batch):
        dst[b, m : m + rows, LEFT : LEFT + cols, :] = inner[b]
        dst[b, pl.ds(at_a, m), LEFT : LEFT + cols, :] = row_a[b]
        dst[b, pl.ds(at_b, m), LEFT : LEFT + cols, :] = jnp.where(true_r, row_b[b], 0.0)
        for r in range(rows + 2 * m):
            x, y = col_a(b, r), jnp.where(true_c, col_b[b, r, 0:m], 0.0)
            dst[b, r, LEFT - m : LEFT, :] = jnp.where(even_c, y, x)
            dst[b, r, LEFT + cols : LEFT + cols + m, :] = jnp.where(even_c, x, y)


def small_columns(read, hs, cs, count, me, order, scratch):
    for s in range(count):
        scratch[order[s] * cs : (order[s] + 1) * cs, :] = read(s, 2 * hs, cs)
    return exchange_order(scratch[...], cs, count, me)


def mix_body(
    ms, order, factor, taps_i, taps_j, tile,
    feat, got_ra, got_rb, got_cb, kept, got, cot_ref,
    src_ref, dconv_ref, row_a, row_b, edge_a, edge_b, grads_ref, chan_ref, small_ref,
    conv_scr, diff_scr, cols_scr, kb_scr, ks_scr, win_scr, wout_scr, w1_scr, w2_scr, w4_scr, bias_scr,
    gw1_scr, gw2_scr, gb_scr, gg_scr, gs_scr, gc_scr, cot_sum,
):
    batch, rows, cols, C = feat.shape
    count = len(order)
    cs = C // count
    taps = taps_i * taps_j
    m = taps_i // 2
    hid = win_scr.shape[0]
    hs = hid // count
    me = device_index(ms)
    half = count // 2
    slot = 2 * hs + 8
    step_rows = (got.shape[0] - half * slot) // (batch * (rows + 2 * m))

    def read(s, first, size):
        at = (s % half) * slot + first
        return (kept if s < half else got)[at : at + size, :]

    def col_a(b, r):
        at = half * slot + (b * (rows + 2 * m) + r) * step_rows
        return got[at : at + m, :]

    fill(ms, src_ref, feat, got_ra, got_rb, col_a, got_cb)
    columns = small_columns(read, hs, cs, count, me, order, cols_scr)
    cols_scr[...] = columns
    rows_form = columns.T
    small_ref[...] = rows_form
    for t in range(taps):
        kb_scr[t] = jnp.broadcast_to(rows_form[t : t + 1, :], (8, C))
    conv_bias = jnp.broadcast_to(rows_form[taps : taps + 1, :], (8, C))

    for s in range(count):
        win_scr[s * hs : (s + 1) * hs, :] = read(s, 0, hs)
        wout_scr[s * hs : (s + 1) * hs, :] = read(s, hs, hs)
    for s in range(count):
        cols_bias = jnp.broadcast_to(read(s, 2 * hs + cs, 1), (LANES, LANES)).T
        bias_scr[s * hs : (s + 1) * hs, :] = cols_bias[0:hs, :]

    scale_row = rows_form[taps + 4 : taps + 5, :]
    wh, wl = split(win_scr[...])
    w1_scr[:, 0:C] = wh
    w1_scr[:, C : 2 * C] = wl
    w1_scr[:, 2 * C : 3 * C] = wh
    oh, ol = split(wout_scr[...] * scale_row)
    w2_scr[:, 0:C] = oh
    w2_scr[:, C : 2 * C] = ol
    w2_scr[:, 2 * C : 3 * C] = oh
    th, tl = split(win_scr[...].T)
    w4_scr[0:C, :] = th
    w4_scr[C : 2 * C, :] = tl

    differences(src_ref, diff_scr)
    weight = lambda i, j: kb_scr[i * taps_j + j]
    pair_sums(weight, taps_i, taps_j, ks_scr)

    def conv_step(b, _):
        for q in range(0, cols, 8):
            acc = depthwise_block(
                lambda r, j: src_ref[b, r, LEFT - m + q + j : LEFT - m + q + j + 8, :],
                lambda r, j: diff_scr[b, r, LEFT - m + q + j : LEFT - m + q + j + 8, :],
                weight, lambda a, j: ks_scr[a * taps_j + j],
                rows, taps_i, taps_j, [conv_bias] * rows,
            )
            for p in range(rows):
                conv_scr[b, p, q : q + 8, :] = acc[p]
        return 0

    lax.fori_loop(0, batch, conv_step, 0)

    for ref in (gw1_scr, gw2_scr, gb_scr, gg_scr, gs_scr, gc_scr, cot_sum):
        ref[...] = jnp.zeros_like(ref)
    tile_rows = tile // cols
    per_image = rows // tile_rows
    gain = cols_scr[:, taps + 1 : taps + 2]
    shift = cols_scr[:, taps + 2 : taps + 3]

    def lanes_sum(x):
        total = x[:, 0:LANES]
        for k in range(LANES, x.shape[1], LANES):
            total = total + x[:, k : k + LANES]
        return total

    def step(t, _):
        b = t // per_image
        p0 = (t % per_image) * tile_rows
        x = conv_scr[b, pl.ds(p0, tile_rows)].reshape(tile, C).T
        mean = jnp.mean(x, axis=0, keepdims=True)
        centred = x - mean
        variance = jnp.mean(centred * centred, axis=0, keepdims=True)
        inverse = lax.rsqrt(variance + norm_eps)
        normed = centred * inverse
        lin = normed * gain + shift
        lh, ll = split(lin)
        cot = cot_ref[b, pl.ds(p0, tile_rows)].reshape(tile, C)
        ch, cl = split(cot)
        act = dot(w1_scr[...], jnp.concatenate([lh, lh, ll], axis=0), NN)
        d_hid = dot(w2_scr[...], jnp.concatenate([ch, ch, cl], axis=1), NT)
        bias = bias_scr[...]
        act = act + jnp.concatenate([bias] * (tile // LANES), axis=1)
        e = jnp.exp2((act * act) * (-half_log2e))
        d = 1.0 + tail_p * jnp.abs(act)
        r = pltpu.reciprocal(d, approx=True)
        r = r * (2.0 - d * r)
        q = tail_c[5] * r + tail_c[4]
        for k in (3, 2, 1, 0):
            q = q * r + tail_c[k]
        q = q * r * e
        phi = jnp.where(act > 0, 1.0 - q, q)
        hidden = act * phi
        d_act = d_hid * (phi + act * e * inverse_root_twopi)
        hh, hl = split(hidden)
        dh, dl = split(d_act)
        gb_scr[...] += lanes_sum(d_act)
        both = dot(w4_scr[...], dh, NN)
        d_lin = both[0:C] + both[C : 2 * C] + dot(w4_scr[0:C, :], dl, NN)
        gw1_scr[...] += dot(dh, jnp.concatenate([lh, ll], axis=0), NT)
        gw1_scr[:, 0:C] += dot(dl, lh, NT)
        gw2_scr[...] += dot(hh, jnp.concatenate([ch, cl], axis=1), NN)
        gw2_scr[:, 0:C] += dot(hl, ch, NN)
        gg_scr[...] += lanes_sum(d_lin * normed)
        gs_scr[...] += lanes_sum(d_lin)
        d_norm = d_lin * gain
        d_conv = inverse * (
            d_norm
            - jnp.mean(d_norm, axis=0, keepdims=True)
            - normed * jnp.mean(d_norm * normed, axis=0, keepdims=True)
        )
        gc_scr[...] += lanes_sum(d_conv)
        dconv_ref[b, pl.ds(p0, tile_rows)] = d_conv.T.reshape(tile_rows, cols, C)
        cot_sum[...] += jnp.sum(cot.reshape(tile // 8, 8, C), axis=0)
        return 0

    lax.fori_loop(0, batch * per_image, step, 0)

    even_r, even_c = even("row"), even("col")
    row_a[...] = dconv_ref[:, pl.ds(jnp.where(even_r, rows - m, 0), m)]
    row_b[...] = dconv_ref[:, pl.ds(jnp.where(even_r, 0, rows - m), m)]
    first, last = dconv_ref[:, :, 0:m], dconv_ref[:, :, cols - m : cols]
    edge_a[...] = jnp.where(even_c, last, first)
    edge_b[...] = jnp.where(even_c, first, last)

    h = gw2_scr[:, 0:C] + gw2_scr[:, C : 2 * C]
    gw1 = (gw1_scr[:, 0:C] + gw1_scr[:, C : 2 * C]) * factor
    gw2 = h * (scale_row * factor)
    gb = (jnp.sum(gb_scr[...].T, axis=0, keepdims=True)) * factor
    for s in range(count):
        grads_ref[s, 0:hs, :] = gw1[s * hs : (s + 1) * hs, :]
        grads_ref[s, hs : 2 * hs, :] = gw2[s * hs : (s + 1) * hs, :]
    total = jnp.sum(cot_sum[...], axis=0, keepdims=True)
    outb = rows_form[taps + 3 : taps + 4, :]
    scale_grad = jnp.sum(h * wout_scr[...], axis=0, keepdims=True) + outb * total
    chan_ref[...] = jnp.zeros_like(chan_ref)
    chan_ref[0:1, 0:C] = jnp.sum(gc_scr[...].T, axis=0, keepdims=True) * factor
    chan_ref[1:2, 0:C] = jnp.sum(gg_scr[...].T, axis=0, keepdims=True) * factor
    chan_ref[2:3, 0:C] = jnp.sum(gs_scr[...].T, axis=0, keepdims=True) * factor
    chan_ref[3:4, 0:C] = total * scale_row * factor
    chan_ref[4:5, 0:C] = scale_grad * factor
    chan_ref[5:6, :] = gb


def kernel_grad_body(ms, order, factor, taps_i, taps_j, count, src_ref, dconv_ref, chan_ref, out_ref, acc_scr, rows_scr, diff_scr, sum_scr):
    batch, rows, cols, C = dconv_ref.shape
    m = taps_i // 2
    taps = taps_i * taps_j
    cs = C // count
    me = device_index(ms)
    n, n0, n1 = rows // 2, (taps_i + 1) // 2, taps_i // 2
    acc_scr[...] = jnp.zeros_like(acc_scr)
    differences(src_ref, diff_scr)
    for b in range(batch):
        for k in range(n):
            sum_scr[b, k] = dconv_ref[b, 2 * k] + dconv_ref[b, 2 * k + 1]

    def step(b, _):
        for j in range(taps_j):
            both = [jnp.zeros((8, C), f32)] * n0
            first = [acc_scr[2 * a * taps_j + j] for a in range(n0)]
            second = [acc_scr[(2 * a + 1) * taps_j + j] for a in range(n1)]
            for q in range(0, cols, 8):
                own, at = pl.ds(q, 8), pl.ds(LEFT - m + q + j, 8)
                ds = [sum_scr[b, k, own, :] for k in range(n)]
                d0 = [dconv_ref[b, 2 * k, own, :] for k in range(n)]
                d1 = [dconv_ref[b, 2 * k + 1, own, :] for k in range(n)]
                for r in range(n + n0 - 1):
                    x, d = src_ref[b, 2 * r + 1, at, :], diff_scr[b, 2 * r, at, :]
                    for a in range(n0):
                        if 0 <= r - a < n:
                            both[a] = both[a] + ds[r - a] * x
                            first[a] = first[a] + d0[r - a] * d
                for r in range(n + n1 - 1):
                    d = diff_scr[b, 2 * r + 1, at, :]
                    for a in range(n1):
                        if 0 <= r - a < n:
                            second[a] = second[a] - d1[r - a] * d
            for a in range(n0):
                acc_scr[2 * a * taps_j + j] = first[a] + both[a]
            for a in range(n1):
                acc_scr[(2 * a + 1) * taps_j + j] = second[a] + both[a]
        return 0

    lax.fori_loop(0, batch, step, 0)
    rows_scr[...] = jnp.zeros_like(rows_scr)
    for t in range(taps):
        rows_scr[t : t + 1, :] = jnp.sum(acc_scr[t], axis=0, keepdims=True) * factor
    rows_scr[taps : taps + 5, :] = chan_ref[0:5, 0:C]
    columns = exchange_order(rows_scr[...].T, cs, count, me)
    out_ref[...] = jnp.zeros_like(out_ref)
    hs = chan_ref.shape[1] // count
    for s in range(count):
        out_ref[s, 0:cs, :] = columns[order[s] * cs : (order[s] + 1) * cs, :]
        out_ref[s, cs : cs + 1, 0:hs] = chan_ref[5:6, s * hs : (s + 1) * hs]


def features_grad_body(ms, taps_i, taps_j, inner, got_ra, got_rb, got_ca, got_cb, small_ref, cot_ref, out_ref, ext_scr, diff_scr, kb_scr, ks_scr):
    batch, rows, cols, C = inner.shape
    m = taps_i // 2
    taps = taps_i * taps_j
    fill(ms, ext_scr, inner, got_ra, got_rb, lambda b, r: got_ca[b, r, 0 : taps_i // 2], got_cb)
    for t in range(taps):
        kb_scr[t] = jnp.broadcast_to(small_ref[t : t + 1, :], (8, C))

    differences(ext_scr, diff_scr)
    weight = lambda i, j: kb_scr[taps - 1 - (i * taps_j + j)]
    pair_sums(weight, taps_i, taps_j, ks_scr)

    def step(b, _):
        for q in range(0, cols, 8):
            acc = depthwise_block(
                lambda r, j: ext_scr[b, r, LEFT - m + q + j : LEFT - m + q + j + 8, :],
                lambda r, j: diff_scr[b, r, LEFT - m + q + j : LEFT - m + q + j + 8, :],
                weight, lambda a, j: ks_scr[a * taps_j + j],
                rows, taps_i, taps_j, [cot_ref[b, p, q : q + 8, :] for p in range(rows)],
            )
            for p in range(rows):
                out_ref[b, p, q : q + 8, :] = acc[p]
        return 0

    lax.fori_loop(0, batch, step, 0)


def finish_body(taps_i, taps_j, cs, hs, *refs):
    parts, outs = refs[:-9], refs[-9:]
    total = parts[0][...]
    for part in parts[1:]:
        total = total + part[...]
    kernel_out, cb, ng, ns, win_out, ib, wout_out, ob, ls = outs
    taps = taps_i * taps_j
    win_out[...] = total[0:hs, :]
    wout_out[...] = total[hs : 2 * hs, :]
    small = total[2 * hs : 2 * hs + 8, :]
    for i in range(taps_i):
        kernel_out[i] = small[0:cs, i * taps_j : (i + 1) * taps_j]
    flipped = small.T
    for n, ref in enumerate((cb, ng, ns, ob, ls)):
        ref[...] = flipped[taps + n : taps + n + 1, 0:cs]
    ib[...] = small[cs : cs + 1, 0:hs]


def flip(x, mask, count):
    return lax.ppermute(x, AXES, [(i, i ^ mask) for i in range(count)])


def groups_of(ms):
    bits_col = ms["col"].bit_length() - 1
    bits_row = ms["row"].bit_length() - 1
    col = [1 << k for k in range(bits_col)]
    row = [1 << (k + bits_col) for k in range(bits_row)]
    rest = col[1:]
    out = [rest[k : k + 2] for k in range(0, len(rest), 2)]
    out += [row[k : k + 2] for k in range(0, len(row), 2)]
    return out + [col[:1]]


def masks(group):
    out = [0]
    for bit in group:
        out += [bit ^ x for x in out]
    return out


def per_device(ms, features, cotangent, conv_kernel, conv_bias, norm_gain, norm_shift, w_in, in_bias, w_out, out_bias, layer_scale):
    batch, rows, cols, C = features.shape
    taps_i, taps_j, cs = conv_kernel.shape
    hs = w_out.shape[0]
    count = ms["row"] * ms["col"]
    hid = hs * count
    m = taps_i // 2
    taps = taps_i * taps_j
    cells = batch * rows * cols * count
    factor = 1.0 / math.sqrt(cells)
    slot = 2 * hs + 8
    wide = ceil8(LEFT + cols + m)

    vm = pltpu.VMEM
    vectors = [v.reshape(1, cs) for v in (conv_bias, norm_gain, norm_shift, out_bias, layer_scale)]
    block, row_a, row_b = call(
        start_body,
        (
            shape(slot, LANES),
            *(shape(batch, m, cols, C) for _ in range(2)),
        ),
        scratch=(
            vm((taps_i, cs, taps_j), f32),
            *(vm((1, cs), f32) for _ in range(5)),
            vm((1, hs), f32),
            vm((hs, C), f32),
            vm((hs, C), f32),
            pltpu.SemaphoreType.DMA((11,)),
        ),
        size=10**6,
        limit=None,
        in_specs=[pl.BlockSpec(memory_space=pl.ANY)] * 10,
    )(features, conv_kernel.transpose(0, 2, 1), *vectors, w_in.T, in_bias.reshape(1, hs), w_out)

    wide_m = (m + 3) // 4 * 4
    edges = (shape(batch, rows + 2 * m, m, C), shape(batch, rows + 2 * m, wide_m, C))
    anywhere, in_vmem = pl.BlockSpec(memory_space=pl.ANY), pl.BlockSpec(memory_space=pltpu.VMEM)
    groups = groups_of(ms)
    order = [0]
    got_ra, got_rb = both_pairs(row_a, row_b, "row")
    parts = [block[None]]
    for n, group in enumerate(groups[:-1]):
        if n == 1:
            slots, edge_a, edge_b = call(
                functools.partial(first_join_body, ms),
                (shape(len(order), slot, LANES), *edges),
                scratch=[vm((batch, rows, m, C), f32) for _ in range(2)],
            )(features, got_ra, got_rb, *parts)
            got_cb = lax.ppermute(edge_b, "col", pairs(ms["col"], True))
        else:
            slots = jnp.concatenate(parts)
        parts = [slots] + [flip(slots, mask, count) for mask in masks(group)[1:]]
        order = [mask ^ x for mask in masks(group) for x in order]
    half = count // 2
    message = call(
        message_body,
        shape(half * slot + edges[0].shape[0] * edges[0].shape[1] * wide_m, LANES),
        in_specs=[anywhere] + [in_vmem] * (1 + len(parts)),
    )(got_cb, edge_a, *parts)
    last = groups[-1][0]
    order += [last ^ x for x in order]
    got = flip(message, last, count)
    tile = 8 * cols
    src, dconv, d_row_a, d_row_b, d_edge_a, d_edge_b, grads, chan, small = call(
        functools.partial(mix_body, ms, order, factor, taps_i, taps_j, tile),
        (
            shape(batch, rows + 2 * m, wide, C),
            shape(batch, rows, cols, C),
            *(shape(batch, m, cols, C) for _ in range(2)),
            *(shape(batch, rows, m, C) for _ in range(2)),
            shape(count, 2 * hs, C),
            shape(8, hid),
            shape(LANES, C),
        ),
        scratch=(
            vm((batch, rows, cols, C), f32),
            vm((batch, rows + 2 * m - 1, wide, C), f32),
            vm((C, LANES), f32),
            vm((taps, 8, C), f32),
            vm(((taps_i + 1) // 2 * taps_j, 8, C), f32),
            vm((hid, C), f32),
            vm((hid, C), f32),
            vm((hid, 3 * C), bf16),
            vm((hid, 3 * C), bf16),
            vm((2 * C, hid), bf16),
            vm((hid, LANES), f32),
            vm((hid, 2 * C), f32),
            vm((hid, 2 * C), f32),
            vm((hid, LANES), f32),
            vm((C, LANES), f32),
            vm((C, LANES), f32),
            vm((C, LANES), f32),
            vm((8, C), f32),
        ),
        flops=12 * 10**9,
        size=8 * 10**6,
        limit=24,
    )(features, got_ra, got_rb, got_cb, message, got, cotangent)

    d_got_ra, d_got_rb = both_pairs(d_row_a, d_row_b, "row")
    large_got = flip(grads[half:], last, count)
    smalls = call(
        functools.partial(kernel_grad_body, ms, order, factor, taps_i, taps_j, count),
        shape(count, 8, LANES),
        scratch=(
            vm((taps, 8, C), f32),
            vm((LANES, C), f32),
            vm((batch, rows + 2 * m - 1, wide, C), f32),
            vm((batch, rows // 2, cols, C), f32),
        ),
        flops=4 * 10**9,
        size=4 * 10**6,
    )(src, dconv, chan)
    small_got = flip(smalls[half:], last, count)
    ways = len(masks(groups[-2]))
    *parts, edge_a, edge_b = call(
        functools.partial(back_join_body, ms),
        (*(shape(half // ways, slot, LANES) for _ in range(ways)), edges[1], edges[1]),
    )(d_edge_a, d_edge_b, d_got_ra, d_got_rb, grads, large_got, smalls, small_got)
    d_got_ca, d_got_cb = both_pairs(edge_a, edge_b, "col")
    for n, group in reversed(list(enumerate(groups[:-1]))):
        parts = [parts[0]] + [flip(part, mask, count) for part, mask in zip(parts[1:], masks(group)[1:])]
        if n:
            whole = parts[0]
            for part in parts[1:]:
                whole = whole + part
            ways = len(masks(groups[n - 1]))
            step = whole.shape[0] // ways
            parts = [whole[k * step : (k + 1) * step] for k in range(ways)]

    features_grad = call(
        functools.partial(features_grad_body, ms, taps_i, taps_j),
        shape(batch, rows, cols, C),
        scratch=(
            vm((batch, rows + 2 * m, wide, C), f32),
            vm((batch, rows + 2 * m - 1, wide, C), f32),
            vm((taps, 8, C), f32),
            vm(((taps_i + 1) // 2 * taps_j, 8, C), f32),
        ),
        flops=4 * 10**9,
        size=4 * 10**6,
    )(dconv, d_got_ra, d_got_rb, d_got_ca, d_got_cb, small, cotangent)

    outs = call(
        functools.partial(finish_body, taps_i, taps_j, cs, hs),
        (
            shape(taps_i, cs, taps_j),
            *(shape(1, cs) for _ in range(3)),
            shape(hs, C),
            shape(1, hs),
            shape(hs, C),
            *(shape(1, cs) for _ in range(2)),
        ),
        size=100000,
    )(*(p.reshape(slot, LANES) for p in parts))
    kernel_grad, cb, ng, ns, win, ib, wout, ob, ls = outs
    return (
        features_grad,
        kernel_grad.transpose(0, 2, 1),
        cb.reshape(cs),
        ng.reshape(cs),
        ns.reshape(cs),
        win.T,
        ib.reshape(hs),
        wout,
        ob.reshape(cs),
        ls.reshape(cs),
    )


def solution(mesh):
    both = P(AXES)
    tiles = P(None, "row", "col", None)
    in_specs = (
        tiles, tiles, P(None, None, AXES), both, both, both, P(None, AXES), both, P(AXES, None), both, both,
    )
    out_specs = (
        tiles, P(None, None, AXES), both, both, both, P(None, AXES), both, P(AXES, None), both, both,
    )
    return jax.shard_map(
        functools.partial(per_device, dict(mesh.shape)),
        mesh=mesh, in_specs=in_specs, out_specs=out_specs, check_vma=False,
    )
```

profile of v0, /device:TPU:0, one launch (start us, length us, event | category | flops | bytes accessed | tf_op | source)
XLA Modules:
  0.0 74.7 jit_solution(1958160209045332185)
XLA Ops:
  0.7 2.1 %shard_map.186 = (f32[40,128]{1,0:T(8,128)}, f32[2,3,64,128]{3,2,1,0:T(8,128)}, f32[2,3,64,128]{3,2,1,0:T(8,128)}) custom-call(f32[2,16,64,128]{3,2,1,0:T(8,128)} %feat.3, f32[7,4,7]{2,1,0:T(4,128)} %bitcast.29, f32[1,4]{1,0:T(1,128)} %bitcast.31, f32[1,4]{1,0:T(1,128)} %bitcast.32, f32[1,4]{1,0:T(1,128)} %bitcast.33, f32[1,4]{1,0:T(1,128)} %bitcast.34, ...), custom_call_target="tpu_custom_call" | custom-call | bytes 1000000 | tf_op jit(solution)/shard_map/pallas_call | solution.py:551
  2.7 3.0 %collective-permute-start = (f32[2,3,64,128]{3,2,1,0:T(8,128)}, f32[2,3,64,128]{3,2,1,0:T(8,128)S(1)}, u32[]{:S(2)}, u32[]{:S(2)}) collective-permute-start(f32[2,3,64,128]{3,2,1,0:T(8,128)} %get-tuple-element.40), channel_id=1, source_target_pairs={{0,8},{8,0},{16,24},{24,16},{1,9},{9,1},{17,25},{25,17},{2,10},{10... | collective-permute-start | bytes 589832 | tf_op jit(solution)/shard_map/ppermute | solution.py:86
  5.7 1.5 %collective-permute-start.1 = (f32[2,3,64,128]{3,2,1,0:T(8,128)}, f32[2,3,64,128]{3,2,1,0:T(8,128)S(1)}, u32[]{:S(2)}, u32[]{:S(2)}) collective-permute-start(f32[2,3,64,128]{3,2,1,0:T(8,128)} %get-tuple-element.41), channel_id=1, source_target_pairs={{0,24},{8,16},{16,8},{24,0},{1,25},{9,17},{17,9},{25,1},{2,26},{10... | collective-permute-start | bytes 589832 | tf_op jit(solution)/shard_map/ppermute | solution.py:86
  7.2 3.6 %collective-permute-start.4 = (f32[1,40,128]{2,1,0:T(8,128)}, f32[1,40,128]{2,1,0:T(8,128)S(1)}, u32[]{:S(2)}, u32[]{:S(2)}) collective-permute-start(f32[1,40,128]{2,1,0:T(8,128)} %bitcast.25), channel_id=1, source_target_pairs={{0,6},{1,7},{2,4},{3,5},{4,2},{5,3},{6,0},{7,1},{8,14},{9,15},{10,... | collective-permute-start | bytes 61448 | tf_op jit(solution)/shard_map/ppermute | solution.py:515
  11.6 1.5 %collective-permute-done.4.refs_3_ = f32[1,40,128]{2,1,0:T(8,128)S(1)} collective-permute-done((f32[1,40,128]{2,1,0:T(8,128)}, f32[1,40,128]{2,1,0:T(8,128)S(1)}, u32[]{:S(2)}, u32[]{:S(2)}) %collective-permute-start.4) | collective-permute-done | bytes 20512 | tf_op jit(solution)/shard_map/ppermute | solution.py:515
  13.1 2.7 %collective-permute-done.3.refs_2_ = f32[1,40,128]{2,1,0:T(8,128)S(1)} collective-permute-done((f32[1,40,128]{2,1,0:T(8,128)}, f32[1,40,128]{2,1,0:T(8,128)S(1)}, u32[]{:S(2)}, u32[]{:S(2)}) %collective-permute-start.3) | collective-permute-done | bytes 20512 | tf_op jit(solution)/shard_map/ppermute | solution.py:515
  17.1 2.2 %collective-permute-start.5 = (f32[2,22,4,128]{3,2,1,0:T(4,128)S(1)}, f32[2,22,4,128]{3,2,1,0:T(4,128)S(1)}, u32[]{:S(2)}, u32[]{:S(2)}) collective-permute-start(f32[2,22,4,128]{3,2,1,0:T(4,128)S(1)} %get-tuple-element.43), channel_id=1, source_target_pairs={{0,7},{1,2},{2,1},{3,4},{4,3},{5,6},{6,5},{7,0},{8,15},{9,10},{10,... | collective-permute-start | bytes 270344 | tf_op jit(solution)/shard_map/ppermute | solution.py:584
  19.3 1.4 %collective-permute-start.8 = (f32[4,40,128]{2,1,0:T(8,128)S(1)}, f32[4,40,128]{2,1,0:T(8,128)S(1)}, u32[]{:S(2)}, u32[]{:S(2)}) collective-permute-start(f32[4,40,128]{2,1,0:T(8,128)S(1)} %get-tuple-element.45.refs_0_), channel_id=1, source_target_pairs={{0,24},{1,25},{2,26},{3,27},{4,28},{5,29},{6,30},{7,31},{8,16},{9,... | collective-permute-start | bytes 245768 | tf_op jit(solution)/shard_map/ppermute | solution.py:515
  20.8 1.5 %collective-permute-start.7 = (f32[4,40,128]{2,1,0:T(8,128)S(1)}, f32[4,40,128]{2,1,0:T(8,128)S(1)}, u32[]{:S(2)}, u32[]{:S(2)}) collective-permute-start(f32[4,40,128]{2,1,0:T(8,128)S(1)} %get-tuple-element.45.refs_0_), channel_id=1, source_target_pairs={{0,16},{1,17},{2,18},{3,19},{4,20},{5,21},{6,22},{7,23},{8,24},{9,... | collective-permute-start | bytes 245768 | tf_op jit(solution)/shard_map/ppermute | solution.py:515
  22.8 2.7 %collective-permute-done.8.refs_3_ = f32[4,40,128]{2,1,0:T(8,128)S(1)} collective-permute-done((f32[4,40,128]{2,1,0:T(8,128)S(1)}, f32[4,40,128]{2,1,0:T(8,128)S(1)}, u32[]{:S(2)}, u32[]{:S(2)}) %collective-permute-start.8) | collective-permute-done | bytes 81952 | tf_op jit(solution)/shard_map/ppermute | solution.py:515
  25.8 0.9 %collective-permute-done.6.refs_1_ = f32[4,40,128]{2,1,0:T(8,128)S(1)} collective-permute-done((f32[4,40,128]{2,1,0:T(8,128)S(1)}, f32[4,40,128]{2,1,0:T(8,128)S(1)}, u32[]{:S(2)}, u32[]{:S(2)}) %collective-permute-start.6) | collective-permute-done | bytes 81952 | tf_op jit(solution)/shard_map/ppermute | solution.py:515
  26.8 1.7 %collective-permute-done.9.got = f32[816,128]{1,0:T(8,128)S(1)} collective-permute-done((f32[816,128]{1,0:T(8,128)S(1)}, f32[816,128]{1,0:T(8,128)S(1)}, u32[]{:S(2)}, u32[]{:S(2)}) %collective-permute-start.9) | collective-permute-done | bytes 417824 | tf_op jit(solution)/shard_map/ppermute | solution.py:515
  28.6 16.7 %shard_map.189 = (f32[2,22,80,128]{3,2,1,0:T(8,128)S(1)}, f32[2,16,64,128]{3,2,1,0:T(8,128)S(1)}, f32[2,3,64,128]{3,2,1,0:T(8,128)S(1)}, f32[2,3,64,128]{3,2,1,0...) custom-call(f32[2,16,64,128]{3,2,1,0:T(8,128)S(1)} %copy-done, ...), custom_call_target="tpu_custom_call" | custom-call | flops 12000000000 | bytes 8000000 | tf_op jit(solution)/shard_map/pallas_call | solution.py:599
  45.9 1.4 %collective-permute-start.11 = (f32[2,3,64,128]{3,2,1,0:T(8,128)S(1)}, f32[2,3,64,128]{3,2,1,0:T(8,128)S(1)}, u32[]{:S(2)}, u32[]{:S(2)}) collective-permute-start(f32[2,3,64,128]{3,2,1,0:T(8,128)S(1)} %get-tuple-element.48), channel_id=1, source_target_pairs={{0,24},{8,16},{16,8},{24,0},{1,25},{9,17},{17,9},{25,1},{2,26},{10... | collective-permute-start | bytes 589832 | tf_op jit(solution)/shard_map/ppermute | solution.py:86
  47.4 6.7 %shard_map.190.small = f32[32,8,128]{2,1,0:T(8,128)S(1)} custom-call(f32[2,22,80,128]{3,2,1,0:T(8,128)S(1)} %get-tuple-element.52.src_ref, f32[2,16,64,128]{3,2,1,0:T(8,128)S(1)} %get-tuple-element.46.dconv_ref.inner, f32[8,512]{1,0:T(8,128)S(1)} %get-tuple-element.53.chan_ref), custom_call_target="tpu_custom_call" | custom-call | flops 4000000000 | bytes 4000000 | tf_op jit(solution)/shard_map/pallas_call | solution.py:637
  54.6 0.9 %collective-permute-done.13.small_got = f32[16,8,128]{2,1,0:T(8,128)S(1)} collective-permute-done((f32[16,8,128]{2,1,0:T(8,128)S(1)}, f32[16,8,128]{2,1,0:T(8,128)S(1)}, u32[]{:S(2)}, u32[]{:S(2)}) %collective-permute-start.13) | collective-permute-done | bytes 65568 | tf_op jit(solution)/shard_map/ppermute | solution.py:515
  55.5 0.9 %collective-permute-done.11.got_b.got_rb = f32[2,3,64,128]{3,2,1,0:T(8,128)S(1)} collective-permute-done((f32[2,3,64,128]{3,2,1,0:T(8,128)S(1)}, f32[2,3,64,128]{3,2,1,0:T(8,128)S(1)}, u32[]{:S(2)}, u32[]{:S(2)}) %collective-permute-start.11) | collective-permute-done | bytes 196640 | tf_op jit(solution)/shard_map/ppermute | solution.py:86
  57.3 1.4 %collective-permute-start.17 = (f32[4,40,128]{2,1,0:T(8,128)S(1)}, f32[4,40,128]{2,1,0:T(8,128)S(1)}, u32[]{:S(2)}, u32[]{:S(2)}) collective-permute-start(f32[4,40,128]{2,1,0:T(8,128)S(1)} %get-tuple-element.59), channel_id=1, source_target_pairs={{0,16},{1,17},{2,18},{3,19},{4,20},{5,21},{6,22},{7,23},{8,24},{9,... | collective-permute-start | bytes 245768 | tf_op jit(solution)/shard_map/ppermute | solution.py:515
  58.6 1.4 %collective-permute-start.18 = (f32[4,40,128]{2,1,0:T(8,128)S(1)}, f32[4,40,128]{2,1,0:T(8,128)S(1)}, u32[]{:S(2)}, u32[]{:S(2)}) collective-permute-start(f32[4,40,128]{2,1,0:T(8,128)S(1)} %get-tuple-element.60), channel_id=1, source_target_pairs={{0,24},{1,25},{2,26},{3,27},{4,28},{5,29},{6,30},{7,31},{8,16},{9,... | collective-permute-start | bytes 245768 | tf_op jit(solution)/shard_map/ppermute | solution.py:515
  60.1 1.6 %collective-permute-start.15 = (f32[2,22,4,128]{3,2,1,0:T(4,128)S(1)}, f32[2,22,4,128]{3,2,1,0:T(4,128)S(1)}, u32[]{:S(2)}, u32[]{:S(2)}) collective-permute-start(f32[2,22,4,128]{3,2,1,0:T(4,128)S(1)} %get-tuple-element.55), channel_id=1, source_target_pairs={{0,7},{1,2},{2,1},{3,4},{4,3},{5,6},{6,5},{7,0},{8,15},{9,10},{10,... | collective-permute-start | bytes 270344 | tf_op jit(solution)/shard_map/ppermute | solution.py:86
  62.4 1.5 %collective-permute-done.18 = f32[4,40,128]{2,1,0:T(8,128)S(1)} collective-permute-done((f32[4,40,128]{2,1,0:T(8,128)S(1)}, f32[4,40,128]{2,1,0:T(8,128)S(1)}, u32[]{:S(2)}, u32[]{:S(2)}) %collective-permute-start.18) | collective-permute-done | bytes 81952 | tf_op jit(solution)/shard_map/ppermute | solution.py:515
  64.0 1.6 %collective-permute-start.21 = (f32[1,40,128]{2,1,0:T(8,128)S(1)}, f32[1,40,128]{2,1,0:T(8,128)S(1)}, u32[]{:S(2)}, u32[]{:S(2)}) collective-permute-start(f32[1,40,128]{2,1,0:T(8,128)S(1)} %get-tuple-element.70), channel_id=1, source_target_pairs={{0,6},{1,7},{2,4},{3,5},{4,2},{5,3},{6,0},{7,1},{8,14},{9,15},{10,... | collective-permute-start | bytes 61448 | tf_op jit(solution)/shard_map/ppermute | solution.py:515
  65.9 2.6 %collective-permute-start.19 = (f32[1,40,128]{2,1,0:T(8,128)S(1)}, f32[1,40,128]{2,1,0:T(8,128)S(1)}, u32[]{:S(2)}, u32[]{:S(2)}) collective-permute-start(f32[1,40,128]{2,1,0:T(8,128)S(1)} %get-tuple-element.72), channel_id=1, source_target_pairs={{0,2},{1,3},{2,0},{3,1},{4,6},{5,7},{6,4},{7,5},{8,10},{9,11},{10,... | collective-permute-start | bytes 61448 | tf_op jit(solution)/shard_map/ppermute | solution.py:515
  68.5 5.4 %shard_map.192 = f32[2,16,64,128]{3,2,1,0:T(8,128)} custom-call(f32[2,16,64,128]{3,2,1,0:T(8,128)S(1)} %get-tuple-element.46.dconv_ref.inner, f32[2,3,64,128]{3,2,1,0:T(8,128)S(1)} %collective-permute-done.10.got_a.got_ra, f32[2,3,64,128]{3,2,1,0:T(8,128)S(1)} %collective-permute-done.11.got_b.got_rb, f32[2,22,4,128]{3,2,1,0:T(4,128)S(1)} %collective-permute-done.14.got_ca, ...), custom_call_target="tpu_custom_call" | custom-call | flops 4000000000 | bytes 4000000 | tf_op jit(solution)/shard_map/pallas_call | solution.py:666
  (38 shorter events, 7.0 us)
Async XLA Ops:
  0.6 15.6 %copy-start = (f32[2,16,64,128]{3,2,1,0:T(8,128)S(1)}, f32[2,16,64,128]{3,2,1,0:T(8,128)}, u32[]{:S(2)}) copy-start(f32[2,16,64,128]{3,2,1,0:T(8,128)} %feat.3) | copy-start | bytes 3145732
  2.7 13.0 %collective-permute-start = (f32[2,3,64,128]{3,2,1,0:T(8,128)}, f32[2,3,64,128]{3,2,1,0:T(8,128)S(1)}, u32[]{:S(2)}, u32[]{:S(2)}) collective-permute-start(f32[2,3,64,128]{3,2,1,0:T(8,128)} %get-tuple-element.40), channel_id=1, source_target_pairs={{0,8},{8,0},{16,24},{24,16},{1,9},{9,1},{17,25},{25,17},{2,10},{10... | collective-permute-start | bytes 589832 | tf_op jit(solution)/shard_map/ppermute | solution.py:86
  5.7 10.5 %collective-permute-start.1 = (f32[2,3,64,128]{3,2,1,0:T(8,128)}, f32[2,3,64,128]{3,2,1,0:T(8,128)S(1)}, u32[]{:S(2)}, u32[]{:S(2)}) collective-permute-start(f32[2,3,64,128]{3,2,1,0:T(8,128)} %get-tuple-element.41), channel_id=1, source_target_pairs={{0,24},{8,16},{16,8},{24,0},{1,25},{9,17},{17,9},{25,1},{2,26},{10... | collective-permute-start | bytes 589832 | tf_op jit(solution)/shard_map/ppermute | solution.py:86
  7.2 5.8 %collective-permute-start.4 = (f32[1,40,128]{2,1,0:T(8,128)}, f32[1,40,128]{2,1,0:T(8,128)S(1)}, u32[]{:S(2)}, u32[]{:S(2)}) collective-permute-start(f32[1,40,128]{2,1,0:T(8,128)} %bitcast.25), channel_id=1, source_target_pairs={{0,6},{1,7},{2,4},{3,5},{4,2},{5,3},{6,0},{7,1},{8,14},{9,15},{10,... | collective-permute-start | bytes 61448 | tf_op jit(solution)/shard_map/ppermute | solution.py:515
  10.8 4.9 %collective-permute-start.3 = (f32[1,40,128]{2,1,0:T(8,128)}, f32[1,40,128]{2,1,0:T(8,128)S(1)}, u32[]{:S(2)}, u32[]{:S(2)}) collective-permute-start(f32[1,40,128]{2,1,0:T(8,128)} %bitcast.26), channel_id=1, source_target_pairs={{0,4},{1,5},{2,6},{3,7},{4,0},{5,1},{6,2},{7,3},{8,12},{9,13},{10,... | collective-permute-start | bytes 61448 | tf_op jit(solution)/shard_map/ppermute | solution.py:515
  10.8 4.9 %collective-permute-start.2 = (f32[1,40,128]{2,1,0:T(8,128)}, f32[1,40,128]{2,1,0:T(8,128)S(1)}, u32[]{:S(2)}, u32[]{:S(2)}) collective-permute-start(f32[1,40,128]{2,1,0:T(8,128)} %bitcast.27), channel_id=1, source_target_pairs={{0,2},{1,3},{2,0},{3,1},{4,6},{5,7},{6,4},{7,5},{8,10},{9,11},{10,... | collective-permute-start | bytes 61448 | tf_op jit(solution)/shard_map/ppermute | solution.py:515
  17.0 11.6 %copy-start.2 = (f32[2,16,64,128]{3,2,1,0:T(8,128)S(1)}, f32[2,16,64,128]{3,2,1,0:T(8,128)}, u32[]{:S(2)}) copy-start(f32[2,16,64,128]{3,2,1,0:T(8,128)} %cot_ref.3) | copy-start | bytes 3145732
  17.1 9.6 %collective-permute-start.5 = (f32[2,22,4,128]{3,2,1,0:T(4,128)S(1)}, f32[2,22,4,128]{3,2,1,0:T(4,128)S(1)}, u32[]{:S(2)}, u32[]{:S(2)}) collective-permute-start(f32[2,22,4,128]{3,2,1,0:T(4,128)S(1)} %get-tuple-element.43), channel_id=1, source_target_pairs={{0,7},{1,2},{2,1},{3,4},{4,3},{5,6},{6,5},{7,0},{8,15},{9,10},{10,... | collective-permute-start | bytes 270344 | tf_op jit(solution)/shard_map/ppermute | solution.py:584
  19.3 6.2 %collective-permute-start.8 = (f32[4,40,128]{2,1,0:T(8,128)S(1)}, f32[4,40,128]{2,1,0:T(8,128)S(1)}, u32[]{:S(2)}, u32[]{:S(2)}) collective-permute-start(f32[4,40,128]{2,1,0:T(8,128)S(1)} %get-tuple-element.45.refs_0_), channel_id=1, source_target_pairs={{0,24},{1,25},{2,26},{3,27},{4,28},{5,29},{6,30},{7,31},{8,16},{9,... | collective-permute-start | bytes 245768 | tf_op jit(solution)/shard_map/ppermute | solution.py:515
  20.8 5.1 %collective-permute-start.7 = (f32[4,40,128]{2,1,0:T(8,128)S(1)}, f32[4,40,128]{2,1,0:T(8,128)S(1)}, u32[]{:S(2)}, u32[]{:S(2)}) collective-permute-start(f32[4,40,128]{2,1,0:T(8,128)S(1)} %get-tuple-element.45.refs_0_), channel_id=1, source_target_pairs={{0,16},{1,17},{2,18},{3,19},{4,20},{5,21},{6,22},{7,23},{8,24},{9,... | collective-permute-start | bytes 245768 | tf_op jit(solution)/shard_map/ppermute | solution.py:515
  22.3 4.4 %collective-permute-start.6 = (f32[4,40,128]{2,1,0:T(8,128)S(1)}, f32[4,40,128]{2,1,0:T(8,128)S(1)}, u32[]{:S(2)}, u32[]{:S(2)}) collective-permute-start(f32[4,40,128]{2,1,0:T(8,128)S(1)} %get-tuple-element.45.refs_0_), channel_id=1, source_target_pairs={{0,8},{1,9},{2,10},{3,11},{4,12},{5,13},{6,14},{7,15},{8,0},{9,1},... | collective-permute-start | bytes 245768 | tf_op jit(solution)/shard_map/ppermute | solution.py:515
  26.8 1.8 %collective-permute-start.9 = (f32[816,128]{1,0:T(8,128)S(1)}, f32[816,128]{1,0:T(8,128)S(1)}, u32[]{:S(2)}, u32[]{:S(2)}) collective-permute-start(f32[816,128]{1,0:T(8,128)S(1)} %shard_map.188.kept), channel_id=1, source_target_pairs={{0,1},{1,0},{2,3},{3,2},{4,5},{5,4},{6,7},{7,6},{8,9},{9,8},{10,11... | collective-permute-start | bytes 1253384 | tf_op jit(solution)/shard_map/ppermute | solution.py:515
  45.3 10.3 %collective-permute-start.10 = (f32[2,3,64,128]{3,2,1,0:T(8,128)S(1)}, f32[2,3,64,128]{3,2,1,0:T(8,128)S(1)}, u32[]{:S(2)}, u32[]{:S(2)}) collective-permute-start(f32[2,3,64,128]{3,2,1,0:T(8,128)S(1)} %get-tuple-element.47), channel_id=1, source_target_pairs={{0,8},{8,0},{16,24},{24,16},{1,9},{9,1},{17,25},{25,17},{2,10},{10... | collective-permute-start | bytes 589832 | tf_op jit(solution)/shard_map/ppermute | solution.py:86
  45.9 10.6 %collective-permute-start.11 = (f32[2,3,64,128]{3,2,1,0:T(8,128)S(1)}, f32[2,3,64,128]{3,2,1,0:T(8,128)S(1)}, u32[]{:S(2)}, u32[]{:S(2)}) collective-permute-start(f32[2,3,64,128]{3,2,1,0:T(8,128)S(1)} %get-tuple-element.48), channel_id=1, source_target_pairs={{0,24},{8,16},{16,8},{24,0},{1,25},{9,17},{17,9},{25,1},{2,26},{10... | collective-permute-start | bytes 589832 | tf_op jit(solution)/shard_map/ppermute | solution.py:86
  47.3 9.1 %collective-permute-start.12 = (f32[16,32,128]{2,1,0:T(8,128)S(1)}, f32[16,32,128]{2,1,0:T(8,128)S(1)}, u32[]{:S(2)}, u32[]{:S(2)}) collective-permute-start(f32[16,32,128]{2,1,0:T(8,128)S(1)} %slice.18), channel_id=1, source_target_pairs={{0,1},{1,0},{2,3},{3,2},{4,5},{5,4},{6,7},{7,6},{8,9},{9,8},{10,11... | collective-permute-start | bytes 786440 | tf_op jit(solution)/shard_map/ppermute | solution.py:515
  54.1 1.5 %collective-permute-start.13 = (f32[16,8,128]{2,1,0:T(8,128)S(1)}, f32[16,8,128]{2,1,0:T(8,128)S(1)}, u32[]{:S(2)}, u32[]{:S(2)}) collective-permute-start(f32[16,8,128]{2,1,0:T(8,128)S(1)} %slice.24), channel_id=1, source_target_pairs={{0,1},{1,0},{2,3},{3,2},{4,5},{5,4},{6,7},{7,6},{8,9},{9,8},{10,11... | collective-permute-start | bytes 196616 | tf_op jit(solution)/shard_map/ppermute | solution.py:515
  56.5 5.3 %collective-permute-start.16 = (f32[4,40,128]{2,1,0:T(8,128)S(1)}, f32[4,40,128]{2,1,0:T(8,128)S(1)}, u32[]{:S(2)}, u32[]{:S(2)}) collective-permute-start(f32[4,40,128]{2,1,0:T(8,128)S(1)} %get-tuple-element.58), channel_id=1, source_target_pairs={{0,8},{1,9},{2,10},{3,11},{4,12},{5,13},{6,14},{7,15},{8,0},{9,1},... | collective-permute-start | bytes 245768 | tf_op jit(solution)/shard_map/ppermute | solution.py:515
  57.3 5.2 %collective-permute-start.17 = (f32[4,40,128]{2,1,0:T(8,128)S(1)}, f32[4,40,128]{2,1,0:T(8,128)S(1)}, u32[]{:S(2)}, u32[]{:S(2)}) collective-permute-start(f32[4,40,128]{2,1,0:T(8,128)S(1)} %get-tuple-element.59), channel_id=1, source_target_pairs={{0,16},{1,17},{2,18},{3,19},{4,20},{5,21},{6,22},{7,23},{8,24},{9,... | collective-permute-start | bytes 245768 | tf_op jit(solution)/shard_map/ppermute | solution.py:515
  58.6 5.3 %collective-permute-start.18 = (f32[4,40,128]{2,1,0:T(8,128)S(1)}, f32[4,40,128]{2,1,0:T(8,128)S(1)}, u32[]{:S(2)}, u32[]{:S(2)}) collective-permute-start(f32[4,40,128]{2,1,0:T(8,128)S(1)} %get-tuple-element.60), channel_id=1, source_target_pairs={{0,24},{1,25},{2,26},{3,27},{4,28},{5,29},{6,30},{7,31},{8,16},{9,... | collective-permute-start | bytes 245768 | tf_op jit(solution)/shard_map/ppermute | solution.py:515
  60.1 8.4 %collective-permute-start.14 = (f32[2,22,4,128]{3,2,1,0:T(4,128)S(1)}, f32[2,22,4,128]{3,2,1,0:T(4,128)S(1)}, u32[]{:S(2)}, u32[]{:S(2)}) collective-permute-start(f32[2,22,4,128]{3,2,1,0:T(4,128)S(1)} %get-tuple-element.54), channel_id=1, source_target_pairs={{0,1},{1,0},{2,3},{3,2},{4,5},{5,4},{6,7},{7,6},{8,9},{9,8},{10,11... | collective-permute-start | bytes 270344 | tf_op jit(solution)/shard_map/ppermute | solution.py:86
  60.1 8.4 %collective-permute-start.15 = (f32[2,22,4,128]{3,2,1,0:T(4,128)S(1)}, f32[2,22,4,128]{3,2,1,0:T(4,128)S(1)}, u32[]{:S(2)}, u32[]{:S(2)}) collective-permute-start(f32[2,22,4,128]{3,2,1,0:T(4,128)S(1)} %get-tuple-element.55), channel_id=1, source_target_pairs={{0,7},{1,2},{2,1},{3,4},{4,3},{5,6},{6,5},{7,0},{8,15},{9,10},{10,... | collective-permute-start | bytes 270344 | tf_op jit(solution)/shard_map/ppermute | solution.py:86
  64.0 9.9 %collective-permute-start.21 = (f32[1,40,128]{2,1,0:T(8,128)S(1)}, f32[1,40,128]{2,1,0:T(8,128)S(1)}, u32[]{:S(2)}, u32[]{:S(2)}) collective-permute-start(f32[1,40,128]{2,1,0:T(8,128)S(1)} %get-tuple-element.70), channel_id=1, source_target_pairs={{0,6},{1,7},{2,4},{3,5},{4,2},{5,3},{6,0},{7,1},{8,14},{9,15},{10,... | collective-permute-start | bytes 61448 | tf_op jit(solution)/shard_map/ppermute | solution.py:515
  65.6 8.3 %collective-permute-start.20 = (f32[1,40,128]{2,1,0:T(8,128)S(1)}, f32[1,40,128]{2,1,0:T(8,128)S(1)}, u32[]{:S(2)}, u32[]{:S(2)}) collective-permute-start(f32[1,40,128]{2,1,0:T(8,128)S(1)} %get-tuple-element.71), channel_id=1, source_target_pairs={{0,4},{1,5},{2,6},{3,7},{4,0},{5,1},{6,2},{7,3},{8,12},{9,13},{10,... | collective-permute-start | bytes 61448 | tf_op jit(solution)/shard_map/ppermute | solution.py:515
  65.9 8.1 %collective-permute-start.19 = (f32[1,40,128]{2,1,0:T(8,128)S(1)}, f32[1,40,128]{2,1,0:T(8,128)S(1)}, u32[]{:S(2)}, u32[]{:S(2)}) collective-permute-start(f32[1,40,128]{2,1,0:T(8,128)S(1)} %get-tuple-element.72), channel_id=1, source_target_pairs={{0,2},{1,3},{2,0},{3,1},{4,6},{5,7},{6,4},{7,5},{8,10},{9,11},{10,... | collective-permute-start | bytes 61448 | tf_op jit(solution)/shard_map/ppermute | solution.py:515
  (1 other events, 0.7 us)
where the time goes:
time: 74.9 us; the launch traced here: 74.7 us
  Pallas kernels  31.8 us (42%)
  starting transfers between devices  27 us (36%)
  waiting for transfers between devices  14.4 us (19%)
  local copies, waits for them, and re-layouts  0.77 us (1%)
    pallas_call x1, Pallas kernels, per_device(): call(functools.partial(mix_body, ms, order, factor, taps_i, taps_j, tile)...  16.7 us
    ppermute x15, starting transfers between devices, flip(): return lax.ppermute(x, AXES, [(i, i ^ mask) for i in range(count)])  16.6 us
    ppermute x15, waiting for transfers between devices, flip(): return lax.ppermute(x, AXES, [(i, i ^ mask) for i in range(count)])  12.9 us
    pallas_call x1, Pallas kernels, per_device(): call(functools.partial(kernel_grad_body, ms, order, factor, taps_i, taps_...  6.65 us
    pallas_call x1, Pallas kernels, per_device(): call(functools.partial(features_grad_body, ms, taps_i, taps_j), shape(bat...  5.44 us
    ppermute x3, starting transfers between devices, both_pairs(): lax.ppermute(b, axis, pairs(count, True))  4.55 us
    ppermute x3, starting transfers between devices, both_pairs(): lax.ppermute(a, axis, pairs(count, False))  3.61 us
    ppermute x1, starting transfers between devices, per_device(): got_cb = lax.ppermute(edge_b, 'col', pairs(ms['col'], True))  2.23 us
  transfers between devices with their start and end apart: 22, of which 12 were waited for; matrix products, arithmetic and copies ran while one was open for 0% of the time, Pallas kernels for 16%

commit v1 on v0

--- a/solution.py
+++ b/solution.py
@@ -184,45 +184,18 @@
     with_corners(ms, edge_a, edge_b, got_a, got_b, out_a, out_b)
 
 
-def differences(src, out):
-    for b in range(src.shape[0]):
-        out[b] = src[b, 0 : src.shape[1] - 1] - src[b, 1:]
-
-
-def pair_sums(weight, taps_i, taps_j, out):
-    for a in range((taps_i + 1) // 2):
-        for j in range(taps_j):
-            w = weight(2 * a, j)
-            if 2 * a + 1 < taps_i:
-                w = w + weight(2 * a + 1, j)
-            out[a * taps_j + j] = w
-
-
-def depthwise_block(read, diff, weight, sums, rows, taps_i, taps_j, start):
-    def add(total, k, term):
-        total[k] = term if total[k] is None else total[k] + term
-
-    n, n0, n1 = rows // 2, (taps_i + 1) // 2, taps_i // 2
-    both, even_rows, odd_rows = [None] * n, list(start[0::2]), list(start[1::2])
+def depthwise_block(read, weight, rows, taps_i, taps_j, start):
+    acc = start
     for j in range(taps_j):
-        w0 = [weight(2 * a, j) for a in range(n0)]
-        w1 = [weight(2 * a + 1, j) for a in range(n1)]
-        ws = [sums(a, j) for a in range(n0)]
-        for r in range(n + n0 - 1):
-            x, d = read(2 * r + 1, j), diff(2 * r, j)
-            for a in range(n0):
-                if 0 <= r - a < n:
-                    add(both, r - a, ws[a] * x)
-                    add(even_rows, r - a, w0[a] * d)
-        for r in range(n + n1 - 1):
-            d = diff(2 * r + 1, j)
-            for a in range(n1):
-                if 0 <= r - a < n:
-                    odd_rows[r - a] = odd_rows[r - a] - w1[a] * d
-    out = []
-    for k in range(n):
-        out += [both[k] + even_rows[k], both[k] + odd_rows[k]]
-    return out
+        w = [weight(i, j) for i in range(taps_i)]
+        for r in range(rows + taps_i - 1):
+            s = read(r, j)
+            for i in range(taps_i):
+                p = r - i
+                if 0 <= p < rows:
+                    term = w[i] * s
+                    acc[p] = term if acc[p] is None else acc[p] + term
+    return acc
 
 
 def fill(ms, dst, inner, row_a, row_b, col_a, col_b):
@@ -252,7 +225,7 @@
     ms, order, factor, taps_i, taps_j, tile,
     feat, got_ra, got_rb, got_cb, kept, got, cot_ref,
     src_ref, dconv_ref, row_a, row_b, edge_a, edge_b, grads_ref, chan_ref, small_ref,
-    conv_scr, diff_scr, cols_scr, kb_scr, ks_scr, win_scr, wout_scr, w1_scr, w2_scr, w4_scr, bias_scr,
+    conv_scr, cols_scr, kb_scr, win_scr, wout_scr, w1_scr, w2_scr, w4_scr, bias_scr,
     gw1_scr, gw2_scr, gb_scr, gg_scr, gs_scr, gc_scr, cot_sum,
 ):
     batch, rows, cols, C = feat.shape
@@ -304,16 +277,11 @@
     w4_scr[0:C, :] = th
     w4_scr[C : 2 * C, :] = tl
 
-    differences(src_ref, diff_scr)
-    weight = lambda i, j: kb_scr[i * taps_j + j]
-    pair_sums(weight, taps_i, taps_j, ks_scr)
-
     def conv_step(b, _):
         for q in range(0, cols, 8):
             acc = depthwise_block(
                 lambda r, j: src_ref[b, r, LEFT - m + q + j : LEFT - m + q + j + 8, :],
-                lambda r, j: diff_scr[b, r, LEFT - m + q + j : LEFT - m + q + j + 8, :],
-                weight, lambda a, j: ks_scr[a * taps_j + j],
+                lambda i, j: kb_scr[i * taps_j + j],
                 rows, taps_i, taps_j, [conv_bias] * rows,
             )
             for p in range(rows):
@@ -413,44 +381,27 @@
     chan_ref[5:6, :] = gb
 
 
-def kernel_grad_body(ms, order, factor, taps_i, taps_j, count, src_ref, dconv_ref, chan_ref, out_ref, acc_scr, rows_scr, diff_scr, sum_scr):
+def kernel_grad_body(ms, order, factor, taps_i, taps_j, count, src_ref, dconv_ref, chan_ref, out_ref, acc_scr, rows_scr):
     batch, rows, cols, C = dconv_ref.shape
     m = taps_i // 2
     taps = taps_i * taps_j
     cs = C // count
     me = device_index(ms)
-    n, n0, n1 = rows // 2, (taps_i + 1) // 2, taps_i // 2
     acc_scr[...] = jnp.zeros_like(acc_scr)
-    differences(src_ref, diff_scr)
-    for b in range(batch):
-        for k in range(n):
-            sum_scr[b, k] = dconv_ref[b, 2 * k] + dconv_ref[b, 2 * k + 1]
 
     def step(b, _):
         for j in range(taps_j):
-            both = [jnp.zeros((8, C), f32)] * n0
-            first = [acc_scr[2 * a * taps_j + j] for a in range(n0)]
-            second = [acc_scr[(2 * a + 1) * taps_j + j] for a in range(n1)]
+            acc = [acc_scr[i * taps_j + j] for i in range(taps_i)]
             for q in range(0, cols, 8):
-                own, at = pl.ds(q, 8), pl.ds(LEFT - m + q + j, 8)
-                ds = [sum_scr[b, k, own, :] for k in range(n)]
-                d0 = [dconv_ref[b, 2 * k, own, :] for k in range(n)]
-                d1 = [dconv_ref[b, 2 * k + 1, own, :] for k in range(n)]
-                for r in range(n + n0 - 1):
-                    x, d = src_ref[b, 2 * r + 1, at, :], diff_scr[b, 2 * r, at, :]
-                    for a in range(n0):
-                        if 0 <= r - a < n:
-                            both[a] = both[a] + ds[r - a] * x
-                            first[a] = first[a] + d0[r - a] * d
-                for r in range(n + n1 - 1):
-                    d = diff_scr[b, 2 * r + 1, at, :]
-                    for a in range(n1):
-                        if 0 <= r - a < n:
-                            second[a] = second[a] - d1[r - a] * d
-            for a in range(n0):
-                acc_scr[2 * a * taps_j + j] = first[a] + both[a]
-            for a in range(n1):
-                acc_scr[(2 * a + 1) * taps_j + j] = second[a] + both[a]
+                d = [dconv_ref[b, p, q : q + 8, :] for p in range(rows)]
+                for r in range(rows + taps_i - 1):
+                    s = src_ref[b, r, LEFT - m + q + j : LEFT - m + q + j + 8, :]
+                    for i in range(taps_i):
+                        p = r - i
+                        if 0 <= p < rows:
+                            acc[i] = acc[i] + d[p] * s
+            for i in range(taps_i):
+                acc_scr[i * taps_j + j] = acc[i]
         return 0
 
     lax.fori_loop(0, batch, step, 0)
@@ -466,7 +417,7 @@
         out_ref[s, cs : cs + 1, 0:hs] = chan_ref[5:6, s * hs : (s + 1) * hs]
 
 
-def features_grad_body(ms, taps_i, taps_j, inner, got_ra, got_rb, got_ca, got_cb, small_ref, cot_ref, out_ref, ext_scr, diff_scr, kb_scr, ks_scr):
+def features_grad_body(ms, taps_i, taps_j, inner, got_ra, got_rb, got_ca, got_cb, small_ref, cot_ref, out_ref, ext_scr, kb_scr):
     batch, rows, cols, C = inner.shape
     m = taps_i // 2
     taps = taps_i * taps_j
@@ -474,16 +425,11 @@
     for t in range(taps):
         kb_scr[t] = jnp.broadcast_to(small_ref[t : t + 1, :], (8, C))
 
-    differences(ext_scr, diff_scr)
-    weight = lambda i, j: kb_scr[taps - 1 - (i * taps_j + j)]
-    pair_sums(weight, taps_i, taps_j, ks_scr)
-
     def step(b, _):
         for q in range(0, cols, 8):
             acc = depthwise_block(
                 lambda r, j: ext_scr[b, r, LEFT - m + q + j : LEFT - m + q + j + 8, :],
-                lambda r, j: diff_scr[b, r, LEFT - m + q + j : LEFT - m + q + j + 8, :],
-                weight, lambda a, j: ks_scr[a * taps_j + j],
+                lambda i, j: kb_scr[taps - 1 - (i * taps_j + j)],
                 rows, taps_i, taps_j, [cot_ref[b, p, q : q + 8, :] for p in range(rows)],
             )
             for p in range(rows):
@@ -609,10 +555,8 @@
         ),
         scratch=(
             vm((batch, rows, cols, C), f32),
-            vm((batch, rows + 2 * m - 1, wide, C), f32),
             vm((C, LANES), f32),
             vm((taps, 8, C), f32),
-            vm(((taps_i + 1) // 2 * taps_j, 8, C), f32),
             vm((hid, C), f32),
             vm((hid, C), f32),
             vm((hid, 3 * C), bf16),
@@ -640,8 +584,6 @@
         scratch=(
             vm((taps, 8, C), f32),
             vm((LANES, C), f32),
-            vm((batch, rows + 2 * m - 1, wide, C), f32),
-            vm((batch, rows // 2, cols, C), f32),
         ),
         flops=4 * 10**9,
         size=4 * 10**6,
@@ -668,9 +610,7 @@
         shape(batch, rows, cols, C),
         scratch=(
             vm((batch, rows + 2 * m, wide, C), f32),
-            vm((batch, rows + 2 * m - 1, wide, C), f32),
             vm((taps, 8, C), f32),
-            vm(((taps_i + 1) // 2 * taps_j, 8, C), f32),
         ),
         flops=4 * 10**9,
         size=4 * 10**6,

time: 74.9 us -> 74.1 us (0.989)
    pallas_call x1, Pallas kernels: 5.44 us -> 4.64 us  [per_device(): call(functools.partial(features_grad_body, ms, taps_i, taps_j), shape(bat...]
  transfers between devices with their start and end apart: 22 -> 22, of which waited for: 12 -> 11; matrix products, arithmetic and copies ran while one was open for 0% -> 0% of each run, Pallas kernels for 16% -> 16%
where the time goes in v1:
time: 74.1 us; the launch traced here: 73.9 us
  Pallas kernels  31.5 us (43%)
  starting transfers between devices  27 us (36%)
  waiting for transfers between devices  13.8 us (19%)
  local copies, waits for them, and re-layouts  0.77 us (1%)
    pallas_call x1, Pallas kernels, per_device(): call(functools.partial(mix_body, ms, order, factor, taps_i, taps_j, tile)...  16.7 us
    ppermute x15, starting transfers between devices, flip(): return lax.ppermute(x, AXES, [(i, i ^ mask) for i in range(count)])  16.6 us
    ppermute x15, waiting for transfers between devices, flip(): return lax.ppermute(x, AXES, [(i, i ^ mask) for i in range(count)])  12.9 us
    pallas_call x1, Pallas kernels, per_device(): call(functools.partial(kernel_grad_body, ms, order, factor, taps_i, taps_...  7.19 us
    pallas_call x1, Pallas kernels, per_device(): call(functools.partial(features_grad_body, ms, taps_i, taps_j), shape(bat...  4.64 us
    ppermute x3, starting transfers between devices, both_pairs(): lax.ppermute(b, axis, pairs(count, True))  4.55 us
    ppermute x3, starting transfers between devices, both_pairs(): lax.ppermute(a, axis, pairs(count, False))  3.61 us
    ppermute x1, starting transfers between devices, per_device(): got_cb = lax.ppermute(edge_b, 'col', pairs(ms['col'], True))  2.23 us
  transfers between devices with their start and end apart: 22, of which 11 were waited for; matrix products, arithmetic and copies ran while one was open for 0% of the time, Pallas kernels for 16%

profile of v1, /device:TPU:0, one launch (start us, length us, event | category | flops | bytes accessed | tf_op | source)
XLA Modules:
  0.0 73.9 jit_solution(5936327883676325465)
XLA Ops:
  0.7 2.1 %shard_map.186 = (f32[40,128]{1,0:T(8,128)}, f32[2,3,64,128]{3,2,1,0:T(8,128)}, f32[2,3,64,128]{3,2,1,0:T(8,128)}) custom-call(f32[2,16,64,128]{3,2,1,0:T(8,128)} %feat.3, f32[7,4,7]{2,1,0:T(4,128)} %bitcast.29, f32[1,4]{1,0:T(1,128)} %bitcast.31, f32[1,4]{1,0:T(1,128)} %bitcast.32, f32[1,4]{1,0:T(1,128)} %bitcast.33, f32[1,4]{1,0:T(1,128)} %bitcast.34, ...), custom_call_target="tpu_custom_call" | custom-call | bytes 1000000 | tf_op jit(solution)/shard_map/pallas_call | solution.py:497
  2.7 3.0 %collective-permute-start = (f32[2,3,64,128]{3,2,1,0:T(8,128)}, f32[2,3,64,128]{3,2,1,0:T(8,128)S(1)}, u32[]{:S(2)}, u32[]{:S(2)}) collective-permute-start(f32[2,3,64,128]{3,2,1,0:T(8,128)} %get-tuple-element.40), channel_id=1, source_target_pairs={{0,8},{8,0},{16,24},{24,16},{1,9},{9,1},{17,25},{25,17},{2,10},{10... | collective-permute-start | bytes 589832 | tf_op jit(solution)/shard_map/ppermute | solution.py:86
  5.7 1.5 %collective-permute-start.1 = (f32[2,3,64,128]{3,2,1,0:T(8,128)}, f32[2,3,64,128]{3,2,1,0:T(8,128)S(1)}, u32[]{:S(2)}, u32[]{:S(2)}) collective-permute-start(f32[2,3,64,128]{3,2,1,0:T(8,128)} %get-tuple-element.41), channel_id=1, source_target_pairs={{0,24},{8,16},{16,8},{24,0},{1,25},{9,17},{17,9},{25,1},{2,26},{10... | collective-permute-start | bytes 589832 | tf_op jit(solution)/shard_map/ppermute | solution.py:86
  7.2 3.6 %collective-permute-start.4 = (f32[1,40,128]{2,1,0:T(8,128)}, f32[1,40,128]{2,1,0:T(8,128)S(1)}, u32[]{:S(2)}, u32[]{:S(2)}) collective-permute-start(f32[1,40,128]{2,1,0:T(8,128)} %bitcast.25), channel_id=1, source_target_pairs={{0,6},{1,7},{2,4},{3,5},{4,2},{5,3},{6,0},{7,1},{8,14},{9,15},{10,... | collective-permute-start | bytes 61448 | tf_op jit(solution)/shard_map/ppermute | solution.py:461
  10.8 0.8 %collective-permute-start.2 = (f32[1,40,128]{2,1,0:T(8,128)}, f32[1,40,128]{2,1,0:T(8,128)S(1)}, u32[]{:S(2)}, u32[]{:S(2)}) collective-permute-start(f32[1,40,128]{2,1,0:T(8,128)} %bitcast.27), channel_id=1, source_target_pairs={{0,2},{1,3},{2,0},{3,1},{4,6},{5,7},{6,4},{7,5},{8,10},{9,11},{10,... | collective-permute-start | bytes 61448 | tf_op jit(solution)/shard_map/ppermute | solution.py:461
  11.6 1.5 %collective-permute-done.4.refs_3_ = f32[1,40,128]{2,1,0:T(8,128)S(1)} collective-permute-done((f32[1,40,128]{2,1,0:T(8,128)}, f32[1,40,128]{2,1,0:T(8,128)S(1)}, u32[]{:S(2)}, u32[]{:S(2)}) %collective-permute-start.4) | collective-permute-done | bytes 20512 | tf_op jit(solution)/shard_map/ppermute | solution.py:461
  13.1 2.7 %collective-permute-done.3.refs_2_ = f32[1,40,128]{2,1,0:T(8,128)S(1)} collective-permute-done((f32[1,40,128]{2,1,0:T(8,128)}, f32[1,40,128]{2,1,0:T(8,128)S(1)}, u32[]{:S(2)}, u32[]{:S(2)}) %collective-permute-start.3) | collective-permute-done | bytes 20512 | tf_op jit(solution)/shard_map/ppermute | solution.py:461
  17.1 2.2 %collective-permute-start.5 = (f32[2,22,4,128]{3,2,1,0:T(4,128)S(1)}, f32[2,22,4,128]{3,2,1,0:T(4,128)S(1)}, u32[]{:S(2)}, u32[]{:S(2)}) collective-permute-start(f32[2,22,4,128]{3,2,1,0:T(4,128)S(1)} %get-tuple-element.43), channel_id=1, source_target_pairs={{0,7},{1,2},{2,1},{3,4},{4,3},{5,6},{6,5},{7,0},{8,15},{9,10},{10,... | collective-permute-start | bytes 270344 | tf_op jit(solution)/shard_map/ppermute | solution.py:530
  19.3 1.4 %collective-permute-start.8 = (f32[4,40,128]{2,1,0:T(8,128)S(1)}, f32[4,40,128]{2,1,0:T(8,128)S(1)}, u32[]{:S(2)}, u32[]{:S(2)}) collective-permute-start(f32[4,40,128]{2,1,0:T(8,128)S(1)} %get-tuple-element.45.refs_0_), channel_id=1, source_target_pairs={{0,24},{1,25},{2,26},{3,27},{4,28},{5,29},{6,30},{7,31},{8,16},{9,... | collective-permute-start | bytes 245768 | tf_op jit(solution)/shard_map/ppermute | solution.py:461
  20.8 1.5 %collective-permute-start.7 = (f32[4,40,128]{2,1,0:T(8,128)S(1)}, f32[4,40,128]{2,1,0:T(8,128)S(1)}, u32[]{:S(2)}, u32[]{:S(2)}) collective-permute-start(f32[4,40,128]{2,1,0:T(8,128)S(1)} %get-tuple-element.45.refs_0_), channel_id=1, source_target_pairs={{0,16},{1,17},{2,18},{3,19},{4,20},{5,21},{6,22},{7,23},{8,24},{9,... | collective-permute-start | bytes 245768 | tf_op jit(solution)/shard_map/ppermute | solution.py:461
  22.8 2.7 %collective-permute-done.8.refs_3_ = f32[4,40,128]{2,1,0:T(8,128)S(1)} collective-permute-done((f32[4,40,128]{2,1,0:T(8,128)S(1)}, f32[4,40,128]{2,1,0:T(8,128)S(1)}, u32[]{:S(2)}, u32[]{:S(2)}) %collective-permute-start.8) | collective-permute-done | bytes 81952 | tf_op jit(solution)/shard_map/ppermute | solution.py:461
  25.8 0.9 %collective-permute-done.6.refs_1_ = f32[4,40,128]{2,1,0:T(8,128)S(1)} collective-permute-done((f32[4,40,128]{2,1,0:T(8,128)S(1)}, f32[4,40,128]{2,1,0:T(8,128)S(1)}, u32[]{:S(2)}, u32[]{:S(2)}) %collective-permute-start.6) | collective-permute-done | bytes 81952 | tf_op jit(solution)/shard_map/ppermute | solution.py:461
  26.8 1.7 %collective-permute-done.9.got = f32[816,128]{1,0:T(8,128)S(1)} collective-permute-done((f32[816,128]{1,0:T(8,128)S(1)}, f32[816,128]{1,0:T(8,128)S(1)}, u32[]{:S(2)}, u32[]{:S(2)}) %collective-permute-start.9) | collective-permute-done | bytes 417824 | tf_op jit(solution)/shard_map/ppermute | solution.py:461
  28.6 16.7 %shard_map.189 = (f32[2,22,80,128]{3,2,1,0:T(8,128)S(1)}, f32[2,16,64,128]{3,2,1,0:T(8,128)S(1)}, f32[2,3,64,128]{3,2,1,0:T(8,128)S(1)}, f32[2,3,64,128]{3,2,1,0...) custom-call(f32[2,16,64,128]{3,2,1,0:T(8,128)S(1)} %copy-done, ...), custom_call_target="tpu_custom_call" | custom-call | flops 12000000000 | bytes 8000000 | tf_op jit(solution)/shard_map/pallas_call | solution.py:545
  45.9 1.4 %collective-permute-start.11 = (f32[2,3,64,128]{3,2,1,0:T(8,128)S(1)}, f32[2,3,64,128]{3,2,1,0:T(8,128)S(1)}, u32[]{:S(2)}, u32[]{:S(2)}) collective-permute-start(f32[2,3,64,128]{3,2,1,0:T(8,128)S(1)} %get-tuple-element.48), channel_id=1, source_target_pairs={{0,24},{8,16},{16,8},{24,0},{1,25},{9,17},{17,9},{25,1},{2,26},{10... | collective-permute-start | bytes 589832 | tf_op jit(solution)/shard_map/ppermute | solution.py:86
  47.4 7.2 %shard_map.190.small = f32[32,8,128]{2,1,0:T(8,128)S(1)} custom-call(f32[2,22,80,128]{3,2,1,0:T(8,128)S(1)} %get-tuple-element.52.src_ref, f32[2,16,64,128]{3,2,1,0:T(8,128)S(1)} %get-tuple-element.46.dconv_ref.inner, f32[8,512]{1,0:T(8,128)S(1)} %get-tuple-element.53.chan_ref), custom_call_target="tpu_custom_call" | custom-call | flops 4000000000 | bytes 4000000 | tf_op jit(solution)/shard_map/pallas_call | solution.py:581
  55.2 0.9 %collective-permute-done.13.small_got = f32[16,8,128]{2,1,0:T(8,128)S(1)} collective-permute-done((f32[16,8,128]{2,1,0:T(8,128)S(1)}, f32[16,8,128]{2,1,0:T(8,128)S(1)}, u32[]{:S(2)}, u32[]{:S(2)}) %collective-permute-start.13) | collective-permute-done | bytes 65568 | tf_op jit(solution)/shard_map/ppermute | solution.py:461
  57.2 1.4 %collective-permute-start.17 = (f32[4,40,128]{2,1,0:T(8,128)S(1)}, f32[4,40,128]{2,1,0:T(8,128)S(1)}, u32[]{:S(2)}, u32[]{:S(2)}) collective-permute-start(f32[4,40,128]{2,1,0:T(8,128)S(1)} %get-tuple-element.59), channel_id=1, source_target_pairs={{0,16},{1,17},{2,18},{3,19},{4,20},{5,21},{6,22},{7,23},{8,24},{9,... | collective-permute-start | bytes 245768 | tf_op jit(solution)/shard_map/ppermute | solution.py:461
  58.6 1.4 %collective-permute-start.18 = (f32[4,40,128]{2,1,0:T(8,128)S(1)}, f32[4,40,128]{2,1,0:T(8,128)S(1)}, u32[]{:S(2)}, u32[]{:S(2)}) collective-permute-start(f32[4,40,128]{2,1,0:T(8,128)S(1)} %get-tuple-element.60), channel_id=1, source_target_pairs={{0,24},{1,25},{2,26},{3,27},{4,28},{5,29},{6,30},{7,31},{8,16},{9,... | collective-permute-start | bytes 245768 | tf_op jit(solution)/shard_map/ppermute | solution.py:461
  60.1 1.6 %collective-permute-start.15 = (f32[2,22,4,128]{3,2,1,0:T(4,128)S(1)}, f32[2,22,4,128]{3,2,1,0:T(4,128)S(1)}, u32[]{:S(2)}, u32[]{:S(2)}) collective-permute-start(f32[2,22,4,128]{3,2,1,0:T(4,128)S(1)} %get-tuple-element.55), channel_id=1, source_target_pairs={{0,7},{1,2},{2,1},{3,4},{4,3},{5,6},{6,5},{7,0},{8,15},{9,10},{10,... | collective-permute-start | bytes 270344 | tf_op jit(solution)/shard_map/ppermute | solution.py:86
  61.9 2.1 %collective-permute-done.18 = f32[4,40,128]{2,1,0:T(8,128)S(1)} collective-permute-done((f32[4,40,128]{2,1,0:T(8,128)S(1)}, f32[4,40,128]{2,1,0:T(8,128)S(1)}, u32[]{:S(2)}, u32[]{:S(2)}) %collective-permute-start.18) | collective-permute-done | bytes 81952 | tf_op jit(solution)/shard_map/ppermute | solution.py:461
  64.0 1.8 %collective-permute-start.21 = (f32[1,40,128]{2,1,0:T(8,128)S(1)}, f32[1,40,128]{2,1,0:T(8,128)S(1)}, u32[]{:S(2)}, u32[]{:S(2)}) collective-permute-start(f32[1,40,128]{2,1,0:T(8,128)S(1)} %get-tuple-element.70), channel_id=1, source_target_pairs={{0,6},{1,7},{2,4},{3,5},{4,2},{5,3},{6,0},{7,1},{8,14},{9,15},{10,... | collective-permute-start | bytes 61448 | tf_op jit(solution)/shard_map/ppermute | solution.py:461
  65.9 2.6 %collective-permute-start.19 = (f32[1,40,128]{2,1,0:T(8,128)S(1)}, f32[1,40,128]{2,1,0:T(8,128)S(1)}, u32[]{:S(2)}, u32[]{:S(2)}) collective-permute-start(f32[1,40,128]{2,1,0:T(8,128)S(1)} %get-tuple-element.72), channel_id=1, source_target_pairs={{0,2},{1,3},{2,0},{3,1},{4,6},{5,7},{6,4},{7,5},{8,10},{9,11},{10,... | collective-permute-start | bytes 61448 | tf_op jit(solution)/shard_map/ppermute | solution.py:461
  68.5 4.6 %shard_map.192 = f32[2,16,64,128]{3,2,1,0:T(8,128)} custom-call(f32[2,16,64,128]{3,2,1,0:T(8,128)S(1)} %get-tuple-element.46.dconv_ref.inner, f32[2,3,64,128]{3,2,1,0:T(8,128)S(1)} %collective-permute-done.10.got_a.got_ra, f32[2,3,64,128]{3,2,1,0:T(8,128)S(1)} %collective-permute-done.11.got_b.got_rb, f32[2,22,4,128]{3,2,1,0:T(4,128)S(1)} %collective-permute-done.14.got_ca, ...), custom_call_target="tpu_custom_call" | custom-call | flops 4000000000 | bytes 4000000 | tf_op jit(solution)/shard_map/pallas_call | solution.py:608
  (38 shorter events, 5.8 us)
Async XLA Ops:
  0.6 15.6 %copy-start = (f32[2,16,64,128]{3,2,1,0:T(8,128)S(1)}, f32[2,16,64,128]{3,2,1,0:T(8,128)}, u32[]{:S(2)}) copy-start(f32[2,16,64,128]{3,2,1,0:T(8,128)} %feat.3) | copy-start | bytes 3145732
  2.7 13.0 %collective-permute-start = (f32[2,3,64,128]{3,2,1,0:T(8,128)}, f32[2,3,64,128]{3,2,1,0:T(8,128)S(1)}, u32[]{:S(2)}, u32[]{:S(2)}) collective-permute-start(f32[2,3,64,128]{3,2,1,0:T(8,128)} %get-tuple-element.40), channel_id=1, source_target_pairs={{0,8},{8,0},{16,24},{24,16},{1,9},{9,1},{17,25},{25,17},{2,10},{10... | collective-permute-start | bytes 589832 | tf_op jit(solution)/shard_map/ppermute | solution.py:86
  5.7 10.5 %collective-permute-start.1 = (f32[2,3,64,128]{3,2,1,0:T(8,128)}, f32[2,3,64,128]{3,2,1,0:T(8,128)S(1)}, u32[]{:S(2)}, u32[]{:S(2)}) collective-permute-start(f32[2,3,64,128]{3,2,1,0:T(8,128)} %get-tuple-element.41), channel_id=1, source_target_pairs={{0,24},{8,16},{16,8},{24,0},{1,25},{9,17},{17,9},{25,1},{2,26},{10... | collective-permute-start | bytes 589832 | tf_op jit(solution)/shard_map/ppermute | solution.py:86
  7.2 5.8 %collective-permute-start.4 = (f32[1,40,128]{2,1,0:T(8,128)}, f32[1,40,128]{2,1,0:T(8,128)S(1)}, u32[]{:S(2)}, u32[]{:S(2)}) collective-permute-start(f32[1,40,128]{2,1,0:T(8,128)} %bitcast.25), channel_id=1, source_target_pairs={{0,6},{1,7},{2,4},{3,5},{4,2},{5,3},{6,0},{7,1},{8,14},{9,15},{10,... | collective-permute-start | bytes 61448 | tf_op jit(solution)/shard_map/ppermute | solution.py:461
  10.8 4.9 %collective-permute-start.3 = (f32[1,40,128]{2,1,0:T(8,128)}, f32[1,40,128]{2,1,0:T(8,128)S(1)}, u32[]{:S(2)}, u32[]{:S(2)}) collective-permute-start(f32[1,40,128]{2,1,0:T(8,128)} %bitcast.26), channel_id=1, source_target_pairs={{0,4},{1,5},{2,6},{3,7},{4,0},{5,1},{6,2},{7,3},{8,12},{9,13},{10,... | collective-permute-start | bytes 61448 | tf_op jit(solution)/shard_map/ppermute | solution.py:461
  10.8 4.9 %collective-permute-start.2 = (f32[1,40,128]{2,1,0:T(8,128)}, f32[1,40,128]{2,1,0:T(8,128)S(1)}, u32[]{:S(2)}, u32[]{:S(2)}) collective-permute-start(f32[1,40,128]{2,1,0:T(8,128)} %bitcast.27), channel_id=1, source_target_pairs={{0,2},{1,3},{2,0},{3,1},{4,6},{5,7},{6,4},{7,5},{8,10},{9,11},{10,... | collective-permute-start | bytes 61448 | tf_op jit(solution)/shard_map/ppermute | solution.py:461
  17.0 11.6 %copy-start.2 = (f32[2,16,64,128]{3,2,1,0:T(8,128)S(1)}, f32[2,16,64,128]{3,2,1,0:T(8,128)}, u32[]{:S(2)}) copy-start(f32[2,16,64,128]{3,2,1,0:T(8,128)} %cot_ref.3) | copy-start | bytes 3145732
  17.1 9.6 %collective-permute-start.5 = (f32[2,22,4,128]{3,2,1,0:T(4,128)S(1)}, f32[2,22,4,128]{3,2,1,0:T(4,128)S(1)}, u32[]{:S(2)}, u32[]{:S(2)}) collective-permute-start(f32[2,22,4,128]{3,2,1,0:T(4,128)S(1)} %get-tuple-element.43), channel_id=1, source_target_pairs={{0,7},{1,2},{2,1},{3,4},{4,3},{5,6},{6,5},{7,0},{8,15},{9,10},{10,... | collective-permute-start | bytes 270344 | tf_op jit(solution)/shard_map/ppermute | solution.py:530
  19.3 6.2 %collective-permute-start.8 = (f32[4,40,128]{2,1,0:T(8,128)S(1)}, f32[4,40,128]{2,1,0:T(8,128)S(1)}, u32[]{:S(2)}, u32[]{:S(2)}) collective-permute-start(f32[4,40,128]{2,1,0:T(8,128)S(1)} %get-tuple-element.45.refs_0_), channel_id=1, source_target_pairs={{0,24},{1,25},{2,26},{3,27},{4,28},{5,29},{6,30},{7,31},{8,16},{9,... | collective-permute-start | bytes 245768 | tf_op jit(solution)/shard_map/ppermute | solution.py:461
  20.8 5.1 %collective-permute-start.7 = (f32[4,40,128]{2,1,0:T(8,128)S(1)}, f32[4,40,128]{2,1,0:T(8,128)S(1)}, u32[]{:S(2)}, u32[]{:S(2)}) collective-permute-start(f32[4,40,128]{2,1,0:T(8,128)S(1)} %get-tuple-element.45.refs_0_), channel_id=1, source_target_pairs={{0,16},{1,17},{2,18},{3,19},{4,20},{5,21},{6,22},{7,23},{8,24},{9,... | collective-permute-start | bytes 245768 | tf_op jit(solution)/shard_map/ppermute | solution.py:461
  22.3 4.4 %collective-permute-start.6 = (f32[4,40,128]{2,1,0:T(8,128)S(1)}, f32[4,40,128]{2,1,0:T(8,128)S(1)}, u32[]{:S(2)}, u32[]{:S(2)}) collective-permute-start(f32[4,40,128]{2,1,0:T(8,128)S(1)} %get-tuple-element.45.refs_0_), channel_id=1, source_target_pairs={{0,8},{1,9},{2,10},{3,11},{4,12},{5,13},{6,14},{7,15},{8,0},{9,1},... | collective-permute-start | bytes 245768 | tf_op jit(solution)/shard_map/ppermute | solution.py:461
  26.8 1.8 %collective-permute-start.9 = (f32[816,128]{1,0:T(8,128)S(1)}, f32[816,128]{1,0:T(8,128)S(1)}, u32[]{:S(2)}, u32[]{:S(2)}) collective-permute-start(f32[816,128]{1,0:T(8,128)S(1)} %shard_map.188.kept), channel_id=1, source_target_pairs={{0,1},{1,0},{2,3},{3,2},{4,5},{5,4},{6,7},{7,6},{8,9},{9,8},{10,11... | collective-permute-start | bytes 1253384 | tf_op jit(solution)/shard_map/ppermute | solution.py:461
  45.3 10.8 %collective-permute-start.10 = (f32[2,3,64,128]{3,2,1,0:T(8,128)S(1)}, f32[2,3,64,128]{3,2,1,0:T(8,128)S(1)}, u32[]{:S(2)}, u32[]{:S(2)}) collective-permute-start(f32[2,3,64,128]{3,2,1,0:T(8,128)S(1)} %get-tuple-element.47), channel_id=1, source_target_pairs={{0,8},{8,0},{16,24},{24,16},{1,9},{9,1},{17,25},{25,17},{2,10},{10... | collective-permute-start | bytes 589832 | tf_op jit(solution)/shard_map/ppermute | solution.py:86
  45.9 10.6 %collective-permute-start.11 = (f32[2,3,64,128]{3,2,1,0:T(8,128)S(1)}, f32[2,3,64,128]{3,2,1,0:T(8,128)S(1)}, u32[]{:S(2)}, u32[]{:S(2)}) collective-permute-start(f32[2,3,64,128]{3,2,1,0:T(8,128)S(1)} %get-tuple-element.48), channel_id=1, source_target_pairs={{0,24},{8,16},{16,8},{24,0},{1,25},{9,17},{17,9},{25,1},{2,26},{10... | collective-permute-start | bytes 589832 | tf_op jit(solution)/shard_map/ppermute | solution.py:86
  47.3 9.1 %collective-permute-start.12 = (f32[16,32,128]{2,1,0:T(8,128)S(1)}, f32[16,32,128]{2,1,0:T(8,128)S(1)}, u32[]{:S(2)}, u32[]{:S(2)}) collective-permute-start(f32[16,32,128]{2,1,0:T(8,128)S(1)} %slice.18), channel_id=1, source_target_pairs={{0,1},{1,0},{2,3},{3,2},{4,5},{5,4},{6,7},{7,6},{8,9},{9,8},{10,11... | collective-permute-start | bytes 786440 | tf_op jit(solution)/shard_map/ppermute | solution.py:461
  54.6 1.5 %collective-permute-start.13 = (f32[16,8,128]{2,1,0:T(8,128)S(1)}, f32[16,8,128]{2,1,0:T(8,128)S(1)}, u32[]{:S(2)}, u32[]{:S(2)}) collective-permute-start(f32[16,8,128]{2,1,0:T(8,128)S(1)} %slice.24), channel_id=1, source_target_pairs={{0,1},{1,0},{2,3},{3,2},{4,5},{5,4},{6,7},{7,6},{8,9},{9,8},{10,11... | collective-permute-start | bytes 196616 | tf_op jit(solution)/shard_map/ppermute | solution.py:461
  56.5 5.2 %collective-permute-start.16 = (f32[4,40,128]{2,1,0:T(8,128)S(1)}, f32[4,40,128]{2,1,0:T(8,128)S(1)}, u32[]{:S(2)}, u32[]{:S(2)}) collective-permute-start(f32[4,40,128]{2,1,0:T(8,128)S(1)} %get-tuple-element.58), channel_id=1, source_target_pairs={{0,8},{1,9},{2,10},{3,11},{4,12},{5,13},{6,14},{7,15},{8,0},{9,1},... | collective-permute-start | bytes 245768 | tf_op jit(solution)/shard_map/ppermute | solution.py:461
  57.2 4.6 %collective-permute-start.17 = (f32[4,40,128]{2,1,0:T(8,128)S(1)}, f32[4,40,128]{2,1,0:T(8,128)S(1)}, u32[]{:S(2)}, u32[]{:S(2)}) collective-permute-start(f32[4,40,128]{2,1,0:T(8,128)S(1)} %get-tuple-element.59), channel_id=1, source_target_pairs={{0,16},{1,17},{2,18},{3,19},{4,20},{5,21},{6,22},{7,23},{8,24},{9,... | collective-permute-start | bytes 245768 | tf_op jit(solution)/shard_map/ppermute | solution.py:461
  58.6 5.3 %collective-permute-start.18 = (f32[4,40,128]{2,1,0:T(8,128)S(1)}, f32[4,40,128]{2,1,0:T(8,128)S(1)}, u32[]{:S(2)}, u32[]{:S(2)}) collective-permute-start(f32[4,40,128]{2,1,0:T(8,128)S(1)} %get-tuple-element.60), channel_id=1, source_target_pairs={{0,24},{1,25},{2,26},{3,27},{4,28},{5,29},{6,30},{7,31},{8,16},{9,... | collective-permute-start | bytes 245768 | tf_op jit(solution)/shard_map/ppermute | solution.py:461
  60.1 8.4 %collective-permute-start.14 = (f32[2,22,4,128]{3,2,1,0:T(4,128)S(1)}, f32[2,22,4,128]{3,2,1,0:T(4,128)S(1)}, u32[]{:S(2)}, u32[]{:S(2)}) collective-permute-start(f32[2,22,4,128]{3,2,1,0:T(4,128)S(1)} %get-tuple-element.54), channel_id=1, source_target_pairs={{0,1},{1,0},{2,3},{3,2},{4,5},{5,4},{6,7},{7,6},{8,9},{9,8},{10,11... | collective-permute-start | bytes 270344 | tf_op jit(solution)/shard_map/ppermute | solution.py:86
  60.1 8.4 %collective-permute-start.15 = (f32[2,22,4,128]{3,2,1,0:T(4,128)S(1)}, f32[2,22,4,128]{3,2,1,0:T(4,128)S(1)}, u32[]{:S(2)}, u32[]{:S(2)}) collective-permute-start(f32[2,22,4,128]{3,2,1,0:T(4,128)S(1)} %get-tuple-element.55), channel_id=1, source_target_pairs={{0,7},{1,2},{2,1},{3,4},{4,3},{5,6},{6,5},{7,0},{8,15},{9,10},{10,... | collective-permute-start | bytes 270344 | tf_op jit(solution)/shard_map/ppermute | solution.py:86
  64.0 9.1 %collective-permute-start.21 = (f32[1,40,128]{2,1,0:T(8,128)S(1)}, f32[1,40,128]{2,1,0:T(8,128)S(1)}, u32[]{:S(2)}, u32[]{:S(2)}) collective-permute-start(f32[1,40,128]{2,1,0:T(8,128)S(1)} %get-tuple-element.70), channel_id=1, source_target_pairs={{0,6},{1,7},{2,4},{3,5},{4,2},{5,3},{6,0},{7,1},{8,14},{9,15},{10,... | collective-permute-start | bytes 61448 | tf_op jit(solution)/shard_map/ppermute | solution.py:461
  65.8 7.3 %collective-permute-start.20 = (f32[1,40,128]{2,1,0:T(8,128)S(1)}, f32[1,40,128]{2,1,0:T(8,128)S(1)}, u32[]{:S(2)}, u32[]{:S(2)}) collective-permute-start(f32[1,40,128]{2,1,0:T(8,128)S(1)} %get-tuple-element.71), channel_id=1, source_target_pairs={{0,4},{1,5},{2,6},{3,7},{4,0},{5,1},{6,2},{7,3},{8,12},{9,13},{10,... | collective-permute-start | bytes 61448 | tf_op jit(solution)/shard_map/ppermute | solution.py:461
  65.9 7.3 %collective-permute-start.19 = (f32[1,40,128]{2,1,0:T(8,128)S(1)}, f32[1,40,128]{2,1,0:T(8,128)S(1)}, u32[]{:S(2)}, u32[]{:S(2)}) collective-permute-start(f32[1,40,128]{2,1,0:T(8,128)S(1)} %get-tuple-element.72), channel_id=1, source_target_pairs={{0,2},{1,3},{2,0},{3,1},{4,6},{5,7},{6,4},{7,5},{8,10},{9,11},{10,... | collective-permute-start | bytes 61448 | tf_op jit(solution)/shard_map/ppermute | solution.py:461
  (1 other events, 0.7 us)

commit v2 on v1

--- a/solution.py
+++ b/solution.py
@@ -30,6 +30,10 @@
 
 def ceil8(n):
     return (n + 7) // 8 * 8
+
+
+def odd_tiles(n):
+    return (n + 7) // 8 // 2 * 16 + 8 if (n + 7) // 8 % 2 == 0 else ceil8(n)
 
 
 def call(body, outs, scratch=(), flops=0, size=0, limit=8, **more):
@@ -224,8 +228,8 @@
 def mix_body(
     ms, order, factor, taps_i, taps_j, tile,
     feat, got_ra, got_rb, got_cb, kept, got, cot_ref,
-    src_ref, dconv_ref, row_a, row_b, edge_a, edge_b, grads_ref, chan_ref, small_ref,
-    conv_scr, cols_scr, kb_scr, win_scr, wout_scr, w1_scr, w2_scr, w4_scr, bias_scr,
+    src_out, dconv_ref, row_a, row_b, edge_a, edge_b, grads_ref, chan_ref, small_ref,
+    src_ref, conv_scr, cols_scr, kb_scr, win_scr, wout_scr, w1_scr, w2_scr, w4_scr, bias_scr,
     gw1_scr, gw2_scr, gb_scr, gg_scr, gs_scr, gc_scr, cot_sum,
 ):
     batch, rows, cols, C = feat.shape
@@ -249,6 +253,7 @@
         return got[at : at + m, :]
 
     fill(ms, src_ref, feat, got_ra, got_rb, col_a, got_cb)
+    src_out[...] = src_ref[...]
     columns = small_columns(read, hs, cs, count, me, order, cols_scr)
     cols_scr[...] = columns
     rows_form = columns.T
@@ -381,12 +386,14 @@
     chan_ref[5:6, :] = gb
 
 
-def kernel_grad_body(ms, order, factor, taps_i, taps_j, count, src_ref, dconv_ref, chan_ref, out_ref, acc_scr, rows_scr):
-    batch, rows, cols, C = dconv_ref.shape
+def kernel_grad_body(ms, order, factor, taps_i, taps_j, count, src_in, dconv_in, chan_ref, out_ref, src_ref, dconv_ref, acc_scr, rows_scr):
+    batch, rows, cols, C = dconv_in.shape
     m = taps_i // 2
     taps = taps_i * taps_j
     cs = C // count
     me = device_index(ms)
+    src_ref[...] = src_in[...]
+    dconv_ref[:, :, 0:cols, :] = dconv_in[...]
     acc_scr[...] = jnp.zeros_like(acc_scr)
 
     def step(b, _):
@@ -490,7 +497,7 @@
     cells = batch * rows * cols * count
     factor = 1.0 / math.sqrt(cells)
     slot = 2 * hs + 8
-    wide = ceil8(LEFT + cols + m)
+    wide = odd_tiles(LEFT + cols + m)
 
     vm = pltpu.VMEM
     vectors = [v.reshape(1, cs) for v in (conv_bias, norm_gain, norm_shift, out_bias, layer_scale)]
@@ -554,6 +561,7 @@
             shape(LANES, C),
         ),
         scratch=(
+            vm((batch, rows + 2 * m, wide, C), f32),
             vm((batch, rows, cols, C), f32),
             vm((C, LANES), f32),
             vm((taps, 8, C), f32),
@@ -582,6 +590,8 @@
         functools.partial(kernel_grad_body, ms, order, factor, taps_i, taps_j, count),
         shape(count, 8, LANES),
         scratch=(
+            vm((batch, rows + 2 * m, wide, C), f32),
+            vm((batch, rows, odd_tiles(cols), C), f32),
             vm((taps, 8, C), f32),
             vm((LANES, C), f32),
         ),

time: 74.1 us -> 75.5 us (1.019)
  waiting for transfers between devices: 13.8 us -> 15.6 us
  Pallas kernels: 31.5 us -> 29.9 us
  local copies, waits for them, and re-layouts: 0.77 us -> 2 us
    ppermute x3, waiting for transfers between devices: 0.89 us -> 2.62 us  [both_pairs(): lax.ppermute(b, axis, pairs(count, True))]
    pallas_call x1, Pallas kernels: 7.19 us -> 5.47 us  [per_device(): call(functools.partial(kernel_grad_body, ms, order, factor, taps_i, taps_...]
    unnamed x6 -> x8, local copies, waits for them, and re-layouts: 0.74 us -> 1.96 us
  transfers between devices with their start and end apart: 22 -> 22, of which waited for: 11 -> 12; matrix products, arithmetic and copies ran while one was open for 0% -> 0% of each run, Pallas kernels for 16% -> 14%
where the time goes in v2:
time: 75.5 us; the launch traced here: 75.2 us
  Pallas kernels  29.9 us (40%)
  starting transfers between devices  27 us (36%)
  waiting for transfers between devices  15.6 us (21%)
  local copies, waits for them, and re-layouts  2 us (3%)
    ppermute x15, starting transfers between devices, flip(): return lax.ppermute(x, AXES, [(i, i ^ mask) for i in range(count)])  16.6 us
    pallas_call x1, Pallas kernels, per_device(): call(functools.partial(mix_body, ms, order, factor, taps_i, taps_j, tile)...  16.2 us
    ppermute x15, waiting for transfers between devices, flip(): return lax.ppermute(x, AXES, [(i, i ^ mask) for i in range(count)])  13 us
    pallas_call x1, Pallas kernels, per_device(): call(functools.partial(kernel_grad_body, ms, order, factor, taps_i, taps_...  5.47 us
    pallas_call x1, Pallas kernels, per_device(): call(functools.partial(features_grad_body, ms, taps_i, taps_j), shape(bat...  5.31 us
    ppermute x3, starting transfers between devices, both_pairs(): lax.ppermute(b, axis, pairs(count, True))  4.54 us
    ppermute x3, starting transfers between devices, both_pairs(): lax.ppermute(a, axis, pairs(count, False))  3.61 us
    ppermute x3, waiting for transfers between devices, both_pairs(): lax.ppermute(b, axis, pairs(count, True))  2.62 us
  transfers between devices with their start and end apart: 22, of which 12 were waited for; matrix products, arithmetic and copies ran while one was open for 0% of the time, Pallas kernels for 14%

profile of v2, /device:TPU:0, one launch (start us, length us, event | category | flops | bytes accessed | tf_op | source)
XLA Modules:
  0.0 75.2 jit_solution(13105232967675605659)
XLA Ops:
  0.7 2.1 %shard_map.186 = (f32[40,128]{1,0:T(8,128)}, f32[2,3,64,128]{3,2,1,0:T(8,128)}, f32[2,3,64,128]{3,2,1,0:T(8,128)}) custom-call(f32[2,16,64,128]{3,2,1,0:T(8,128)} %feat.3, f32[7,4,7]{2,1,0:T(4,128)} %bitcast.29, f32[1,4]{1,0:T(1,128)} %bitcast.31, f32[1,4]{1,0:T(1,128)} %bitcast.32, f32[1,4]{1,0:T(1,128)} %bitcast.33, f32[1,4]{1,0:T(1,128)} %bitcast.34, ...), custom_call_target="tpu_custom_call" | custom-call | bytes 1000000 | tf_op jit(solution)/shard_map/pallas_call | solution.py:504
  2.7 3.0 %collective-permute-start = (f32[2,3,64,128]{3,2,1,0:T(8,128)}, f32[2,3,64,128]{3,2,1,0:T(8,128)S(1)}, u32[]{:S(2)}, u32[]{:S(2)}) collective-permute-start(f32[2,3,64,128]{3,2,1,0:T(8,128)} %get-tuple-element.40), channel_id=1, source_target_pairs={{0,8},{8,0},{16,24},{24,16},{1,9},{9,1},{17,25},{25,17},{2,10},{10... | collective-permute-start | bytes 589832 | tf_op jit(solution)/shard_map/ppermute | solution.py:90
  5.7 1.5 %collective-permute-start.1 = (f32[2,3,64,128]{3,2,1,0:T(8,128)}, f32[2,3,64,128]{3,2,1,0:T(8,128)S(1)}, u32[]{:S(2)}, u32[]{:S(2)}) collective-permute-start(f32[2,3,64,128]{3,2,1,0:T(8,128)} %get-tuple-element.41), channel_id=1, source_target_pairs={{0,24},{8,16},{16,8},{24,0},{1,25},{9,17},{17,9},{25,1},{2,26},{10... | collective-permute-start | bytes 589832 | tf_op jit(solution)/shard_map/ppermute | solution.py:90
  7.2 3.6 %collective-permute-start.4 = (f32[1,40,128]{2,1,0:T(8,128)}, f32[1,40,128]{2,1,0:T(8,128)S(1)}, u32[]{:S(2)}, u32[]{:S(2)}) collective-permute-start(f32[1,40,128]{2,1,0:T(8,128)} %bitcast.25), channel_id=1, source_target_pairs={{0,6},{1,7},{2,4},{3,5},{4,2},{5,3},{6,0},{7,1},{8,14},{9,15},{10,... | collective-permute-start | bytes 61448 | tf_op jit(solution)/shard_map/ppermute | solution.py:468
  11.6 1.5 %collective-permute-done.4.refs_3_ = f32[1,40,128]{2,1,0:T(8,128)S(1)} collective-permute-done((f32[1,40,128]{2,1,0:T(8,128)}, f32[1,40,128]{2,1,0:T(8,128)S(1)}, u32[]{:S(2)}, u32[]{:S(2)}) %collective-permute-start.4) | collective-permute-done | bytes 20512 | tf_op jit(solution)/shard_map/ppermute | solution.py:468
  13.1 2.7 %collective-permute-done.3.refs_2_ = f32[1,40,128]{2,1,0:T(8,128)S(1)} collective-permute-done((f32[1,40,128]{2,1,0:T(8,128)}, f32[1,40,128]{2,1,0:T(8,128)S(1)}, u32[]{:S(2)}, u32[]{:S(2)}) %collective-permute-start.3) | collective-permute-done | bytes 20512 | tf_op jit(solution)/shard_map/ppermute | solution.py:468
  16.3 1.2 %copy-done = f32[2,16,64,128]{3,2,1,0:T(8,128)S(1)} copy-done((f32[2,16,64,128]{3,2,1,0:T(8,128)S(1)}, f32[2,16,64,128]{3,2,1,0:T(8,128)}, u32[]{:S(2)}) %copy-start) | copy-done | bytes 1048600
  18.3 2.2 %collective-permute-start.5 = (f32[2,22,4,128]{3,2,1,0:T(4,128)S(1)}, f32[2,22,4,128]{3,2,1,0:T(4,128)S(1)}, u32[]{:S(2)}, u32[]{:S(2)}) collective-permute-start(f32[2,22,4,128]{3,2,1,0:T(4,128)S(1)} %get-tuple-element.43), channel_id=1, source_target_pairs={{0,7},{1,2},{2,1},{3,4},{4,3},{5,6},{6,5},{7,0},{8,15},{9,10},{10,... | collective-permute-start | bytes 270344 | tf_op jit(solution)/shard_map/ppermute | solution.py:537
  20.5 1.4 %collective-permute-start.8 = (f32[4,40,128]{2,1,0:T(8,128)S(1)}, f32[4,40,128]{2,1,0:T(8,128)S(1)}, u32[]{:S(2)}, u32[]{:S(2)}) collective-permute-start(f32[4,40,128]{2,1,0:T(8,128)S(1)} %get-tuple-element.45.refs_0_), channel_id=1, source_target_pairs={{0,24},{1,25},{2,26},{3,27},{4,28},{5,29},{6,30},{7,31},{8,16},{9,... | collective-permute-start | bytes 245768 | tf_op jit(solution)/shard_map/ppermute | solution.py:468
  22.0 1.5 %collective-permute-start.7 = (f32[4,40,128]{2,1,0:T(8,128)S(1)}, f32[4,40,128]{2,1,0:T(8,128)S(1)}, u32[]{:S(2)}, u32[]{:S(2)}) collective-permute-start(f32[4,40,128]{2,1,0:T(8,128)S(1)} %get-tuple-element.45.refs_0_), channel_id=1, source_target_pairs={{0,16},{1,17},{2,18},{3,19},{4,20},{5,21},{6,22},{7,23},{8,24},{9,... | collective-permute-start | bytes 245768 | tf_op jit(solution)/shard_map/ppermute | solution.py:468
  24.0 2.7 %collective-permute-done.8.refs_3_ = f32[4,40,128]{2,1,0:T(8,128)S(1)} collective-permute-done((f32[4,40,128]{2,1,0:T(8,128)S(1)}, f32[4,40,128]{2,1,0:T(8,128)S(1)}, u32[]{:S(2)}, u32[]{:S(2)}) %collective-permute-start.8) | collective-permute-done | bytes 81952 | tf_op jit(solution)/shard_map/ppermute | solution.py:468
  28.1 1.7 %collective-permute-done.9.got = f32[816,128]{1,0:T(8,128)S(1)} collective-permute-done((f32[816,128]{1,0:T(8,128)S(1)}, f32[816,128]{1,0:T(8,128)S(1)}, u32[]{:S(2)}, u32[]{:S(2)}) %collective-permute-start.9) | collective-permute-done | bytes 417824 | tf_op jit(solution)/shard_map/ppermute | solution.py:468
  29.8 16.2 %shard_map.189 = (f32[2,22,88,128]{3,2,1,0:T(8,128)S(1)}, f32[2,16,64,128]{3,2,1,0:T(8,128)S(1)}, f32[2,3,64,128]{3,2,1,0:T(8,128)S(1)}, f32[2,3,64,128]{3,2,1,0...) custom-call(f32[2,16,64,128]{3,2,1,0:T(8,128)S(1)} %copy-done.1, ...), custom_call_target="tpu_custom_call" | custom-call | flops 12000000000 | bytes 8000000 | tf_op jit(solution)/shard_map/pallas_call | solution.py:552
  46.6 1.4 %collective-permute-start.11 = (f32[2,3,64,128]{3,2,1,0:T(8,128)S(1)}, f32[2,3,64,128]{3,2,1,0:T(8,128)S(1)}, u32[]{:S(2)}, u32[]{:S(2)}) collective-permute-start(f32[2,3,64,128]{3,2,1,0:T(8,128)S(1)} %get-tuple-element.48), channel_id=1, source_target_pairs={{0,24},{8,16},{16,8},{24,0},{1,25},{9,17},{17,9},{25,1},{2,26},{10... | collective-permute-start | bytes 589832 | tf_op jit(solution)/shard_map/ppermute | solution.py:90
  48.1 5.5 %shard_map.190.small = f32[32,8,128]{2,1,0:T(8,128)S(1)} custom-call(f32[2,22,88,128]{3,2,1,0:T(8,128)S(1)} %get-tuple-element.52.src_in, f32[2,16,64,128]{3,2,1,0:T(8,128)S(1)} %get-tuple-element.46.dconv_in.inner, f32[8,512]{1,0:T(8,128)S(1)} %get-tuple-element.53.chan_ref), custom_call_target="tpu_custom_call" | custom-call | flops 4000000000 | bytes 4000000 | tf_op jit(solution)/shard_map/pallas_call | solution.py:589
  54.1 0.9 %collective-permute-done.13.small_got = f32[16,8,128]{2,1,0:T(8,128)S(1)} collective-permute-done((f32[16,8,128]{2,1,0:T(8,128)S(1)}, f32[16,8,128]{2,1,0:T(8,128)S(1)}, u32[]{:S(2)}, u32[]{:S(2)}) %collective-permute-start.13) | collective-permute-done | bytes 65568 | tf_op jit(solution)/shard_map/ppermute | solution.py:468
  55.1 2.1 %collective-permute-done.11.got_b.got_rb = f32[2,3,64,128]{3,2,1,0:T(8,128)S(1)} collective-permute-done((f32[2,3,64,128]{3,2,1,0:T(8,128)S(1)}, f32[2,3,64,128]{3,2,1,0:T(8,128)S(1)}, u32[]{:S(2)}, u32[]{:S(2)}) %collective-permute-start.11) | collective-permute-done | bytes 196640 | tf_op jit(solution)/shard_map/ppermute | solution.py:90
  58.0 1.4 %collective-permute-start.17 = (f32[4,40,128]{2,1,0:T(8,128)S(1)}, f32[4,40,128]{2,1,0:T(8,128)S(1)}, u32[]{:S(2)}, u32[]{:S(2)}) collective-permute-start(f32[4,40,128]{2,1,0:T(8,128)S(1)} %get-tuple-element.59), channel_id=1, source_target_pairs={{0,16},{1,17},{2,18},{3,19},{4,20},{5,21},{6,22},{7,23},{8,24},{9,... | collective-permute-start | bytes 245768 | tf_op jit(solution)/shard_map/ppermute | solution.py:468
  59.3 1.4 %collective-permute-start.18 = (f32[4,40,128]{2,1,0:T(8,128)S(1)}, f32[4,40,128]{2,1,0:T(8,128)S(1)}, u32[]{:S(2)}, u32[]{:S(2)}) collective-permute-start(f32[4,40,128]{2,1,0:T(8,128)S(1)} %get-tuple-element.60), channel_id=1, source_target_pairs={{0,24},{1,25},{2,26},{3,27},{4,28},{5,29},{6,30},{7,31},{8,16},{9,... | collective-permute-start | bytes 245768 | tf_op jit(solution)/shard_map/ppermute | solution.py:468
  60.8 1.6 %collective-permute-start.15 = (f32[2,22,4,128]{3,2,1,0:T(4,128)S(1)}, f32[2,22,4,128]{3,2,1,0:T(4,128)S(1)}, u32[]{:S(2)}, u32[]{:S(2)}) collective-permute-start(f32[2,22,4,128]{3,2,1,0:T(4,128)S(1)} %get-tuple-element.55), channel_id=1, source_target_pairs={{0,7},{1,2},{2,1},{3,4},{4,3},{5,6},{6,5},{7,0},{8,15},{9,10},{10,... | collective-permute-start | bytes 270344 | tf_op jit(solution)/shard_map/ppermute | solution.py:90
  63.3 1.4 %collective-permute-done.18 = f32[4,40,128]{2,1,0:T(8,128)S(1)} collective-permute-done((f32[4,40,128]{2,1,0:T(8,128)S(1)}, f32[4,40,128]{2,1,0:T(8,128)S(1)}, u32[]{:S(2)}, u32[]{:S(2)}) %collective-permute-start.18) | collective-permute-done | bytes 81952 | tf_op jit(solution)/shard_map/ppermute | solution.py:468
  64.7 1.6 %collective-permute-start.21 = (f32[1,40,128]{2,1,0:T(8,128)S(1)}, f32[1,40,128]{2,1,0:T(8,128)S(1)}, u32[]{:S(2)}, u32[]{:S(2)}) collective-permute-start(f32[1,40,128]{2,1,0:T(8,128)S(1)} %get-tuple-element.70), channel_id=1, source_target_pairs={{0,6},{1,7},{2,4},{3,5},{4,2},{5,3},{6,0},{7,1},{8,14},{9,15},{10,... | collective-permute-start | bytes 61448 | tf_op jit(solution)/shard_map/ppermute | solution.py:468
  66.6 2.6 %collective-permute-start.19 = (f32[1,40,128]{2,1,0:T(8,128)S(1)}, f32[1,40,128]{2,1,0:T(8,128)S(1)}, u32[]{:S(2)}, u32[]{:S(2)}) collective-permute-start(f32[1,40,128]{2,1,0:T(8,128)S(1)} %get-tuple-element.72), channel_id=1, source_target_pairs={{0,2},{1,3},{2,0},{3,1},{4,6},{5,7},{6,4},{7,5},{8,10},{9,11},{10,... | collective-permute-start | bytes 61448 | tf_op jit(solution)/shard_map/ppermute | solution.py:468
  69.2 5.3 %shard_map.192 = f32[2,16,64,128]{3,2,1,0:T(8,128)} custom-call(f32[2,16,64,128]{3,2,1,0:T(8,128)S(1)} %get-tuple-element.46.dconv_in.inner, f32[2,3,64,128]{3,2,1,0:T(8,128)S(1)} %collective-permute-done.10.got_a.got_ra, f32[2,3,64,128]{3,2,1,0:T(8,128)S(1)} %collective-permute-done.11.got_b.got_rb, f32[2,22,4,128]{3,2,1,0:T(4,128)S(1)} %collective-permute-done.14.got_ca, ...), custom_call_target="tpu_custom_call" | custom-call | flops 4000000000 | bytes 4000000 | tf_op jit(solution)/shard_map/pallas_call | solution.py:618
  (40 shorter events, 8.0 us)
Async XLA Ops:
  0.6 29.2 %copy-start.1 = (f32[2,16,64,128]{3,2,1,0:T(8,128)S(1)}, f32[2,16,64,128]{3,2,1,0:T(8,128)}, u32[]{:S(2)}) copy-start(f32[2,16,64,128]{3,2,1,0:T(8,128)} %feat.3) | copy-start | bytes 3145732
  2.7 13.0 %collective-permute-start = (f32[2,3,64,128]{3,2,1,0:T(8,128)}, f32[2,3,64,128]{3,2,1,0:T(8,128)S(1)}, u32[]{:S(2)}, u32[]{:S(2)}) collective-permute-start(f32[2,3,64,128]{3,2,1,0:T(8,128)} %get-tuple-element.40), channel_id=1, source_target_pairs={{0,8},{8,0},{16,24},{24,16},{1,9},{9,1},{17,25},{25,17},{2,10},{10... | collective-permute-start | bytes 589832 | tf_op jit(solution)/shard_map/ppermute | solution.py:90
  5.7 10.5 %collective-permute-start.1 = (f32[2,3,64,128]{3,2,1,0:T(8,128)}, f32[2,3,64,128]{3,2,1,0:T(8,128)S(1)}, u32[]{:S(2)}, u32[]{:S(2)}) collective-permute-start(f32[2,3,64,128]{3,2,1,0:T(8,128)} %get-tuple-element.41), channel_id=1, source_target_pairs={{0,24},{8,16},{16,8},{24,0},{1,25},{9,17},{17,9},{25,1},{2,26},{10... | collective-permute-start | bytes 589832 | tf_op jit(solution)/shard_map/ppermute | solution.py:90
  7.2 5.8 %collective-permute-start.4 = (f32[1,40,128]{2,1,0:T(8,128)}, f32[1,40,128]{2,1,0:T(8,128)S(1)}, u32[]{:S(2)}, u32[]{:S(2)}) collective-permute-start(f32[1,40,128]{2,1,0:T(8,128)} %bitcast.25), channel_id=1, source_target_pairs={{0,6},{1,7},{2,4},{3,5},{4,2},{5,3},{6,0},{7,1},{8,14},{9,15},{10,... | collective-permute-start | bytes 61448 | tf_op jit(solution)/shard_map/ppermute | solution.py:468
  10.8 4.9 %collective-permute-start.3 = (f32[1,40,128]{2,1,0:T(8,128)}, f32[1,40,128]{2,1,0:T(8,128)S(1)}, u32[]{:S(2)}, u32[]{:S(2)}) collective-permute-start(f32[1,40,128]{2,1,0:T(8,128)} %bitcast.26), channel_id=1, source_target_pairs={{0,4},{1,5},{2,6},{3,7},{4,0},{5,1},{6,2},{7,3},{8,12},{9,13},{10,... | collective-permute-start | bytes 61448 | tf_op jit(solution)/shard_map/ppermute | solution.py:468
  10.8 4.9 %collective-permute-start.2 = (f32[1,40,128]{2,1,0:T(8,128)}, f32[1,40,128]{2,1,0:T(8,128)S(1)}, u32[]{:S(2)}, u32[]{:S(2)}) collective-permute-start(f32[1,40,128]{2,1,0:T(8,128)} %bitcast.27), channel_id=1, source_target_pairs={{0,2},{1,3},{2,0},{3,1},{4,6},{5,7},{6,4},{7,5},{8,10},{9,11},{10,... | collective-permute-start | bytes 61448 | tf_op jit(solution)/shard_map/ppermute | solution.py:468
  18.2 11.6 %copy-start.3 = (f32[2,16,64,128]{3,2,1,0:T(8,128)S(1)}, f32[2,16,64,128]{3,2,1,0:T(8,128)}, u32[]{:S(2)}) copy-start(f32[2,16,64,128]{3,2,1,0:T(8,128)} %cot_ref.3) | copy-start | bytes 3145732
  18.3 9.6 %collective-permute-start.5 = (f32[2,22,4,128]{3,2,1,0:T(4,128)S(1)}, f32[2,22,4,128]{3,2,1,0:T(4,128)S(1)}, u32[]{:S(2)}, u32[]{:S(2)}) collective-permute-start(f32[2,22,4,128]{3,2,1,0:T(4,128)S(1)} %get-tuple-element.43), channel_id=1, source_target_pairs={{0,7},{1,2},{2,1},{3,4},{4,3},{5,6},{6,5},{7,0},{8,15},{9,10},{10,... | collective-permute-start | bytes 270344 | tf_op jit(solution)/shard_map/ppermute | solution.py:537
  20.5 6.2 %collective-permute-start.8 = (f32[4,40,128]{2,1,0:T(8,128)S(1)}, f32[4,40,128]{2,1,0:T(8,128)S(1)}, u32[]{:S(2)}, u32[]{:S(2)}) collective-permute-start(f32[4,40,128]{2,1,0:T(8,128)S(1)} %get-tuple-element.45.refs_0_), channel_id=1, source_target_pairs={{0,24},{1,25},{2,26},{3,27},{4,28},{5,29},{6,30},{7,31},{8,16},{9,... | collective-permute-start | bytes 245768 | tf_op jit(solution)/shard_map/ppermute | solution.py:468
  22.0 5.1 %collective-permute-start.7 = (f32[4,40,128]{2,1,0:T(8,128)S(1)}, f32[4,40,128]{2,1,0:T(8,128)S(1)}, u32[]{:S(2)}, u32[]{:S(2)}) collective-permute-start(f32[4,40,128]{2,1,0:T(8,128)S(1)} %get-tuple-element.45.refs_0_), channel_id=1, source_target_pairs={{0,16},{1,17},{2,18},{3,19},{4,20},{5,21},{6,22},{7,23},{8,24},{9,... | collective-permute-start | bytes 245768 | tf_op jit(solution)/shard_map/ppermute | solution.py:468
  23.5 4.4 %collective-permute-start.6 = (f32[4,40,128]{2,1,0:T(8,128)S(1)}, f32[4,40,128]{2,1,0:T(8,128)S(1)}, u32[]{:S(2)}, u32[]{:S(2)}) collective-permute-start(f32[4,40,128]{2,1,0:T(8,128)S(1)} %get-tuple-element.45.refs_0_), channel_id=1, source_target_pairs={{0,8},{1,9},{2,10},{3,11},{4,12},{5,13},{6,14},{7,15},{8,0},{9,1},... | collective-permute-start | bytes 245768 | tf_op jit(solution)/shard_map/ppermute | solution.py:468
  28.0 1.8 %collective-permute-start.9 = (f32[816,128]{1,0:T(8,128)S(1)}, f32[816,128]{1,0:T(8,128)S(1)}, u32[]{:S(2)}, u32[]{:S(2)}) collective-permute-start(f32[816,128]{1,0:T(8,128)S(1)} %shard_map.188.kept), channel_id=1, source_target_pairs={{0,1},{1,0},{2,3},{3,2},{4,5},{5,4},{6,7},{7,6},{8,9},{9,8},{10,11... | collective-permute-start | bytes 1253384 | tf_op jit(solution)/shard_map/ppermute | solution.py:468
  46.0 9.1 %collective-permute-start.10 = (f32[2,3,64,128]{3,2,1,0:T(8,128)S(1)}, f32[2,3,64,128]{3,2,1,0:T(8,128)S(1)}, u32[]{:S(2)}, u32[]{:S(2)}) collective-permute-start(f32[2,3,64,128]{3,2,1,0:T(8,128)S(1)} %get-tuple-element.47), channel_id=1, source_target_pairs={{0,8},{8,0},{16,24},{24,16},{1,9},{9,1},{17,25},{25,17},{2,10},{10... | collective-permute-start | bytes 589832 | tf_op jit(solution)/shard_map/ppermute | solution.py:90
  46.6 10.6 %collective-permute-start.11 = (f32[2,3,64,128]{3,2,1,0:T(8,128)S(1)}, f32[2,3,64,128]{3,2,1,0:T(8,128)S(1)}, u32[]{:S(2)}, u32[]{:S(2)}) collective-permute-start(f32[2,3,64,128]{3,2,1,0:T(8,128)S(1)} %get-tuple-element.48), channel_id=1, source_target_pairs={{0,24},{8,16},{16,8},{24,0},{1,25},{9,17},{17,9},{25,1},{2,26},{10... | collective-permute-start | bytes 589832 | tf_op jit(solution)/shard_map/ppermute | solution.py:90
  48.0 9.1 %collective-permute-start.12 = (f32[16,32,128]{2,1,0:T(8,128)S(1)}, f32[16,32,128]{2,1,0:T(8,128)S(1)}, u32[]{:S(2)}, u32[]{:S(2)}) collective-permute-start(f32[16,32,128]{2,1,0:T(8,128)S(1)} %slice.18), channel_id=1, source_target_pairs={{0,1},{1,0},{2,3},{3,2},{4,5},{5,4},{6,7},{7,6},{8,9},{9,8},{10,11... | collective-permute-start | bytes 786440 | tf_op jit(solution)/shard_map/ppermute | solution.py:468
  53.6 1.5 %collective-permute-start.13 = (f32[16,8,128]{2,1,0:T(8,128)S(1)}, f32[16,8,128]{2,1,0:T(8,128)S(1)}, u32[]{:S(2)}, u32[]{:S(2)}) collective-permute-start(f32[16,8,128]{2,1,0:T(8,128)S(1)} %slice.24), channel_id=1, source_target_pairs={{0,1},{1,0},{2,3},{3,2},{4,5},{5,4},{6,7},{7,6},{8,9},{9,8},{10,11... | collective-permute-start | bytes 196616 | tf_op jit(solution)/shard_map/ppermute | solution.py:468
  57.2 5.3 %collective-permute-start.16 = (f32[4,40,128]{2,1,0:T(8,128)S(1)}, f32[4,40,128]{2,1,0:T(8,128)S(1)}, u32[]{:S(2)}, u32[]{:S(2)}) collective-permute-start(f32[4,40,128]{2,1,0:T(8,128)S(1)} %get-tuple-element.58), channel_id=1, source_target_pairs={{0,8},{1,9},{2,10},{3,11},{4,12},{5,13},{6,14},{7,15},{8,0},{9,1},... | collective-permute-start | bytes 245768 | tf_op jit(solution)/shard_map/ppermute | solution.py:468
  58.0 5.3 %collective-permute-start.17 = (f32[4,40,128]{2,1,0:T(8,128)S(1)}, f32[4,40,128]{2,1,0:T(8,128)S(1)}, u32[]{:S(2)}, u32[]{:S(2)}) collective-permute-start(f32[4,40,128]{2,1,0:T(8,128)S(1)} %get-tuple-element.59), channel_id=1, source_target_pairs={{0,16},{1,17},{2,18},{3,19},{4,20},{5,21},{6,22},{7,23},{8,24},{9,... | collective-permute-start | bytes 245768 | tf_op jit(solution)/shard_map/ppermute | solution.py:468
  59.3 5.3 %collective-permute-start.18 = (f32[4,40,128]{2,1,0:T(8,128)S(1)}, f32[4,40,128]{2,1,0:T(8,128)S(1)}, u32[]{:S(2)}, u32[]{:S(2)}) collective-permute-start(f32[4,40,128]{2,1,0:T(8,128)S(1)} %get-tuple-element.60), channel_id=1, source_target_pairs={{0,24},{1,25},{2,26},{3,27},{4,28},{5,29},{6,30},{7,31},{8,16},{9,... | collective-permute-start | bytes 245768 | tf_op jit(solution)/shard_map/ppermute | solution.py:468
  60.8 8.4 %collective-permute-start.14 = (f32[2,22,4,128]{3,2,1,0:T(4,128)S(1)}, f32[2,22,4,128]{3,2,1,0:T(4,128)S(1)}, u32[]{:S(2)}, u32[]{:S(2)}) collective-permute-start(f32[2,22,4,128]{3,2,1,0:T(4,128)S(1)} %get-tuple-element.54), channel_id=1, source_target_pairs={{0,1},{1,0},{2,3},{3,2},{4,5},{5,4},{6,7},{7,6},{8,9},{9,8},{10,11... | collective-permute-start | bytes 270344 | tf_op jit(solution)/shard_map/ppermute | solution.py:90
  60.8 8.4 %collective-permute-start.15 = (f32[2,22,4,128]{3,2,1,0:T(4,128)S(1)}, f32[2,22,4,128]{3,2,1,0:T(4,128)S(1)}, u32[]{:S(2)}, u32[]{:S(2)}) collective-permute-start(f32[2,22,4,128]{3,2,1,0:T(4,128)S(1)} %get-tuple-element.55), channel_id=1, source_target_pairs={{0,7},{1,2},{2,1},{3,4},{4,3},{5,6},{6,5},{7,0},{8,15},{9,10},{10,... | collective-permute-start | bytes 270344 | tf_op jit(solution)/shard_map/ppermute | solution.py:90
  64.7 9.8 %collective-permute-start.21 = (f32[1,40,128]{2,1,0:T(8,128)S(1)}, f32[1,40,128]{2,1,0:T(8,128)S(1)}, u32[]{:S(2)}, u32[]{:S(2)}) collective-permute-start(f32[1,40,128]{2,1,0:T(8,128)S(1)} %get-tuple-element.70), channel_id=1, source_target_pairs={{0,6},{1,7},{2,4},{3,5},{4,2},{5,3},{6,0},{7,1},{8,14},{9,15},{10,... | collective-permute-start | bytes 61448 | tf_op jit(solution)/shard_map/ppermute | solution.py:468
  66.3 8.2 %collective-permute-start.20 = (f32[1,40,128]{2,1,0:T(8,128)S(1)}, f32[1,40,128]{2,1,0:T(8,128)S(1)}, u32[]{:S(2)}, u32[]{:S(2)}) collective-permute-start(f32[1,40,128]{2,1,0:T(8,128)S(1)} %get-tuple-element.71), channel_id=1, source_target_pairs={{0,4},{1,5},{2,6},{3,7},{4,0},{5,1},{6,2},{7,3},{8,12},{9,13},{10,... | collective-permute-start | bytes 61448 | tf_op jit(solution)/shard_map/ppermute | solution.py:468
  66.6 7.9 %collective-permute-start.19 = (f32[1,40,128]{2,1,0:T(8,128)S(1)}, f32[1,40,128]{2,1,0:T(8,128)S(1)}, u32[]{:S(2)}, u32[]{:S(2)}) collective-permute-start(f32[1,40,128]{2,1,0:T(8,128)S(1)} %get-tuple-element.72), channel_id=1, source_target_pairs={{0,2},{1,3},{2,0},{3,1},{4,6},{5,7},{6,4},{7,5},{8,10},{9,11},{10,... | collective-permute-start | bytes 61448 | tf_op jit(solution)/shard_map/ppermute | solution.py:468
  (2 other events, 2.0 us)

commit v3 on v2

--- a/solution.py
+++ b/solution.py
@@ -30,10 +30,6 @@
 
 def ceil8(n):
     return (n + 7) // 8 * 8
-
-
-def odd_tiles(n):
-    return (n + 7) // 8 // 2 * 16 + 8 if (n + 7) // 8 % 2 == 0 else ceil8(n)
 
 
 def call(body, outs, scratch=(), flops=0, size=0, limit=8, **more):
@@ -497,7 +493,7 @@
     cells = batch * rows * cols * count
     factor = 1.0 / math.sqrt(cells)
     slot = 2 * hs + 8
-    wide = odd_tiles(LEFT + cols + m)
+    wide = ceil8(LEFT + cols + m)
 
     vm = pltpu.VMEM
     vectors = [v.reshape(1, cs) for v in (conv_bias, norm_gain, norm_shift, out_bias, layer_scale)]
@@ -548,7 +544,7 @@
     last = groups[-1][0]
     order += [last ^ x for x in order]
     got = flip(message, last, count)
-    tile = 8 * cols
+    tile = rows * cols
     src, dconv, d_row_a, d_row_b, d_edge_a, d_edge_b, grads, chan, small = call(
         functools.partial(mix_body, ms, order, factor, taps_i, taps_j, tile),
         (
@@ -591,7 +587,7 @@
         shape(count, 8, LANES),
         scratch=(
             vm((batch, rows + 2 * m, wide, C), f32),
-            vm((batch, rows, odd_tiles(cols), C), f32),
+            vm((batch, rows, cols + 8, C), f32),
             vm((taps, 8, C), f32),
             vm((LANES, C), f32),
         ),

time: 75.5 us -> 71.8 us (0.951)
  Pallas kernels: 29.9 us -> 27 us
  local copies, waits for them, and re-layouts: 2 us -> 0.77 us
    pallas_call x1, Pallas kernels: 16.2 us -> 14.4 us  [per_device(): call(functools.partial(mix_body, ms, order, factor, taps_i, taps_j, tile)...]
    unnamed x8 -> x6, local copies, waits for them, and re-layouts: 1.96 us -> 0.74 us
  transfers between devices with their start and end apart: 22 -> 22, of which waited for: 12 -> 12; matrix products, arithmetic and copies ran while one was open for 0% -> 0% of each run, Pallas kernels for 14% -> 13%
where the time goes in v3:
time: 71.8 us; the launch traced here: 71.6 us
  Pallas kernels  27 us (38%)
  starting transfers between devices  26.9 us (37%)
  waiting for transfers between devices  16.2 us (23%)
  local copies, waits for them, and re-layouts  0.77 us (1%)
  between operations  0.74 us (1%)
    ppermute x15, starting transfers between devices, flip(): return lax.ppermute(x, AXES, [(i, i ^ mask) for i in range(count)])  16.6 us
    pallas_call x1, Pallas kernels, per_device(): call(functools.partial(mix_body, ms, order, factor, taps_i, taps_j, tile)...  14.4 us
    ppermute x15, waiting for transfers between devices, flip(): return lax.ppermute(x, AXES, [(i, i ^ mask) for i in range(count)])  12.9 us
    pallas_call x1, Pallas kernels, per_device(): call(functools.partial(kernel_grad_body, ms, order, factor, taps_i, taps_...  4.92 us
    pallas_call x1, Pallas kernels, per_device(): call(functools.partial(features_grad_body, ms, taps_i, taps_j), shape(bat...  4.64 us
    ppermute x3, starting transfers between devices, both_pairs(): lax.ppermute(b, axis, pairs(count, True))  4.54 us
    ppermute x3, starting transfers between devices, both_pairs(): lax.ppermute(a, axis, pairs(count, False))  3.61 us
    ppermute x3, waiting for transfers between devices, both_pairs(): lax.ppermute(b, axis, pairs(count, True))  3.2 us
  transfers between devices with their start and end apart: 22, of which 12 were waited for; matrix products, arithmetic and copies ran while one was open for 0% of the time, Pallas kernels for 13%

profile of v3, /device:TPU:0, one launch (start us, length us, event | category | flops | bytes accessed | tf_op | source)
XLA Modules:
  0.0 71.6 jit_solution(4337135726288692615)
XLA Ops:
  0.7 2.1 %shard_map.186 = (f32[40,128]{1,0:T(8,128)}, f32[2,3,64,128]{3,2,1,0:T(8,128)}, f32[2,3,64,128]{3,2,1,0:T(8,128)}) custom-call(f32[2,16,64,128]{3,2,1,0:T(8,128)} %feat.3, f32[7,4,7]{2,1,0:T(4,128)} %bitcast.29, f32[1,4]{1,0:T(1,128)} %bitcast.31, f32[1,4]{1,0:T(1,128)} %bitcast.32, f32[1,4]{1,0:T(1,128)} %bitcast.33, f32[1,4]{1,0:T(1,128)} %bitcast.34, ...), custom_call_target="tpu_custom_call" | custom-call | bytes 1000000 | tf_op jit(solution)/shard_map/pallas_call | solution.py:500
  2.7 3.0 %collective-permute-start = (f32[2,3,64,128]{3,2,1,0:T(8,128)}, f32[2,3,64,128]{3,2,1,0:T(8,128)S(1)}, u32[]{:S(2)}, u32[]{:S(2)}) collective-permute-start(f32[2,3,64,128]{3,2,1,0:T(8,128)} %get-tuple-element.40), channel_id=1, source_target_pairs={{0,8},{8,0},{16,24},{24,16},{1,9},{9,1},{17,25},{25,17},{2,10},{10... | collective-permute-start | bytes 589832 | tf_op jit(solution)/shard_map/ppermute | solution.py:86
  5.7 1.5 %collective-permute-start.1 = (f32[2,3,64,128]{3,2,1,0:T(8,128)}, f32[2,3,64,128]{3,2,1,0:T(8,128)S(1)}, u32[]{:S(2)}, u32[]{:S(2)}) collective-permute-start(f32[2,3,64,128]{3,2,1,0:T(8,128)} %get-tuple-element.41), channel_id=1, source_target_pairs={{0,24},{8,16},{16,8},{24,0},{1,25},{9,17},{17,9},{25,1},{2,26},{10... | collective-permute-start | bytes 589832 | tf_op jit(solution)/shard_map/ppermute | solution.py:86
  7.2 3.6 %collective-permute-start.4 = (f32[1,40,128]{2,1,0:T(8,128)}, f32[1,40,128]{2,1,0:T(8,128)S(1)}, u32[]{:S(2)}, u32[]{:S(2)}) collective-permute-start(f32[1,40,128]{2,1,0:T(8,128)} %bitcast.25), channel_id=1, source_target_pairs={{0,6},{1,7},{2,4},{3,5},{4,2},{5,3},{6,0},{7,1},{8,14},{9,15},{10,... | collective-permute-start | bytes 61448 | tf_op jit(solution)/shard_map/ppermute | solution.py:464
  11.6 1.5 %collective-permute-done.4.refs_3_ = f32[1,40,128]{2,1,0:T(8,128)S(1)} collective-permute-done((f32[1,40,128]{2,1,0:T(8,128)}, f32[1,40,128]{2,1,0:T(8,128)S(1)}, u32[]{:S(2)}, u32[]{:S(2)}) %collective-permute-start.4) | collective-permute-done | bytes 20512 | tf_op jit(solution)/shard_map/ppermute | solution.py:464
  13.1 2.7 %collective-permute-done.3.refs_2_ = f32[1,40,128]{2,1,0:T(8,128)S(1)} collective-permute-done((f32[1,40,128]{2,1,0:T(8,128)}, f32[1,40,128]{2,1,0:T(8,128)S(1)}, u32[]{:S(2)}, u32[]{:S(2)}) %collective-permute-start.3) | collective-permute-done | bytes 20512 | tf_op jit(solution)/shard_map/ppermute | solution.py:464
  17.1 2.2 %collective-permute-start.5 = (f32[2,22,4,128]{3,2,1,0:T(4,128)S(1)}, f32[2,22,4,128]{3,2,1,0:T(4,128)S(1)}, u32[]{:S(2)}, u32[]{:S(2)}) collective-permute-start(f32[2,22,4,128]{3,2,1,0:T(4,128)S(1)} %get-tuple-element.43), channel_id=1, source_target_pairs={{0,7},{1,2},{2,1},{3,4},{4,3},{5,6},{6,5},{7,0},{8,15},{9,10},{10,... | collective-permute-start | bytes 270344 | tf_op jit(solution)/shard_map/ppermute | solution.py:533
  19.3 1.4 %collective-permute-start.8 = (f32[4,40,128]{2,1,0:T(8,128)S(1)}, f32[4,40,128]{2,1,0:T(8,128)S(1)}, u32[]{:S(2)}, u32[]{:S(2)}) collective-permute-start(f32[4,40,128]{2,1,0:T(8,128)S(1)} %get-tuple-element.45.refs_0_), channel_id=1, source_target_pairs={{0,24},{1,25},{2,26},{3,27},{4,28},{5,29},{6,30},{7,31},{8,16},{9,... | collective-permute-start | bytes 245768 | tf_op jit(solution)/shard_map/ppermute | solution.py:464
  20.8 1.5 %collective-permute-start.7 = (f32[4,40,128]{2,1,0:T(8,128)S(1)}, f32[4,40,128]{2,1,0:T(8,128)S(1)}, u32[]{:S(2)}, u32[]{:S(2)}) collective-permute-start(f32[4,40,128]{2,1,0:T(8,128)S(1)} %get-tuple-element.45.refs_0_), channel_id=1, source_target_pairs={{0,16},{1,17},{2,18},{3,19},{4,20},{5,21},{6,22},{7,23},{8,24},{9,... | collective-permute-start | bytes 245768 | tf_op jit(solution)/shard_map/ppermute | solution.py:464
  22.8 2.7 %collective-permute-done.8.refs_3_ = f32[4,40,128]{2,1,0:T(8,128)S(1)} collective-permute-done((f32[4,40,128]{2,1,0:T(8,128)S(1)}, f32[4,40,128]{2,1,0:T(8,128)S(1)}, u32[]{:S(2)}, u32[]{:S(2)}) %collective-permute-start.8) | collective-permute-done | bytes 81952 | tf_op jit(solution)/shard_map/ppermute | solution.py:464
  25.8 0.9 %collective-permute-done.6.refs_1_ = f32[4,40,128]{2,1,0:T(8,128)S(1)} collective-permute-done((f32[4,40,128]{2,1,0:T(8,128)S(1)}, f32[4,40,128]{2,1,0:T(8,128)S(1)}, u32[]{:S(2)}, u32[]{:S(2)}) %collective-permute-start.6) | collective-permute-done | bytes 81952 | tf_op jit(solution)/shard_map/ppermute | solution.py:464
  26.8 1.7 %collective-permute-done.9.got = f32[816,128]{1,0:T(8,128)S(1)} collective-permute-done((f32[816,128]{1,0:T(8,128)S(1)}, f32[816,128]{1,0:T(8,128)S(1)}, u32[]{:S(2)}, u32[]{:S(2)}) %collective-permute-start.9) | collective-permute-done | bytes 417824 | tf_op jit(solution)/shard_map/ppermute | solution.py:464
  28.6 14.4 %shard_map.189 = (f32[2,22,80,128]{3,2,1,0:T(8,128)S(1)}, f32[2,16,64,128]{3,2,1,0:T(8,128)S(1)}, f32[2,3,64,128]{3,2,1,0:T(8,128)S(1)}, f32[2,3,64,128]{3,2,1,0...) custom-call(f32[2,16,64,128]{3,2,1,0:T(8,128)S(1)} %copy-done, ...), custom_call_target="tpu_custom_call" | custom-call | flops 12000000000 | bytes 8000000 | tf_op jit(solution)/shard_map/pallas_call | solution.py:548
  43.6 1.4 %collective-permute-start.11 = (f32[2,3,64,128]{3,2,1,0:T(8,128)S(1)}, f32[2,3,64,128]{3,2,1,0:T(8,128)S(1)}, u32[]{:S(2)}, u32[]{:S(2)}) collective-permute-start(f32[2,3,64,128]{3,2,1,0:T(8,128)S(1)} %get-tuple-element.48), channel_id=1, source_target_pairs={{0,24},{8,16},{16,8},{24,0},{1,25},{9,17},{17,9},{25,1},{2,26},{10... | collective-permute-start | bytes 589832 | tf_op jit(solution)/shard_map/ppermute | solution.py:86
  45.2 4.9 %shard_map.190.small = f32[32,8,128]{2,1,0:T(8,128)S(1)} custom-call(f32[2,22,80,128]{3,2,1,0:T(8,128)S(1)} %get-tuple-element.52.src_in, f32[2,16,64,128]{3,2,1,0:T(8,128)S(1)} %get-tuple-element.46.dconv_in.inner, f32[8,512]{1,0:T(8,128)S(1)} %get-tuple-element.53.chan_ref), custom_call_target="tpu_custom_call" | custom-call | flops 4000000000 | bytes 4000000 | tf_op jit(solution)/shard_map/pallas_call | solution.py:585
  50.6 0.9 %collective-permute-done.13.small_got = f32[16,8,128]{2,1,0:T(8,128)S(1)} collective-permute-done((f32[16,8,128]{2,1,0:T(8,128)S(1)}, f32[16,8,128]{2,1,0:T(8,128)S(1)}, u32[]{:S(2)}, u32[]{:S(2)}) %collective-permute-start.13) | collective-permute-done | bytes 65568 | tf_op jit(solution)/shard_map/ppermute | solution.py:464
  51.5 2.7 %collective-permute-done.11.got_b.got_rb = f32[2,3,64,128]{3,2,1,0:T(8,128)S(1)} collective-permute-done((f32[2,3,64,128]{3,2,1,0:T(8,128)S(1)}, f32[2,3,64,128]{3,2,1,0:T(8,128)S(1)}, u32[]{:S(2)}, u32[]{:S(2)}) %collective-permute-start.11) | collective-permute-done | bytes 196640 | tf_op jit(solution)/shard_map/ppermute | solution.py:86
  55.0 1.4 %collective-permute-start.17 = (f32[4,40,128]{2,1,0:T(8,128)S(1)}, f32[4,40,128]{2,1,0:T(8,128)S(1)}, u32[]{:S(2)}, u32[]{:S(2)}) collective-permute-start(f32[4,40,128]{2,1,0:T(8,128)S(1)} %get-tuple-element.59), channel_id=1, source_target_pairs={{0,16},{1,17},{2,18},{3,19},{4,20},{5,21},{6,22},{7,23},{8,24},{9,... | collective-permute-start | bytes 245768 | tf_op jit(solution)/shard_map/ppermute | solution.py:464
  56.4 1.4 %collective-permute-start.18 = (f32[4,40,128]{2,1,0:T(8,128)S(1)}, f32[4,40,128]{2,1,0:T(8,128)S(1)}, u32[]{:S(2)}, u32[]{:S(2)}) collective-permute-start(f32[4,40,128]{2,1,0:T(8,128)S(1)} %get-tuple-element.60), channel_id=1, source_target_pairs={{0,24},{1,25},{2,26},{3,27},{4,28},{5,29},{6,30},{7,31},{8,16},{9,... | collective-permute-start | bytes 245768 | tf_op jit(solution)/shard_map/ppermute | solution.py:464
  57.8 1.6 %collective-permute-start.15 = (f32[2,22,4,128]{3,2,1,0:T(4,128)S(1)}, f32[2,22,4,128]{3,2,1,0:T(4,128)S(1)}, u32[]{:S(2)}, u32[]{:S(2)}) collective-permute-start(f32[2,22,4,128]{3,2,1,0:T(4,128)S(1)} %get-tuple-element.55), channel_id=1, source_target_pairs={{0,7},{1,2},{2,1},{3,4},{4,3},{5,6},{6,5},{7,0},{8,15},{9,10},{10,... | collective-permute-start | bytes 270344 | tf_op jit(solution)/shard_map/ppermute | solution.py:86
  60.3 1.4 %collective-permute-done.18 = f32[4,40,128]{2,1,0:T(8,128)S(1)} collective-permute-done((f32[4,40,128]{2,1,0:T(8,128)S(1)}, f32[4,40,128]{2,1,0:T(8,128)S(1)}, u32[]{:S(2)}, u32[]{:S(2)}) %collective-permute-start.18) | collective-permute-done | bytes 81952 | tf_op jit(solution)/shard_map/ppermute | solution.py:464
  61.8 1.6 %collective-permute-start.21 = (f32[1,40,128]{2,1,0:T(8,128)S(1)}, f32[1,40,128]{2,1,0:T(8,128)S(1)}, u32[]{:S(2)}, u32[]{:S(2)}) collective-permute-start(f32[1,40,128]{2,1,0:T(8,128)S(1)} %get-tuple-element.70), channel_id=1, source_target_pairs={{0,6},{1,7},{2,4},{3,5},{4,2},{5,3},{6,0},{7,1},{8,14},{9,15},{10,... | collective-permute-start | bytes 61448 | tf_op jit(solution)/shard_map/ppermute | solution.py:464
  63.6 2.6 %collective-permute-start.19 = (f32[1,40,128]{2,1,0:T(8,128)S(1)}, f32[1,40,128]{2,1,0:T(8,128)S(1)}, u32[]{:S(2)}, u32[]{:S(2)}) collective-permute-start(f32[1,40,128]{2,1,0:T(8,128)S(1)} %get-tuple-element.72), channel_id=1, source_target_pairs={{0,2},{1,3},{2,0},{3,1},{4,6},{5,7},{6,4},{7,5},{8,10},{9,11},{10,... | collective-permute-start | bytes 61448 | tf_op jit(solution)/shard_map/ppermute | solution.py:464
  66.2 4.6 %shard_map.192 = f32[2,16,64,128]{3,2,1,0:T(8,128)} custom-call(f32[2,16,64,128]{3,2,1,0:T(8,128)S(1)} %get-tuple-element.46.dconv_in.inner, f32[2,3,64,128]{3,2,1,0:T(8,128)S(1)} %collective-permute-done.10.got_a.got_ra, f32[2,3,64,128]{3,2,1,0:T(8,128)S(1)} %collective-permute-done.11.got_b.got_rb, f32[2,22,4,128]{3,2,1,0:T(4,128)S(1)} %collective-permute-done.14.got_ca, ...), custom_call_target="tpu_custom_call" | custom-call | flops 4000000000 | bytes 4000000 | tf_op jit(solution)/shard_map/pallas_call | solution.py:614
  (38 shorter events, 7.1 us)
Async XLA Ops:
  0.6 15.6 %copy-start = (f32[2,16,64,128]{3,2,1,0:T(8,128)S(1)}, f32[2,16,64,128]{3,2,1,0:T(8,128)}, u32[]{:S(2)}) copy-start(f32[2,16,64,128]{3,2,1,0:T(8,128)} %feat.3) | copy-start | bytes 3145732
  2.7 13.0 %collective-permute-start = (f32[2,3,64,128]{3,2,1,0:T(8,128)}, f32[2,3,64,128]{3,2,1,0:T(8,128)S(1)}, u32[]{:S(2)}, u32[]{:S(2)}) collective-permute-start(f32[2,3,64,128]{3,2,1,0:T(8,128)} %get-tuple-element.40), channel_id=1, source_target_pairs={{0,8},{8,0},{16,24},{24,16},{1,9},{9,1},{17,25},{25,17},{2,10},{10... | collective-permute-start | bytes 589832 | tf_op jit(solution)/shard_map/ppermute | solution.py:86
  5.7 10.5 %collective-permute-start.1 = (f32[2,3,64,128]{3,2,1,0:T(8,128)}, f32[2,3,64,128]{3,2,1,0:T(8,128)S(1)}, u32[]{:S(2)}, u32[]{:S(2)}) collective-permute-start(f32[2,3,64,128]{3,2,1,0:T(8,128)} %get-tuple-element.41), channel_id=1, source_target_pairs={{0,24},{8,16},{16,8},{24,0},{1,25},{9,17},{17,9},{25,1},{2,26},{10... | collective-permute-start | bytes 589832 | tf_op jit(solution)/shard_map/ppermute | solution.py:86
  7.2 5.8 %collective-permute-start.4 = (f32[1,40,128]{2,1,0:T(8,128)}, f32[1,40,128]{2,1,0:T(8,128)S(1)}, u32[]{:S(2)}, u32[]{:S(2)}) collective-permute-start(f32[1,40,128]{2,1,0:T(8,128)} %bitcast.25), channel_id=1, source_target_pairs={{0,6},{1,7},{2,4},{3,5},{4,2},{5,3},{6,0},{7,1},{8,14},{9,15},{10,... | collective-permute-start | bytes 61448 | tf_op jit(solution)/shard_map/ppermute | solution.py:464
  10.8 4.9 %collective-permute-start.3 = (f32[1,40,128]{2,1,0:T(8,128)}, f32[1,40,128]{2,1,0:T(8,128)S(1)}, u32[]{:S(2)}, u32[]{:S(2)}) collective-permute-start(f32[1,40,128]{2,1,0:T(8,128)} %bitcast.26), channel_id=1, source_target_pairs={{0,4},{1,5},{2,6},{3,7},{4,0},{5,1},{6,2},{7,3},{8,12},{9,13},{10,... | collective-permute-start | bytes 61448 | tf_op jit(solution)/shard_map/ppermute | solution.py:464
  10.8 4.9 %collective-permute-start.2 = (f32[1,40,128]{2,1,0:T(8,128)}, f32[1,40,128]{2,1,0:T(8,128)S(1)}, u32[]{:S(2)}, u32[]{:S(2)}) collective-permute-start(f32[1,40,128]{2,1,0:T(8,128)} %bitcast.27), channel_id=1, source_target_pairs={{0,2},{1,3},{2,0},{3,1},{4,6},{5,7},{6,4},{7,5},{8,10},{9,11},{10,... | collective-permute-start | bytes 61448 | tf_op jit(solution)/shard_map/ppermute | solution.py:464
  17.0 11.6 %copy-start.2 = (f32[2,16,64,128]{3,2,1,0:T(8,128)S(1)}, f32[2,16,64,128]{3,2,1,0:T(8,128)}, u32[]{:S(2)}) copy-start(f32[2,16,64,128]{3,2,1,0:T(8,128)} %cot_ref.3) | copy-start | bytes 3145732
  17.1 9.6 %collective-permute-start.5 = (f32[2,22,4,128]{3,2,1,0:T(4,128)S(1)}, f32[2,22,4,128]{3,2,1,0:T(4,128)S(1)}, u32[]{:S(2)}, u32[]{:S(2)}) collective-permute-start(f32[2,22,4,128]{3,2,1,0:T(4,128)S(1)} %get-tuple-element.43), channel_id=1, source_target_pairs={{0,7},{1,2},{2,1},{3,4},{4,3},{5,6},{6,5},{7,0},{8,15},{9,10},{10,... | collective-permute-start | bytes 270344 | tf_op jit(solution)/shard_map/ppermute | solution.py:533
  19.3 6.2 %collective-permute-start.8 = (f32[4,40,128]{2,1,0:T(8,128)S(1)}, f32[4,40,128]{2,1,0:T(8,128)S(1)}, u32[]{:S(2)}, u32[]{:S(2)}) collective-permute-start(f32[4,40,128]{2,1,0:T(8,128)S(1)} %get-tuple-element.45.refs_0_), channel_id=1, source_target_pairs={{0,24},{1,25},{2,26},{3,27},{4,28},{5,29},{6,30},{7,31},{8,16},{9,... | collective-permute-start | bytes 245768 | tf_op jit(solution)/shard_map/ppermute | solution.py:464
  20.8 5.1 %collective-permute-start.7 = (f32[4,40,128]{2,1,0:T(8,128)S(1)}, f32[4,40,128]{2,1,0:T(8,128)S(1)}, u32[]{:S(2)}, u32[]{:S(2)}) collective-permute-start(f32[4,40,128]{2,1,0:T(8,128)S(1)} %get-tuple-element.45.refs_0_), channel_id=1, source_target_pairs={{0,16},{1,17},{2,18},{3,19},{4,20},{5,21},{6,22},{7,23},{8,24},{9,... | collective-permute-start | bytes 245768 | tf_op jit(solution)/shard_map/ppermute | solution.py:464
  22.3 4.4 %collective-permute-start.6 = (f32[4,40,128]{2,1,0:T(8,128)S(1)}, f32[4,40,128]{2,1,0:T(8,128)S(1)}, u32[]{:S(2)}, u32[]{:S(2)}) collective-permute-start(f32[4,40,128]{2,1,0:T(8,128)S(1)} %get-tuple-element.45.refs_0_), channel_id=1, source_target_pairs={{0,8},{1,9},{2,10},{3,11},{4,12},{5,13},{6,14},{7,15},{8,0},{9,1},... | collective-permute-start | bytes 245768 | tf_op jit(solution)/shard_map/ppermute | solution.py:464
  26.8 1.8 %collective-permute-start.9 = (f32[816,128]{1,0:T(8,128)S(1)}, f32[816,128]{1,0:T(8,128)S(1)}, u32[]{:S(2)}, u32[]{:S(2)}) collective-permute-start(f32[816,128]{1,0:T(8,128)S(1)} %shard_map.188.kept), channel_id=1, source_target_pairs={{0,1},{1,0},{2,3},{3,2},{4,5},{5,4},{6,7},{7,6},{8,9},{9,8},{10,11... | collective-permute-start | bytes 1253384 | tf_op jit(solution)/shard_map/ppermute | solution.py:464
  43.0 8.5 %collective-permute-start.10 = (f32[2,3,64,128]{3,2,1,0:T(8,128)S(1)}, f32[2,3,64,128]{3,2,1,0:T(8,128)S(1)}, u32[]{:S(2)}, u32[]{:S(2)}) collective-permute-start(f32[2,3,64,128]{3,2,1,0:T(8,128)S(1)} %get-tuple-element.47), channel_id=1, source_target_pairs={{0,8},{8,0},{16,24},{24,16},{1,9},{9,1},{17,25},{25,17},{2,10},{10... | collective-permute-start | bytes 589832 | tf_op jit(solution)/shard_map/ppermute | solution.py:86
  43.6 10.6 %collective-permute-start.11 = (f32[2,3,64,128]{3,2,1,0:T(8,128)S(1)}, f32[2,3,64,128]{3,2,1,0:T(8,128)S(1)}, u32[]{:S(2)}, u32[]{:S(2)}) collective-permute-start(f32[2,3,64,128]{3,2,1,0:T(8,128)S(1)} %get-tuple-element.48), channel_id=1, source_target_pairs={{0,24},{8,16},{16,8},{24,0},{1,25},{9,17},{17,9},{25,1},{2,26},{10... | collective-permute-start | bytes 589832 | tf_op jit(solution)/shard_map/ppermute | solution.py:86
  45.1 9.1 %collective-permute-start.12 = (f32[16,32,128]{2,1,0:T(8,128)S(1)}, f32[16,32,128]{2,1,0:T(8,128)S(1)}, u32[]{:S(2)}, u32[]{:S(2)}) collective-permute-start(f32[16,32,128]{2,1,0:T(8,128)S(1)} %slice.18), channel_id=1, source_target_pairs={{0,1},{1,0},{2,3},{3,2},{4,5},{5,4},{6,7},{7,6},{8,9},{9,8},{10,11... | collective-permute-start | bytes 786440 | tf_op jit(solution)/shard_map/ppermute | solution.py:464
  50.1 1.4 %collective-permute-start.13 = (f32[16,8,128]{2,1,0:T(8,128)S(1)}, f32[16,8,128]{2,1,0:T(8,128)S(1)}, u32[]{:S(2)}, u32[]{:S(2)}) collective-permute-start(f32[16,8,128]{2,1,0:T(8,128)S(1)} %slice.24), channel_id=1, source_target_pairs={{0,1},{1,0},{2,3},{3,2},{4,5},{5,4},{6,7},{7,6},{8,9},{9,8},{10,11... | collective-permute-start | bytes 196616 | tf_op jit(solution)/shard_map/ppermute | solution.py:464
  54.3 5.3 %collective-permute-start.16 = (f32[4,40,128]{2,1,0:T(8,128)S(1)}, f32[4,40,128]{2,1,0:T(8,128)S(1)}, u32[]{:S(2)}, u32[]{:S(2)}) collective-permute-start(f32[4,40,128]{2,1,0:T(8,128)S(1)} %get-tuple-element.58), channel_id=1, source_target_pairs={{0,8},{1,9},{2,10},{3,11},{4,12},{5,13},{6,14},{7,15},{8,0},{9,1},... | collective-permute-start | bytes 245768 | tf_op jit(solution)/shard_map/ppermute | solution.py:464
  55.0 5.3 %collective-permute-start.17 = (f32[4,40,128]{2,1,0:T(8,128)S(1)}, f32[4,40,128]{2,1,0:T(8,128)S(1)}, u32[]{:S(2)}, u32[]{:S(2)}) collective-permute-start(f32[4,40,128]{2,1,0:T(8,128)S(1)} %get-tuple-element.59), channel_id=1, source_target_pairs={{0,16},{1,17},{2,18},{3,19},{4,20},{5,21},{6,22},{7,23},{8,24},{9,... | collective-permute-start | bytes 245768 | tf_op jit(solution)/shard_map/ppermute | solution.py:464
  56.4 5.3 %collective-permute-start.18 = (f32[4,40,128]{2,1,0:T(8,128)S(1)}, f32[4,40,128]{2,1,0:T(8,128)S(1)}, u32[]{:S(2)}, u32[]{:S(2)}) collective-permute-start(f32[4,40,128]{2,1,0:T(8,128)S(1)} %get-tuple-element.60), channel_id=1, source_target_pairs={{0,24},{1,25},{2,26},{3,27},{4,28},{5,29},{6,30},{7,31},{8,16},{9,... | collective-permute-start | bytes 245768 | tf_op jit(solution)/shard_map/ppermute | solution.py:464
  57.8 8.4 %collective-permute-start.14 = (f32[2,22,4,128]{3,2,1,0:T(4,128)S(1)}, f32[2,22,4,128]{3,2,1,0:T(4,128)S(1)}, u32[]{:S(2)}, u32[]{:S(2)}) collective-permute-start(f32[2,22,4,128]{3,2,1,0:T(4,128)S(1)} %get-tuple-element.54), channel_id=1, source_target_pairs={{0,1},{1,0},{2,3},{3,2},{4,5},{5,4},{6,7},{7,6},{8,9},{9,8},{10,11... | collective-permute-start | bytes 270344 | tf_op jit(solution)/shard_map/ppermute | solution.py:86
  57.8 8.4 %collective-permute-start.15 = (f32[2,22,4,128]{3,2,1,0:T(4,128)S(1)}, f32[2,22,4,128]{3,2,1,0:T(4,128)S(1)}, u32[]{:S(2)}, u32[]{:S(2)}) collective-permute-start(f32[2,22,4,128]{3,2,1,0:T(4,128)S(1)} %get-tuple-element.55), channel_id=1, source_target_pairs={{0,7},{1,2},{2,1},{3,4},{4,3},{5,6},{6,5},{7,0},{8,15},{9,10},{10,... | collective-permute-start | bytes 270344 | tf_op jit(solution)/shard_map/ppermute | solution.py:86
  61.8 9.1 %collective-permute-start.21 = (f32[1,40,128]{2,1,0:T(8,128)S(1)}, f32[1,40,128]{2,1,0:T(8,128)S(1)}, u32[]{:S(2)}, u32[]{:S(2)}) collective-permute-start(f32[1,40,128]{2,1,0:T(8,128)S(1)} %get-tuple-element.70), channel_id=1, source_target_pairs={{0,6},{1,7},{2,4},{3,5},{4,2},{5,3},{6,0},{7,1},{8,14},{9,15},{10,... | collective-permute-start | bytes 61448 | tf_op jit(solution)/shard_map/ppermute | solution.py:464
  63.3 7.5 %collective-permute-start.20 = (f32[1,40,128]{2,1,0:T(8,128)S(1)}, f32[1,40,128]{2,1,0:T(8,128)S(1)}, u32[]{:S(2)}, u32[]{:S(2)}) collective-permute-start(f32[1,40,128]{2,1,0:T(8,128)S(1)} %get-tuple-element.71), channel_id=1, source_target_pairs={{0,4},{1,5},{2,6},{3,7},{4,0},{5,1},{6,2},{7,3},{8,12},{9,13},{10,... | collective-permute-start | bytes 61448 | tf_op jit(solution)/shard_map/ppermute | solution.py:464
  63.6 7.3 %collective-permute-start.19 = (f32[1,40,128]{2,1,0:T(8,128)S(1)}, f32[1,40,128]{2,1,0:T(8,128)S(1)}, u32[]{:S(2)}, u32[]{:S(2)}) collective-permute-start(f32[1,40,128]{2,1,0:T(8,128)S(1)} %get-tuple-element.72), channel_id=1, source_target_pairs={{0,2},{1,3},{2,0},{3,1},{4,6},{5,7},{6,4},{7,5},{8,10},{9,11},{10,... | collective-permute-start | bytes 61448 | tf_op jit(solution)/shard_map/ppermute | solution.py:464
  (1 other events, 0.7 us)

commit v4 on v3

--- a/solution.py
+++ b/solution.py
@@ -278,23 +278,17 @@
     w4_scr[0:C, :] = th
     w4_scr[C : 2 * C, :] = tl
 
-    def conv_step(b, _):
-        for q in range(0, cols, 8):
-            acc = depthwise_block(
-                lambda r, j: src_ref[b, r, LEFT - m + q + j : LEFT - m + q + j + 8, :],
-                lambda i, j: kb_scr[i * taps_j + j],
-                rows, taps_i, taps_j, [conv_bias] * rows,
-            )
-            for p in range(rows):
-                conv_scr[b, p, q : q + 8, :] = acc[p]
-        return 0
-
-    lax.fori_loop(0, batch, conv_step, 0)
+    def conv_block(b, q):
+        acc = depthwise_block(
+            lambda r, j: src_ref[b, r, LEFT - m + q + j : LEFT - m + q + j + 8, :],
+            lambda i, j: kb_scr[i * taps_j + j],
+            rows, taps_i, taps_j, [conv_bias] * rows,
+        )
+        for p in range(rows):
+            conv_scr[b, p, q : q + 8, :] = acc[p]
 
     for ref in (gw1_scr, gw2_scr, gb_scr, gg_scr, gs_scr, gc_scr, cot_sum):
         ref[...] = jnp.zeros_like(ref)
-    tile_rows = tile // cols
-    per_image = rows // tile_rows
     gain = cols_scr[:, taps + 1 : taps + 2]
     shift = cols_scr[:, taps + 2 : taps + 3]
 
@@ -304,10 +298,8 @@
             total = total + x[:, k : k + LANES]
         return total
 
-    def step(t, _):
-        b = t // per_image
-        p0 = (t % per_image) * tile_rows
-        x = conv_scr[b, pl.ds(p0, tile_rows)].reshape(tile, C).T
+    def image(b):
+        x = conv_scr[b].reshape(tile, C).T
         mean = jnp.mean(x, axis=0, keepdims=True)
         centred = x - mean
         variance = jnp.mean(centred * centred, axis=0, keepdims=True)
@@ -315,10 +307,12 @@
         normed = centred * inverse
         lin = normed * gain + shift
         lh, ll = split(lin)
-        cot = cot_ref[b, pl.ds(p0, tile_rows)].reshape(tile, C)
+        cot = cot_ref[b].reshape(tile, C)
         ch, cl = split(cot)
+        yield
         act = dot(w1_scr[...], jnp.concatenate([lh, lh, ll], axis=0), NN)
         d_hid = dot(w2_scr[...], jnp.concatenate([ch, ch, cl], axis=1), NT)
+        yield
         bias = bias_scr[...]
         act = act + jnp.concatenate([bias] * (tile // LANES), axis=1)
         e = jnp.exp2((act * act) * (-half_log2e))
@@ -332,15 +326,18 @@
         phi = jnp.where(act > 0, 1.0 - q, q)
         hidden = act * phi
         d_act = d_hid * (phi + act * e * inverse_root_twopi)
+        yield
         hh, hl = split(hidden)
         dh, dl = split(d_act)
         gb_scr[...] += lanes_sum(d_act)
         both = dot(w4_scr[...], dh, NN)
         d_lin = both[0:C] + both[C : 2 * C] + dot(w4_scr[0:C, :], dl, NN)
+        yield
         gw1_scr[...] += dot(dh, jnp.concatenate([lh, ll], axis=0), NT)
         gw1_scr[:, 0:C] += dot(dl, lh, NT)
         gw2_scr[...] += dot(hh, jnp.concatenate([ch, cl], axis=1), NN)
         gw2_scr[:, 0:C] += dot(hl, ch, NN)
+        yield
         gg_scr[...] += lanes_sum(d_lin * normed)
         gs_scr[...] += lanes_sum(d_lin)
         d_norm = d_lin * gain
@@ -350,11 +347,22 @@
             - normed * jnp.mean(d_norm * normed, axis=0, keepdims=True)
         )
         gc_scr[...] += lanes_sum(d_conv)
-        dconv_ref[b, pl.ds(p0, tile_rows)] = d_conv.T.reshape(tile_rows, cols, C)
+        dconv_ref[b] = d_conv.T.reshape(rows, cols, C)
         cot_sum[...] += jnp.sum(cot.reshape(tile // 8, 8, C), axis=0)
-        return 0
-
-    lax.fori_loop(0, batch * per_image, step, 0)
+
+    blocks = list(range(0, cols, 8))
+    for q in blocks:
+        conv_block(0, q)
+    for b in range(batch):
+        ahead = list(blocks) if b + 1 < batch else []
+        stages = 5
+        share = -(-len(ahead) // stages)
+        for _ in image(b):
+            for q in ahead[:share]:
+                conv_block(b + 1, q)
+            ahead = ahead[share:]
+        for q in ahead:
+            conv_block(b + 1, q)
 
     even_r, even_c = even("row"), even("col")
     row_a[...] = dconv_ref[:, pl.ds(jnp.where(even_r, rows - m, 0), m)]

time: 71.8 us -> 71.2 us (level)
  no operation moved by 1% of the time
where the time goes in v4:
time: 71.2 us; the launch traced here: 71 us
  starting transfers between devices  27 us (38%)
  Pallas kernels  26.3 us (37%)
  waiting for transfers between devices  16.1 us (23%)
  local copies, waits for them, and re-layouts  0.77 us (1%)
  between operations  0.74 us (1%)
    ppermute x15, starting transfers between devices, flip(): return lax.ppermute(x, AXES, [(i, i ^ mask) for i in range(count)])  16.6 us
    pallas_call x1, Pallas kernels, per_device(): call(functools.partial(mix_body, ms, order, factor, taps_i, taps_j, tile)...  13.8 us
    ppermute x15, waiting for transfers between devices, flip(): return lax.ppermute(x, AXES, [(i, i ^ mask) for i in range(count)])  12.9 us
    pallas_call x1, Pallas kernels, per_device(): call(functools.partial(kernel_grad_body, ms, order, factor, taps_i, taps_...  4.89 us
    pallas_call x1, Pallas kernels, per_device(): call(functools.partial(features_grad_body, ms, taps_i, taps_j), shape(bat...  4.64 us
    ppermute x3, starting transfers between devices, both_pairs(): lax.ppermute(b, axis, pairs(count, True))  4.58 us
    ppermute x3, starting transfers between devices, both_pairs(): lax.ppermute(a, axis, pairs(count, False))  3.59 us
    ppermute x3, waiting for transfers between devices, both_pairs(): lax.ppermute(b, axis, pairs(count, True))  3.21 us
  transfers between devices with their start and end apart: 22, of which 12 were waited for; matrix products, arithmetic and copies ran while one was open for 0% of the time, Pallas kernels for 13%

profile of v4, /device:TPU:0, one launch (start us, length us, event | category | flops | bytes accessed | tf_op | source)
XLA Modules:
  0.0 71.0 jit_solution(14630988192686214175)
XLA Ops:
  0.7 2.1 %shard_map.186 = (f32[40,128]{1,0:T(8,128)}, f32[2,3,64,128]{3,2,1,0:T(8,128)}, f32[2,3,64,128]{3,2,1,0:T(8,128)}) custom-call(f32[2,16,64,128]{3,2,1,0:T(8,128)} %feat.3, f32[7,4,7]{2,1,0:T(4,128)} %bitcast.29, f32[1,4]{1,0:T(1,128)} %bitcast.31, f32[1,4]{1,0:T(1,128)} %bitcast.32, f32[1,4]{1,0:T(1,128)} %bitcast.33, f32[1,4]{1,0:T(1,128)} %bitcast.34, ...), custom_call_target="tpu_custom_call" | custom-call | bytes 1000000 | tf_op jit(solution)/shard_map/pallas_call | solution.py:508
  2.7 3.0 %collective-permute-start = (f32[2,3,64,128]{3,2,1,0:T(8,128)}, f32[2,3,64,128]{3,2,1,0:T(8,128)S(1)}, u32[]{:S(2)}, u32[]{:S(2)}) collective-permute-start(f32[2,3,64,128]{3,2,1,0:T(8,128)} %get-tuple-element.40), channel_id=1, source_target_pairs={{0,8},{8,0},{16,24},{24,16},{1,9},{9,1},{17,25},{25,17},{2,10},{10... | collective-permute-start | bytes 589832 | tf_op jit(solution)/shard_map/ppermute | solution.py:86
  5.7 1.5 %collective-permute-start.1 = (f32[2,3,64,128]{3,2,1,0:T(8,128)}, f32[2,3,64,128]{3,2,1,0:T(8,128)S(1)}, u32[]{:S(2)}, u32[]{:S(2)}) collective-permute-start(f32[2,3,64,128]{3,2,1,0:T(8,128)} %get-tuple-element.41), channel_id=1, source_target_pairs={{0,24},{8,16},{16,8},{24,0},{1,25},{9,17},{17,9},{25,1},{2,26},{10... | collective-permute-start | bytes 589832 | tf_op jit(solution)/shard_map/ppermute | solution.py:86
  7.2 3.6 %collective-permute-start.4 = (f32[1,40,128]{2,1,0:T(8,128)}, f32[1,40,128]{2,1,0:T(8,128)S(1)}, u32[]{:S(2)}, u32[]{:S(2)}) collective-permute-start(f32[1,40,128]{2,1,0:T(8,128)} %bitcast.25), channel_id=1, source_target_pairs={{0,6},{1,7},{2,4},{3,5},{4,2},{5,3},{6,0},{7,1},{8,14},{9,15},{10,... | collective-permute-start | bytes 61448 | tf_op jit(solution)/shard_map/ppermute | solution.py:472
  11.6 1.5 %collective-permute-done.4.refs_3_ = f32[1,40,128]{2,1,0:T(8,128)S(1)} collective-permute-done((f32[1,40,128]{2,1,0:T(8,128)}, f32[1,40,128]{2,1,0:T(8,128)S(1)}, u32[]{:S(2)}, u32[]{:S(2)}) %collective-permute-start.4) | collective-permute-done | bytes 20512 | tf_op jit(solution)/shard_map/ppermute | solution.py:472
  13.1 2.7 %collective-permute-done.3.refs_2_ = f32[1,40,128]{2,1,0:T(8,128)S(1)} collective-permute-done((f32[1,40,128]{2,1,0:T(8,128)}, f32[1,40,128]{2,1,0:T(8,128)S(1)}, u32[]{:S(2)}, u32[]{:S(2)}) %collective-permute-start.3) | collective-permute-done | bytes 20512 | tf_op jit(solution)/shard_map/ppermute | solution.py:472
  17.1 2.2 %collective-permute-start.5 = (f32[2,22,4,128]{3,2,1,0:T(4,128)S(1)}, f32[2,22,4,128]{3,2,1,0:T(4,128)S(1)}, u32[]{:S(2)}, u32[]{:S(2)}) collective-permute-start(f32[2,22,4,128]{3,2,1,0:T(4,128)S(1)} %get-tuple-element.43), channel_id=1, source_target_pairs={{0,7},{1,2},{2,1},{3,4},{4,3},{5,6},{6,5},{7,0},{8,15},{9,10},{10,... | collective-permute-start | bytes 270344 | tf_op jit(solution)/shard_map/ppermute | solution.py:541
  19.3 1.4 %collective-permute-start.8 = (f32[4,40,128]{2,1,0:T(8,128)S(1)}, f32[4,40,128]{2,1,0:T(8,128)S(1)}, u32[]{:S(2)}, u32[]{:S(2)}) collective-permute-start(f32[4,40,128]{2,1,0:T(8,128)S(1)} %get-tuple-element.45.refs_0_), channel_id=1, source_target_pairs={{0,24},{1,25},{2,26},{3,27},{4,28},{5,29},{6,30},{7,31},{8,16},{9,... | collective-permute-start | bytes 245768 | tf_op jit(solution)/shard_map/ppermute | solution.py:472
  20.8 1.5 %collective-permute-start.7 = (f32[4,40,128]{2,1,0:T(8,128)S(1)}, f32[4,40,128]{2,1,0:T(8,128)S(1)}, u32[]{:S(2)}, u32[]{:S(2)}) collective-permute-start(f32[4,40,128]{2,1,0:T(8,128)S(1)} %get-tuple-element.45.refs_0_), channel_id=1, source_target_pairs={{0,16},{1,17},{2,18},{3,19},{4,20},{5,21},{6,22},{7,23},{8,24},{9,... | collective-permute-start | bytes 245768 | tf_op jit(solution)/shard_map/ppermute | solution.py:472
  22.8 2.7 %collective-permute-done.8.refs_3_ = f32[4,40,128]{2,1,0:T(8,128)S(1)} collective-permute-done((f32[4,40,128]{2,1,0:T(8,128)S(1)}, f32[4,40,128]{2,1,0:T(8,128)S(1)}, u32[]{:S(2)}, u32[]{:S(2)}) %collective-permute-start.8) | collective-permute-done | bytes 81952 | tf_op jit(solution)/shard_map/ppermute | solution.py:472
  25.8 0.9 %collective-permute-done.6.refs_1_ = f32[4,40,128]{2,1,0:T(8,128)S(1)} collective-permute-done((f32[4,40,128]{2,1,0:T(8,128)S(1)}, f32[4,40,128]{2,1,0:T(8,128)S(1)}, u32[]{:S(2)}, u32[]{:S(2)}) %collective-permute-start.6) | collective-permute-done | bytes 81952 | tf_op jit(solution)/shard_map/ppermute | solution.py:472
  26.8 1.7 %collective-permute-done.9.got = f32[816,128]{1,0:T(8,128)S(1)} collective-permute-done((f32[816,128]{1,0:T(8,128)S(1)}, f32[816,128]{1,0:T(8,128)S(1)}, u32[]{:S(2)}, u32[]{:S(2)}) %collective-permute-start.9) | collective-permute-done | bytes 417824 | tf_op jit(solution)/shard_map/ppermute | solution.py:472
  28.6 13.8 %shard_map.189 = (f32[2,22,80,128]{3,2,1,0:T(8,128)S(1)}, f32[2,16,64,128]{3,2,1,0:T(8,128)S(1)}, f32[2,3,64,128]{3,2,1,0:T(8,128)S(1)}, f32[2,3,64,128]{3,2,1,0...) custom-call(f32[2,16,64,128]{3,2,1,0:T(8,128)S(1)} %copy-done, ...), custom_call_target="tpu_custom_call" | custom-call | flops 12000000000 | bytes 8000000 | tf_op jit(solution)/shard_map/pallas_call | solution.py:556
  43.0 1.5 %collective-permute-start.11 = (f32[2,3,64,128]{3,2,1,0:T(8,128)S(1)}, f32[2,3,64,128]{3,2,1,0:T(8,128)S(1)}, u32[]{:S(2)}, u32[]{:S(2)}) collective-permute-start(f32[2,3,64,128]{3,2,1,0:T(8,128)S(1)} %get-tuple-element.48), channel_id=1, source_target_pairs={{0,24},{8,16},{16,8},{24,0},{1,25},{9,17},{17,9},{25,1},{2,26},{10... | collective-permute-start | bytes 589832 | tf_op jit(solution)/shard_map/ppermute | solution.py:86
  44.5 4.9 %shard_map.190.small = f32[32,8,128]{2,1,0:T(8,128)S(1)} custom-call(f32[2,22,80,128]{3,2,1,0:T(8,128)S(1)} %get-tuple-element.52.src_in, f32[2,16,64,128]{3,2,1,0:T(8,128)S(1)} %get-tuple-element.46.dconv_in.inner, f32[8,512]{1,0:T(8,128)S(1)} %get-tuple-element.53.chan_ref), custom_call_target="tpu_custom_call" | custom-call | flops 4000000000 | bytes 4000000 | tf_op jit(solution)/shard_map/pallas_call | solution.py:593
  50.0 0.9 %collective-permute-done.13.small_got = f32[16,8,128]{2,1,0:T(8,128)S(1)} collective-permute-done((f32[16,8,128]{2,1,0:T(8,128)S(1)}, f32[16,8,128]{2,1,0:T(8,128)S(1)}, u32[]{:S(2)}, u32[]{:S(2)}) %collective-permute-start.13) | collective-permute-done | bytes 65568 | tf_op jit(solution)/shard_map/ppermute | solution.py:472
  50.9 2.7 %collective-permute-done.11.got_b.got_rb = f32[2,3,64,128]{3,2,1,0:T(8,128)S(1)} collective-permute-done((f32[2,3,64,128]{3,2,1,0:T(8,128)S(1)}, f32[2,3,64,128]{3,2,1,0:T(8,128)S(1)}, u32[]{:S(2)}, u32[]{:S(2)}) %collective-permute-start.11) | collective-permute-done | bytes 196640 | tf_op jit(solution)/shard_map/ppermute | solution.py:86
  54.4 1.4 %collective-permute-start.17 = (f32[4,40,128]{2,1,0:T(8,128)S(1)}, f32[4,40,128]{2,1,0:T(8,128)S(1)}, u32[]{:S(2)}, u32[]{:S(2)}) collective-permute-start(f32[4,40,128]{2,1,0:T(8,128)S(1)} %get-tuple-element.59), channel_id=1, source_target_pairs={{0,16},{1,17},{2,18},{3,19},{4,20},{5,21},{6,22},{7,23},{8,24},{9,... | collective-permute-start | bytes 245768 | tf_op jit(solution)/shard_map/ppermute | solution.py:472
  55.7 1.5 %collective-permute-start.18 = (f32[4,40,128]{2,1,0:T(8,128)S(1)}, f32[4,40,128]{2,1,0:T(8,128)S(1)}, u32[]{:S(2)}, u32[]{:S(2)}) collective-permute-start(f32[4,40,128]{2,1,0:T(8,128)S(1)} %get-tuple-element.60), channel_id=1, source_target_pairs={{0,24},{1,25},{2,26},{3,27},{4,28},{5,29},{6,30},{7,31},{8,16},{9,... | collective-permute-start | bytes 245768 | tf_op jit(solution)/shard_map/ppermute | solution.py:472
  57.2 1.6 %collective-permute-start.15 = (f32[2,22,4,128]{3,2,1,0:T(4,128)S(1)}, f32[2,22,4,128]{3,2,1,0:T(4,128)S(1)}, u32[]{:S(2)}, u32[]{:S(2)}) collective-permute-start(f32[2,22,4,128]{3,2,1,0:T(4,128)S(1)} %get-tuple-element.55), channel_id=1, source_target_pairs={{0,7},{1,2},{2,1},{3,4},{4,3},{5,6},{6,5},{7,0},{8,15},{9,10},{10,... | collective-permute-start | bytes 270344 | tf_op jit(solution)/shard_map/ppermute | solution.py:86
  59.7 1.4 %collective-permute-done.18 = f32[4,40,128]{2,1,0:T(8,128)S(1)} collective-permute-done((f32[4,40,128]{2,1,0:T(8,128)S(1)}, f32[4,40,128]{2,1,0:T(8,128)S(1)}, u32[]{:S(2)}, u32[]{:S(2)}) %collective-permute-start.18) | collective-permute-done | bytes 81952 | tf_op jit(solution)/shard_map/ppermute | solution.py:472
  61.1 1.6 %collective-permute-start.21 = (f32[1,40,128]{2,1,0:T(8,128)S(1)}, f32[1,40,128]{2,1,0:T(8,128)S(1)}, u32[]{:S(2)}, u32[]{:S(2)}) collective-permute-start(f32[1,40,128]{2,1,0:T(8,128)S(1)} %get-tuple-element.70), channel_id=1, source_target_pairs={{0,6},{1,7},{2,4},{3,5},{4,2},{5,3},{6,0},{7,1},{8,14},{9,15},{10,... | collective-permute-start | bytes 61448 | tf_op jit(solution)/shard_map/ppermute | solution.py:472
  63.0 2.6 %collective-permute-start.19 = (f32[1,40,128]{2,1,0:T(8,128)S(1)}, f32[1,40,128]{2,1,0:T(8,128)S(1)}, u32[]{:S(2)}, u32[]{:S(2)}) collective-permute-start(f32[1,40,128]{2,1,0:T(8,128)S(1)} %get-tuple-element.72), channel_id=1, source_target_pairs={{0,2},{1,3},{2,0},{3,1},{4,6},{5,7},{6,4},{7,5},{8,10},{9,11},{10,... | collective-permute-start | bytes 61448 | tf_op jit(solution)/shard_map/ppermute | solution.py:472
  65.6 4.6 %shard_map.192 = f32[2,16,64,128]{3,2,1,0:T(8,128)} custom-call(f32[2,16,64,128]{3,2,1,0:T(8,128)S(1)} %get-tuple-element.46.dconv_in.inner, f32[2,3,64,128]{3,2,1,0:T(8,128)S(1)} %collective-permute-done.10.got_a.got_ra, f32[2,3,64,128]{3,2,1,0:T(8,128)S(1)} %collective-permute-done.11.got_b.got_rb, f32[2,22,4,128]{3,2,1,0:T(4,128)S(1)} %collective-permute-done.14.got_ca, ...), custom_call_target="tpu_custom_call" | custom-call | flops 4000000000 | bytes 4000000 | tf_op jit(solution)/shard_map/pallas_call | solution.py:622
  (38 shorter events, 7.0 us)
Async XLA Ops:
  0.6 15.6 %copy-start = (f32[2,16,64,128]{3,2,1,0:T(8,128)S(1)}, f32[2,16,64,128]{3,2,1,0:T(8,128)}, u32[]{:S(2)}) copy-start(f32[2,16,64,128]{3,2,1,0:T(8,128)} %feat.3) | copy-start | bytes 3145732
  2.7 13.0 %collective-permute-start = (f32[2,3,64,128]{3,2,1,0:T(8,128)}, f32[2,3,64,128]{3,2,1,0:T(8,128)S(1)}, u32[]{:S(2)}, u32[]{:S(2)}) collective-permute-start(f32[2,3,64,128]{3,2,1,0:T(8,128)} %get-tuple-element.40), channel_id=1, source_target_pairs={{0,8},{8,0},{16,24},{24,16},{1,9},{9,1},{17,25},{25,17},{2,10},{10... | collective-permute-start | bytes 589832 | tf_op jit(solution)/shard_map/ppermute | solution.py:86
  5.7 10.5 %collective-permute-start.1 = (f32[2,3,64,128]{3,2,1,0:T(8,128)}, f32[2,3,64,128]{3,2,1,0:T(8,128)S(1)}, u32[]{:S(2)}, u32[]{:S(2)}) collective-permute-start(f32[2,3,64,128]{3,2,1,0:T(8,128)} %get-tuple-element.41), channel_id=1, source_target_pairs={{0,24},{8,16},{16,8},{24,0},{1,25},{9,17},{17,9},{25,1},{2,26},{10... | collective-permute-start | bytes 589832 | tf_op jit(solution)/shard_map/ppermute | solution.py:86
  7.2 5.8 %collective-permute-start.4 = (f32[1,40,128]{2,1,0:T(8,128)}, f32[1,40,128]{2,1,0:T(8,128)S(1)}, u32[]{:S(2)}, u32[]{:S(2)}) collective-permute-start(f32[1,40,128]{2,1,0:T(8,128)} %bitcast.25), channel_id=1, source_target_pairs={{0,6},{1,7},{2,4},{3,5},{4,2},{5,3},{6,0},{7,1},{8,14},{9,15},{10,... | collective-permute-start | bytes 61448 | tf_op jit(solution)/shard_map/ppermute | solution.py:472
  10.8 4.9 %collective-permute-start.3 = (f32[1,40,128]{2,1,0:T(8,128)}, f32[1,40,128]{2,1,0:T(8,128)S(1)}, u32[]{:S(2)}, u32[]{:S(2)}) collective-permute-start(f32[1,40,128]{2,1,0:T(8,128)} %bitcast.26), channel_id=1, source_target_pairs={{0,4},{1,5},{2,6},{3,7},{4,0},{5,1},{6,2},{7,3},{8,12},{9,13},{10,... | collective-permute-start | bytes 61448 | tf_op jit(solution)/shard_map/ppermute | solution.py:472
  10.8 4.9 %collective-permute-start.2 = (f32[1,40,128]{2,1,0:T(8,128)}, f32[1,40,128]{2,1,0:T(8,128)S(1)}, u32[]{:S(2)}, u32[]{:S(2)}) collective-permute-start(f32[1,40,128]{2,1,0:T(8,128)} %bitcast.27), channel_id=1, source_target_pairs={{0,2},{1,3},{2,0},{3,1},{4,6},{5,7},{6,4},{7,5},{8,10},{9,11},{10,... | collective-permute-start | bytes 61448 | tf_op jit(solution)/shard_map/ppermute | solution.py:472
  17.0 11.6 %copy-start.2 = (f32[2,16,64,128]{3,2,1,0:T(8,128)S(1)}, f32[2,16,64,128]{3,2,1,0:T(8,128)}, u32[]{:S(2)}) copy-start(f32[2,16,64,128]{3,2,1,0:T(8,128)} %cot_ref.3) | copy-start | bytes 3145732
  17.1 9.6 %collective-permute-start.5 = (f32[2,22,4,128]{3,2,1,0:T(4,128)S(1)}, f32[2,22,4,128]{3,2,1,0:T(4,128)S(1)}, u32[]{:S(2)}, u32[]{:S(2)}) collective-permute-start(f32[2,22,4,128]{3,2,1,0:T(4,128)S(1)} %get-tuple-element.43), channel_id=1, source_target_pairs={{0,7},{1,2},{2,1},{3,4},{4,3},{5,6},{6,5},{7,0},{8,15},{9,10},{10,... | collective-permute-start | bytes 270344 | tf_op jit(solution)/shard_map/ppermute | solution.py:541
  19.3 6.2 %collective-permute-start.8 = (f32[4,40,128]{2,1,0:T(8,128)S(1)}, f32[4,40,128]{2,1,0:T(8,128)S(1)}, u32[]{:S(2)}, u32[]{:S(2)}) collective-permute-start(f32[4,40,128]{2,1,0:T(8,128)S(1)} %get-tuple-element.45.refs_0_), channel_id=1, source_target_pairs={{0,24},{1,25},{2,26},{3,27},{4,28},{5,29},{6,30},{7,31},{8,16},{9,... | collective-permute-start | bytes 245768 | tf_op jit(solution)/shard_map/ppermute | solution.py:472
  20.8 5.1 %collective-permute-start.7 = (f32[4,40,128]{2,1,0:T(8,128)S(1)}, f32[4,40,128]{2,1,0:T(8,128)S(1)}, u32[]{:S(2)}, u32[]{:S(2)}) collective-permute-start(f32[4,40,128]{2,1,0:T(8,128)S(1)} %get-tuple-element.45.refs_0_), channel_id=1, source_target_pairs={{0,16},{1,17},{2,18},{3,19},{4,20},{5,21},{6,22},{7,23},{8,24},{9,... | collective-permute-start | bytes 245768 | tf_op jit(solution)/shard_map/ppermute | solution.py:472
  22.3 4.4 %collective-permute-start.6 = (f32[4,40,128]{2,1,0:T(8,128)S(1)}, f32[4,40,128]{2,1,0:T(8,128)S(1)}, u32[]{:S(2)}, u32[]{:S(2)}) collective-permute-start(f32[4,40,128]{2,1,0:T(8,128)S(1)} %get-tuple-element.45.refs_0_), channel_id=1, source_target_pairs={{0,8},{1,9},{2,10},{3,11},{4,12},{5,13},{6,14},{7,15},{8,0},{9,1},... | collective-permute-start | bytes 245768 | tf_op jit(solution)/shard_map/ppermute | solution.py:472
  26.8 1.8 %collective-permute-start.9 = (f32[816,128]{1,0:T(8,128)S(1)}, f32[816,128]{1,0:T(8,128)S(1)}, u32[]{:S(2)}, u32[]{:S(2)}) collective-permute-start(f32[816,128]{1,0:T(8,128)S(1)} %shard_map.188.kept), channel_id=1, source_target_pairs={{0,1},{1,0},{2,3},{3,2},{4,5},{5,4},{6,7},{7,6},{8,9},{9,8},{10,11... | collective-permute-start | bytes 1253384 | tf_op jit(solution)/shard_map/ppermute | solution.py:472
  42.4 8.5 %collective-permute-start.10 = (f32[2,3,64,128]{3,2,1,0:T(8,128)S(1)}, f32[2,3,64,128]{3,2,1,0:T(8,128)S(1)}, u32[]{:S(2)}, u32[]{:S(2)}) collective-permute-start(f32[2,3,64,128]{3,2,1,0:T(8,128)S(1)} %get-tuple-element.47), channel_id=1, source_target_pairs={{0,8},{8,0},{16,24},{24,16},{1,9},{9,1},{17,25},{25,17},{2,10},{10... | collective-permute-start | bytes 589832 | tf_op jit(solution)/shard_map/ppermute | solution.py:86
  43.0 10.6 %collective-permute-start.11 = (f32[2,3,64,128]{3,2,1,0:T(8,128)S(1)}, f32[2,3,64,128]{3,2,1,0:T(8,128)S(1)}, u32[]{:S(2)}, u32[]{:S(2)}) collective-permute-start(f32[2,3,64,128]{3,2,1,0:T(8,128)S(1)} %get-tuple-element.48), channel_id=1, source_target_pairs={{0,24},{8,16},{16,8},{24,0},{1,25},{9,17},{17,9},{25,1},{2,26},{10... | collective-permute-start | bytes 589832 | tf_op jit(solution)/shard_map/ppermute | solution.py:86
  44.5 9.1 %collective-permute-start.12 = (f32[16,32,128]{2,1,0:T(8,128)S(1)}, f32[16,32,128]{2,1,0:T(8,128)S(1)}, u32[]{:S(2)}, u32[]{:S(2)}) collective-permute-start(f32[16,32,128]{2,1,0:T(8,128)S(1)} %slice.18), channel_id=1, source_target_pairs={{0,1},{1,0},{2,3},{3,2},{4,5},{5,4},{6,7},{7,6},{8,9},{9,8},{10,11... | collective-permute-start | bytes 786440 | tf_op jit(solution)/shard_map/ppermute | solution.py:472
  49.4 1.4 %collective-permute-start.13 = (f32[16,8,128]{2,1,0:T(8,128)S(1)}, f32[16,8,128]{2,1,0:T(8,128)S(1)}, u32[]{:S(2)}, u32[]{:S(2)}) collective-permute-start(f32[16,8,128]{2,1,0:T(8,128)S(1)} %slice.24), channel_id=1, source_target_pairs={{0,1},{1,0},{2,3},{3,2},{4,5},{5,4},{6,7},{7,6},{8,9},{9,8},{10,11... | collective-permute-start | bytes 196616 | tf_op jit(solution)/shard_map/ppermute | solution.py:472
  53.6 5.3 %collective-permute-start.16 = (f32[4,40,128]{2,1,0:T(8,128)S(1)}, f32[4,40,128]{2,1,0:T(8,128)S(1)}, u32[]{:S(2)}, u32[]{:S(2)}) collective-permute-start(f32[4,40,128]{2,1,0:T(8,128)S(1)} %get-tuple-element.58), channel_id=1, source_target_pairs={{0,8},{1,9},{2,10},{3,11},{4,12},{5,13},{6,14},{7,15},{8,0},{9,1},... | collective-permute-start | bytes 245768 | tf_op jit(solution)/shard_map/ppermute | solution.py:472
  54.4 5.3 %collective-permute-start.17 = (f32[4,40,128]{2,1,0:T(8,128)S(1)}, f32[4,40,128]{2,1,0:T(8,128)S(1)}, u32[]{:S(2)}, u32[]{:S(2)}) collective-permute-start(f32[4,40,128]{2,1,0:T(8,128)S(1)} %get-tuple-element.59), channel_id=1, source_target_pairs={{0,16},{1,17},{2,18},{3,19},{4,20},{5,21},{6,22},{7,23},{8,24},{9,... | collective-permute-start | bytes 245768 | tf_op jit(solution)/shard_map/ppermute | solution.py:472
  55.7 5.3 %collective-permute-start.18 = (f32[4,40,128]{2,1,0:T(8,128)S(1)}, f32[4,40,128]{2,1,0:T(8,128)S(1)}, u32[]{:S(2)}, u32[]{:S(2)}) collective-permute-start(f32[4,40,128]{2,1,0:T(8,128)S(1)} %get-tuple-element.60), channel_id=1, source_target_pairs={{0,24},{1,25},{2,26},{3,27},{4,28},{5,29},{6,30},{7,31},{8,16},{9,... | collective-permute-start | bytes 245768 | tf_op jit(solution)/shard_map/ppermute | solution.py:472
  57.2 8.4 %collective-permute-start.14 = (f32[2,22,4,128]{3,2,1,0:T(4,128)S(1)}, f32[2,22,4,128]{3,2,1,0:T(4,128)S(1)}, u32[]{:S(2)}, u32[]{:S(2)}) collective-permute-start(f32[2,22,4,128]{3,2,1,0:T(4,128)S(1)} %get-tuple-element.54), channel_id=1, source_target_pairs={{0,1},{1,0},{2,3},{3,2},{4,5},{5,4},{6,7},{7,6},{8,9},{9,8},{10,11... | collective-permute-start | bytes 270344 | tf_op jit(solution)/shard_map/ppermute | solution.py:86
  57.2 8.4 %collective-permute-start.15 = (f32[2,22,4,128]{3,2,1,0:T(4,128)S(1)}, f32[2,22,4,128]{3,2,1,0:T(4,128)S(1)}, u32[]{:S(2)}, u32[]{:S(2)}) collective-permute-start(f32[2,22,4,128]{3,2,1,0:T(4,128)S(1)} %get-tuple-element.55), channel_id=1, source_target_pairs={{0,7},{1,2},{2,1},{3,4},{4,3},{5,6},{6,5},{7,0},{8,15},{9,10},{10,... | collective-permute-start | bytes 270344 | tf_op jit(solution)/shard_map/ppermute | solution.py:86
  61.1 9.1 %collective-permute-start.21 = (f32[1,40,128]{2,1,0:T(8,128)S(1)}, f32[1,40,128]{2,1,0:T(8,128)S(1)}, u32[]{:S(2)}, u32[]{:S(2)}) collective-permute-start(f32[1,40,128]{2,1,0:T(8,128)S(1)} %get-tuple-element.70), channel_id=1, source_target_pairs={{0,6},{1,7},{2,4},{3,5},{4,2},{5,3},{6,0},{7,1},{8,14},{9,15},{10,... | collective-permute-start | bytes 61448 | tf_op jit(solution)/shard_map/ppermute | solution.py:472
  62.7 7.5 %collective-permute-start.20 = (f32[1,40,128]{2,1,0:T(8,128)S(1)}, f32[1,40,128]{2,1,0:T(8,128)S(1)}, u32[]{:S(2)}, u32[]{:S(2)}) collective-permute-start(f32[1,40,128]{2,1,0:T(8,128)S(1)} %get-tuple-element.71), channel_id=1, source_target_pairs={{0,4},{1,5},{2,6},{3,7},{4,0},{5,1},{6,2},{7,3},{8,12},{9,13},{10,... | collective-permute-start | bytes 61448 | tf_op jit(solution)/shard_map/ppermute | solution.py:472
  63.0 7.3 %collective-permute-start.19 = (f32[1,40,128]{2,1,0:T(8,128)S(1)}, f32[1,40,128]{2,1,0:T(8,128)S(1)}, u32[]{:S(2)}, u32[]{:S(2)}) collective-permute-start(f32[1,40,128]{2,1,0:T(8,128)S(1)} %get-tuple-element.72), channel_id=1, source_target_pairs={{0,2},{1,3},{2,0},{3,1},{4,6},{5,7},{6,4},{7,5},{8,10},{9,11},{10,... | collective-permute-start | bytes 61448 | tf_op jit(solution)/shard_map/ppermute | solution.py:472
  (1 other events, 0.7 us)

commit v5 on v4

--- a/solution.py
+++ b/solution.py
@@ -225,7 +225,7 @@
     ms, order, factor, taps_i, taps_j, tile,
     feat, got_ra, got_rb, got_cb, kept, got, cot_ref,
     src_out, dconv_ref, row_a, row_b, edge_a, edge_b, grads_ref, chan_ref, small_ref,
-    src_ref, conv_scr, cols_scr, kb_scr, win_scr, wout_scr, w1_scr, w2_scr, w4_scr, bias_scr,
+    src_ref, conv_scr, cols_scr, kb_scr, win_scr, wout_scr, w1_scr, w2_scr, w4_scr, bias_scr, bias_rows,
     gw1_scr, gw2_scr, gb_scr, gg_scr, gs_scr, gc_scr, cot_sum,
 ):
     batch, rows, cols, C = feat.shape
@@ -261,9 +261,10 @@
     for s in range(count):
         win_scr[s * hs : (s + 1) * hs, :] = read(s, 0, hs)
         wout_scr[s * hs : (s + 1) * hs, :] = read(s, hs, hs)
+        bias_rows[s : s + 1, :] = read(s, 2 * hs + cs, 1)
+    bias_columns = bias_rows[...].T
     for s in range(count):
-        cols_bias = jnp.broadcast_to(read(s, 2 * hs + cs, 1), (LANES, LANES)).T
-        bias_scr[s * hs : (s + 1) * hs, :] = cols_bias[0:hs, :]
+        bias_scr[s * hs : (s + 1) * hs, :] = jnp.broadcast_to(bias_columns[0:hs, s : s + 1], (hs, LANES))
 
     scale_row = rows_form[taps + 4 : taps + 5, :]
     wh, wl = split(win_scr[...])
@@ -575,6 +576,7 @@
             vm((hid, 3 * C), bf16),
             vm((2 * C, hid), bf16),
             vm((hid, LANES), f32),
+            vm((ceil8(max(count, LANES)), LANES), f32),
             vm((hid, 2 * C), f32),
             vm((hid, 2 * C), f32),
             vm((hid, LANES), f32),

time: 71.2 us -> 71.2 us (level)
  no operation moved by 1% of the time
where the time goes in v5:
time: 71.2 us; the launch traced here: 71 us
  starting transfers between devices  27 us (38%)
  Pallas kernels  26.3 us (37%)
  waiting for transfers between devices  16.2 us (23%)
  local copies, waits for them, and re-layouts  0.77 us (1%)
  between operations  0.74 us (1%)
    ppermute x15, starting transfers between devices, flip(): return lax.ppermute(x, AXES, [(i, i ^ mask) for i in range(count)])  16.6 us
    pallas_call x1, Pallas kernels, per_device(): call(functools.partial(mix_body, ms, order, factor, taps_i, taps_j, tile)...  13.8 us
    ppermute x15, waiting for transfers between devices, flip(): return lax.ppermute(x, AXES, [(i, i ^ mask) for i in range(count)])  12.9 us
    pallas_call x1, Pallas kernels, per_device(): call(functools.partial(kernel_grad_body, ms, order, factor, taps_i, taps_...  4.88 us
    pallas_call x1, Pallas kernels, per_device(): call(functools.partial(features_grad_body, ms, taps_i, taps_j), shape(bat...  4.64 us
    ppermute x3, starting transfers between devices, both_pairs(): lax.ppermute(b, axis, pairs(count, True))  4.56 us
    ppermute x3, starting transfers between devices, both_pairs(): lax.ppermute(a, axis, pairs(count, False))  3.6 us
    ppermute x3, waiting for transfers between devices, both_pairs(): lax.ppermute(b, axis, pairs(count, True))  3.21 us
  transfers between devices with their start and end apart: 22, of which 12 were waited for; matrix products, arithmetic and copies ran while one was open for 0% of the time, Pallas kernels for 13%

profile of v5, /device:TPU:0, one launch (start us, length us, event | category | flops | bytes accessed | tf_op | source)
XLA Modules:
  0.0 71.0 jit_solution(10993610357475395274)
XLA Ops:
  0.7 2.1 %shard_map.186 = (f32[40,128]{1,0:T(8,128)}, f32[2,3,64,128]{3,2,1,0:T(8,128)}, f32[2,3,64,128]{3,2,1,0:T(8,128)}) custom-call(f32[2,16,64,128]{3,2,1,0:T(8,128)} %feat.3, f32[7,4,7]{2,1,0:T(4,128)} %bitcast.29, f32[1,4]{1,0:T(1,128)} %bitcast.31, f32[1,4]{1,0:T(1,128)} %bitcast.32, f32[1,4]{1,0:T(1,128)} %bitcast.33, f32[1,4]{1,0:T(1,128)} %bitcast.34, ...), custom_call_target="tpu_custom_call" | custom-call | bytes 1000000 | tf_op jit(solution)/shard_map/pallas_call | solution.py:509
  2.7 3.0 %collective-permute-start = (f32[2,3,64,128]{3,2,1,0:T(8,128)}, f32[2,3,64,128]{3,2,1,0:T(8,128)S(1)}, u32[]{:S(2)}, u32[]{:S(2)}) collective-permute-start(f32[2,3,64,128]{3,2,1,0:T(8,128)} %get-tuple-element.40), channel_id=1, source_target_pairs={{0,8},{8,0},{16,24},{24,16},{1,9},{9,1},{17,25},{25,17},{2,10},{10... | collective-permute-start | bytes 589832 | tf_op jit(solution)/shard_map/ppermute | solution.py:86
  5.7 1.5 %collective-permute-start.1 = (f32[2,3,64,128]{3,2,1,0:T(8,128)}, f32[2,3,64,128]{3,2,1,0:T(8,128)S(1)}, u32[]{:S(2)}, u32[]{:S(2)}) collective-permute-start(f32[2,3,64,128]{3,2,1,0:T(8,128)} %get-tuple-element.41), channel_id=1, source_target_pairs={{0,24},{8,16},{16,8},{24,0},{1,25},{9,17},{17,9},{25,1},{2,26},{10... | collective-permute-start | bytes 589832 | tf_op jit(solution)/shard_map/ppermute | solution.py:86
  7.2 3.6 %collective-permute-start.4 = (f32[1,40,128]{2,1,0:T(8,128)}, f32[1,40,128]{2,1,0:T(8,128)S(1)}, u32[]{:S(2)}, u32[]{:S(2)}) collective-permute-start(f32[1,40,128]{2,1,0:T(8,128)} %bitcast.25), channel_id=1, source_target_pairs={{0,6},{1,7},{2,4},{3,5},{4,2},{5,3},{6,0},{7,1},{8,14},{9,15},{10,... | collective-permute-start | bytes 61448 | tf_op jit(solution)/shard_map/ppermute | solution.py:473
  11.6 1.5 %collective-permute-done.4.refs_3_ = f32[1,40,128]{2,1,0:T(8,128)S(1)} collective-permute-done((f32[1,40,128]{2,1,0:T(8,128)}, f32[1,40,128]{2,1,0:T(8,128)S(1)}, u32[]{:S(2)}, u32[]{:S(2)}) %collective-permute-start.4) | collective-permute-done | bytes 20512 | tf_op jit(solution)/shard_map/ppermute | solution.py:473
  13.1 2.7 %collective-permute-done.3.refs_2_ = f32[1,40,128]{2,1,0:T(8,128)S(1)} collective-permute-done((f32[1,40,128]{2,1,0:T(8,128)}, f32[1,40,128]{2,1,0:T(8,128)S(1)}, u32[]{:S(2)}, u32[]{:S(2)}) %collective-permute-start.3) | collective-permute-done | bytes 20512 | tf_op jit(solution)/shard_map/ppermute | solution.py:473
  17.1 2.2 %collective-permute-start.5 = (f32[2,22,4,128]{3,2,1,0:T(4,128)S(1)}, f32[2,22,4,128]{3,2,1,0:T(4,128)S(1)}, u32[]{:S(2)}, u32[]{:S(2)}) collective-permute-start(f32[2,22,4,128]{3,2,1,0:T(4,128)S(1)} %get-tuple-element.43), channel_id=1, source_target_pairs={{0,7},{1,2},{2,1},{3,4},{4,3},{5,6},{6,5},{7,0},{8,15},{9,10},{10,... | collective-permute-start | bytes 270344 | tf_op jit(solution)/shard_map/ppermute | solution.py:542
  19.3 1.4 %collective-permute-start.8 = (f32[4,40,128]{2,1,0:T(8,128)S(1)}, f32[4,40,128]{2,1,0:T(8,128)S(1)}, u32[]{:S(2)}, u32[]{:S(2)}) collective-permute-start(f32[4,40,128]{2,1,0:T(8,128)S(1)} %get-tuple-element.45.refs_0_), channel_id=1, source_target_pairs={{0,24},{1,25},{2,26},{3,27},{4,28},{5,29},{6,30},{7,31},{8,16},{9,... | collective-permute-start | bytes 245768 | tf_op jit(solution)/shard_map/ppermute | solution.py:473
  20.8 1.5 %collective-permute-start.7 = (f32[4,40,128]{2,1,0:T(8,128)S(1)}, f32[4,40,128]{2,1,0:T(8,128)S(1)}, u32[]{:S(2)}, u32[]{:S(2)}) collective-permute-start(f32[4,40,128]{2,1,0:T(8,128)S(1)} %get-tuple-element.45.refs_0_), channel_id=1, source_target_pairs={{0,16},{1,17},{2,18},{3,19},{4,20},{5,21},{6,22},{7,23},{8,24},{9,... | collective-permute-start | bytes 245768 | tf_op jit(solution)/shard_map/ppermute | solution.py:473
  22.8 2.7 %collective-permute-done.8.refs_3_ = f32[4,40,128]{2,1,0:T(8,128)S(1)} collective-permute-done((f32[4,40,128]{2,1,0:T(8,128)S(1)}, f32[4,40,128]{2,1,0:T(8,128)S(1)}, u32[]{:S(2)}, u32[]{:S(2)}) %collective-permute-start.8) | collective-permute-done | bytes 81952 | tf_op jit(solution)/shard_map/ppermute | solution.py:473
  25.8 0.9 %collective-permute-done.6.refs_1_ = f32[4,40,128]{2,1,0:T(8,128)S(1)} collective-permute-done((f32[4,40,128]{2,1,0:T(8,128)S(1)}, f32[4,40,128]{2,1,0:T(8,128)S(1)}, u32[]{:S(2)}, u32[]{:S(2)}) %collective-permute-start.6) | collective-permute-done | bytes 81952 | tf_op jit(solution)/shard_map/ppermute | solution.py:473
  26.8 1.7 %collective-permute-done.9.got = f32[816,128]{1,0:T(8,128)S(1)} collective-permute-done((f32[816,128]{1,0:T(8,128)S(1)}, f32[816,128]{1,0:T(8,128)S(1)}, u32[]{:S(2)}, u32[]{:S(2)}) %collective-permute-start.9) | collective-permute-done | bytes 417824 | tf_op jit(solution)/shard_map/ppermute | solution.py:473
  28.6 13.8 %shard_map.189 = (f32[2,22,80,128]{3,2,1,0:T(8,128)S(1)}, f32[2,16,64,128]{3,2,1,0:T(8,128)S(1)}, f32[2,3,64,128]{3,2,1,0:T(8,128)S(1)}, f32[2,3,64,128]{3,2,1,0...) custom-call(f32[2,16,64,128]{3,2,1,0:T(8,128)S(1)} %copy-done, ...), custom_call_target="tpu_custom_call" | custom-call | flops 12000000000 | bytes 8000000 | tf_op jit(solution)/shard_map/pallas_call | solution.py:557
  43.0 1.5 %collective-permute-start.11 = (f32[2,3,64,128]{3,2,1,0:T(8,128)S(1)}, f32[2,3,64,128]{3,2,1,0:T(8,128)S(1)}, u32[]{:S(2)}, u32[]{:S(2)}) collective-permute-start(f32[2,3,64,128]{3,2,1,0:T(8,128)S(1)} %get-tuple-element.48), channel_id=1, source_target_pairs={{0,24},{8,16},{16,8},{24,0},{1,25},{9,17},{17,9},{25,1},{2,26},{10... | collective-permute-start | bytes 589832 | tf_op jit(solution)/shard_map/ppermute | solution.py:86
  44.5 4.9 %shard_map.190.small = f32[32,8,128]{2,1,0:T(8,128)S(1)} custom-call(f32[2,22,80,128]{3,2,1,0:T(8,128)S(1)} %get-tuple-element.52.src_in, f32[2,16,64,128]{3,2,1,0:T(8,128)S(1)} %get-tuple-element.46.dconv_in.inner, f32[8,512]{1,0:T(8,128)S(1)} %get-tuple-element.53.chan_ref), custom_call_target="tpu_custom_call" | custom-call | flops 4000000000 | bytes 4000000 | tf_op jit(solution)/shard_map/pallas_call | solution.py:595
  50.0 0.9 %collective-permute-done.13.small_got = f32[16,8,128]{2,1,0:T(8,128)S(1)} collective-permute-done((f32[16,8,128]{2,1,0:T(8,128)S(1)}, f32[16,8,128]{2,1,0:T(8,128)S(1)}, u32[]{:S(2)}, u32[]{:S(2)}) %collective-permute-start.13) | collective-permute-done | bytes 65568 | tf_op jit(solution)/shard_map/ppermute | solution.py:473
  50.9 2.7 %collective-permute-done.11.got_b.got_rb = f32[2,3,64,128]{3,2,1,0:T(8,128)S(1)} collective-permute-done((f32[2,3,64,128]{3,2,1,0:T(8,128)S(1)}, f32[2,3,64,128]{3,2,1,0:T(8,128)S(1)}, u32[]{:S(2)}, u32[]{:S(2)}) %collective-permute-start.11) | collective-permute-done | bytes 196640 | tf_op jit(solution)/shard_map/ppermute | solution.py:86
  54.4 1.4 %collective-permute-start.17 = (f32[4,40,128]{2,1,0:T(8,128)S(1)}, f32[4,40,128]{2,1,0:T(8,128)S(1)}, u32[]{:S(2)}, u32[]{:S(2)}) collective-permute-start(f32[4,40,128]{2,1,0:T(8,128)S(1)} %get-tuple-element.59), channel_id=1, source_target_pairs={{0,16},{1,17},{2,18},{3,19},{4,20},{5,21},{6,22},{7,23},{8,24},{9,... | collective-permute-start | bytes 245768 | tf_op jit(solution)/shard_map/ppermute | solution.py:473
  55.7 1.5 %collective-permute-start.18 = (f32[4,40,128]{2,1,0:T(8,128)S(1)}, f32[4,40,128]{2,1,0:T(8,128)S(1)}, u32[]{:S(2)}, u32[]{:S(2)}) collective-permute-start(f32[4,40,128]{2,1,0:T(8,128)S(1)} %get-tuple-element.60), channel_id=1, source_target_pairs={{0,24},{1,25},{2,26},{3,27},{4,28},{5,29},{6,30},{7,31},{8,16},{9,... | collective-permute-start | bytes 245768 | tf_op jit(solution)/shard_map/ppermute | solution.py:473
  57.2 1.6 %collective-permute-start.15 = (f32[2,22,4,128]{3,2,1,0:T(4,128)S(1)}, f32[2,22,4,128]{3,2,1,0:T(4,128)S(1)}, u32[]{:S(2)}, u32[]{:S(2)}) collective-permute-start(f32[2,22,4,128]{3,2,1,0:T(4,128)S(1)} %get-tuple-element.55), channel_id=1, source_target_pairs={{0,7},{1,2},{2,1},{3,4},{4,3},{5,6},{6,5},{7,0},{8,15},{9,10},{10,... | collective-permute-start | bytes 270344 | tf_op jit(solution)/shard_map/ppermute | solution.py:86
  59.7 1.4 %collective-permute-done.18 = f32[4,40,128]{2,1,0:T(8,128)S(1)} collective-permute-done((f32[4,40,128]{2,1,0:T(8,128)S(1)}, f32[4,40,128]{2,1,0:T(8,128)S(1)}, u32[]{:S(2)}, u32[]{:S(2)}) %collective-permute-start.18) | collective-permute-done | bytes 81952 | tf_op jit(solution)/shard_map/ppermute | solution.py:473
  61.1 1.6 %collective-permute-start.21 = (f32[1,40,128]{2,1,0:T(8,128)S(1)}, f32[1,40,128]{2,1,0:T(8,128)S(1)}, u32[]{:S(2)}, u32[]{:S(2)}) collective-permute-start(f32[1,40,128]{2,1,0:T(8,128)S(1)} %get-tuple-element.70), channel_id=1, source_target_pairs={{0,6},{1,7},{2,4},{3,5},{4,2},{5,3},{6,0},{7,1},{8,14},{9,15},{10,... | collective-permute-start | bytes 61448 | tf_op jit(solution)/shard_map/ppermute | solution.py:473
  63.0 2.6 %collective-permute-start.19 = (f32[1,40,128]{2,1,0:T(8,128)S(1)}, f32[1,40,128]{2,1,0:T(8,128)S(1)}, u32[]{:S(2)}, u32[]{:S(2)}) collective-permute-start(f32[1,40,128]{2,1,0:T(8,128)S(1)} %get-tuple-element.72), channel_id=1, source_target_pairs={{0,2},{1,3},{2,0},{3,1},{4,6},{5,7},{6,4},{7,5},{8,10},{9,11},{10,... | collective-permute-start | bytes 61448 | tf_op jit(solution)/shard_map/ppermute | solution.py:473
  65.6 4.6 %shard_map.192 = f32[2,16,64,128]{3,2,1,0:T(8,128)} custom-call(f32[2,16,64,128]{3,2,1,0:T(8,128)S(1)} %get-tuple-element.46.dconv_in.inner, f32[2,3,64,128]{3,2,1,0:T(8,128)S(1)} %collective-permute-done.10.got_a.got_ra, f32[2,3,64,128]{3,2,1,0:T(8,128)S(1)} %collective-permute-done.11.got_b.got_rb, f32[2,22,4,128]{3,2,1,0:T(4,128)S(1)} %collective-permute-done.14.got_ca, ...), custom_call_target="tpu_custom_call" | custom-call | flops 4000000000 | bytes 4000000 | tf_op jit(solution)/shard_map/pallas_call | solution.py:624
  (38 shorter events, 7.1 us)
Async XLA Ops:
  0.6 15.6 %copy-start = (f32[2,16,64,128]{3,2,1,0:T(8,128)S(1)}, f32[2,16,64,128]{3,2,1,0:T(8,128)}, u32[]{:S(2)}) copy-start(f32[2,16,64,128]{3,2,1,0:T(8,128)} %feat.3) | copy-start | bytes 3145732
  2.7 13.0 %collective-permute-start = (f32[2,3,64,128]{3,2,1,0:T(8,128)}, f32[2,3,64,128]{3,2,1,0:T(8,128)S(1)}, u32[]{:S(2)}, u32[]{:S(2)}) collective-permute-start(f32[2,3,64,128]{3,2,1,0:T(8,128)} %get-tuple-element.40), channel_id=1, source_target_pairs={{0,8},{8,0},{16,24},{24,16},{1,9},{9,1},{17,25},{25,17},{2,10},{10... | collective-permute-start | bytes 589832 | tf_op jit(solution)/shard_map/ppermute | solution.py:86
  5.7 10.5 %collective-permute-start.1 = (f32[2,3,64,128]{3,2,1,0:T(8,128)}, f32[2,3,64,128]{3,2,1,0:T(8,128)S(1)}, u32[]{:S(2)}, u32[]{:S(2)}) collective-permute-start(f32[2,3,64,128]{3,2,1,0:T(8,128)} %get-tuple-element.41), channel_id=1, source_target_pairs={{0,24},{8,16},{16,8},{24,0},{1,25},{9,17},{17,9},{25,1},{2,26},{10... | collective-permute-start | bytes 589832 | tf_op jit(solution)/shard_map/ppermute | solution.py:86
  7.2 5.8 %collective-permute-start.4 = (f32[1,40,128]{2,1,0:T(8,128)}, f32[1,40,128]{2,1,0:T(8,128)S(1)}, u32[]{:S(2)}, u32[]{:S(2)}) collective-permute-start(f32[1,40,128]{2,1,0:T(8,128)} %bitcast.25), channel_id=1, source_target_pairs={{0,6},{1,7},{2,4},{3,5},{4,2},{5,3},{6,0},{7,1},{8,14},{9,15},{10,... | collective-permute-start | bytes 61448 | tf_op jit(solution)/shard_map/ppermute | solution.py:473
  10.8 4.9 %collective-permute-start.3 = (f32[1,40,128]{2,1,0:T(8,128)}, f32[1,40,128]{2,1,0:T(8,128)S(1)}, u32[]{:S(2)}, u32[]{:S(2)}) collective-permute-start(f32[1,40,128]{2,1,0:T(8,128)} %bitcast.26), channel_id=1, source_target_pairs={{0,4},{1,5},{2,6},{3,7},{4,0},{5,1},{6,2},{7,3},{8,12},{9,13},{10,... | collective-permute-start | bytes 61448 | tf_op jit(solution)/shard_map/ppermute | solution.py:473
  10.8 4.9 %collective-permute-start.2 = (f32[1,40,128]{2,1,0:T(8,128)}, f32[1,40,128]{2,1,0:T(8,128)S(1)}, u32[]{:S(2)}, u32[]{:S(2)}) collective-permute-start(f32[1,40,128]{2,1,0:T(8,128)} %bitcast.27), channel_id=1, source_target_pairs={{0,2},{1,3},{2,0},{3,1},{4,6},{5,7},{6,4},{7,5},{8,10},{9,11},{10,... | collective-permute-start | bytes 61448 | tf_op jit(solution)/shard_map/ppermute | solution.py:473
  17.0 11.6 %copy-start.2 = (f32[2,16,64,128]{3,2,1,0:T(8,128)S(1)}, f32[2,16,64,128]{3,2,1,0:T(8,128)}, u32[]{:S(2)}) copy-start(f32[2,16,64,128]{3,2,1,0:T(8,128)} %cot_ref.3) | copy-start | bytes 3145732
  17.1 9.6 %collective-permute-start.5 = (f32[2,22,4,128]{3,2,1,0:T(4,128)S(1)}, f32[2,22,4,128]{3,2,1,0:T(4,128)S(1)}, u32[]{:S(2)}, u32[]{:S(2)}) collective-permute-start(f32[2,22,4,128]{3,2,1,0:T(4,128)S(1)} %get-tuple-element.43), channel_id=1, source_target_pairs={{0,7},{1,2},{2,1},{3,4},{4,3},{5,6},{6,5},{7,0},{8,15},{9,10},{10,... | collective-permute-start | bytes 270344 | tf_op jit(solution)/shard_map/ppermute | solution.py:542
  19.3 6.2 %collective-permute-start.8 = (f32[4,40,128]{2,1,0:T(8,128)S(1)}, f32[4,40,128]{2,1,0:T(8,128)S(1)}, u32[]{:S(2)}, u32[]{:S(2)}) collective-permute-start(f32[4,40,128]{2,1,0:T(8,128)S(1)} %get-tuple-element.45.refs_0_), channel_id=1, source_target_pairs={{0,24},{1,25},{2,26},{3,27},{4,28},{5,29},{6,30},{7,31},{8,16},{9,... | collective-permute-start | bytes 245768 | tf_op jit(solution)/shard_map/ppermute | solution.py:473
  20.8 5.1 %collective-permute-start.7 = (f32[4,40,128]{2,1,0:T(8,128)S(1)}, f32[4,40,128]{2,1,0:T(8,128)S(1)}, u32[]{:S(2)}, u32[]{:S(2)}) collective-permute-start(f32[4,40,128]{2,1,0:T(8,128)S(1)} %get-tuple-element.45.refs_0_), channel_id=1, source_target_pairs={{0,16},{1,17},{2,18},{3,19},{4,20},{5,21},{6,22},{7,23},{8,24},{9,... | collective-permute-start | bytes 245768 | tf_op jit(solution)/shard_map/ppermute | solution.py:473
  22.3 4.4 %collective-permute-start.6 = (f32[4,40,128]{2,1,0:T(8,128)S(1)}, f32[4,40,128]{2,1,0:T(8,128)S(1)}, u32[]{:S(2)}, u32[]{:S(2)}) collective-permute-start(f32[4,40,128]{2,1,0:T(8,128)S(1)} %get-tuple-element.45.refs_0_), channel_id=1, source_target_pairs={{0,8},{1,9},{2,10},{3,11},{4,12},{5,13},{6,14},{7,15},{8,0},{9,1},... | collective-permute-start | bytes 245768 | tf_op jit(solution)/shard_map/ppermute | solution.py:473
  26.8 1.8 %collective-permute-start.9 = (f32[816,128]{1,0:T(8,128)S(1)}, f32[816,128]{1,0:T(8,128)S(1)}, u32[]{:S(2)}, u32[]{:S(2)}) collective-permute-start(f32[816,128]{1,0:T(8,128)S(1)} %shard_map.188.kept), channel_id=1, source_target_pairs={{0,1},{1,0},{2,3},{3,2},{4,5},{5,4},{6,7},{7,6},{8,9},{9,8},{10,11... | collective-permute-start | bytes 1253384 | tf_op jit(solution)/shard_map/ppermute | solution.py:473
  42.4 8.5 %collective-permute-start.10 = (f32[2,3,64,128]{3,2,1,0:T(8,128)S(1)}, f32[2,3,64,128]{3,2,1,0:T(8,128)S(1)}, u32[]{:S(2)}, u32[]{:S(2)}) collective-permute-start(f32[2,3,64,128]{3,2,1,0:T(8,128)S(1)} %get-tuple-element.47), channel_id=1, source_target_pairs={{0,8},{8,0},{16,24},{24,16},{1,9},{9,1},{17,25},{25,17},{2,10},{10... | collective-permute-start | bytes 589832 | tf_op jit(solution)/shard_map/ppermute | solution.py:86
  43.0 10.6 %collective-permute-start.11 = (f32[2,3,64,128]{3,2,1,0:T(8,128)S(1)}, f32[2,3,64,128]{3,2,1,0:T(8,128)S(1)}, u32[]{:S(2)}, u32[]{:S(2)}) collective-permute-start(f32[2,3,64,128]{3,2,1,0:T(8,128)S(1)} %get-tuple-element.48), channel_id=1, source_target_pairs={{0,24},{8,16},{16,8},{24,0},{1,25},{9,17},{17,9},{25,1},{2,26},{10... | collective-permute-start | bytes 589832 | tf_op jit(solution)/shard_map/ppermute | solution.py:86
  44.4 9.1 %collective-permute-start.12 = (f32[16,32,128]{2,1,0:T(8,128)S(1)}, f32[16,32,128]{2,1,0:T(8,128)S(1)}, u32[]{:S(2)}, u32[]{:S(2)}) collective-permute-start(f32[16,32,128]{2,1,0:T(8,128)S(1)} %slice.18), channel_id=1, source_target_pairs={{0,1},{1,0},{2,3},{3,2},{4,5},{5,4},{6,7},{7,6},{8,9},{9,8},{10,11... | collective-permute-start | bytes 786440 | tf_op jit(solution)/shard_map/ppermute | solution.py:473
  49.4 1.5 %collective-permute-start.13 = (f32[16,8,128]{2,1,0:T(8,128)S(1)}, f32[16,8,128]{2,1,0:T(8,128)S(1)}, u32[]{:S(2)}, u32[]{:S(2)}) collective-permute-start(f32[16,8,128]{2,1,0:T(8,128)S(1)} %slice.24), channel_id=1, source_target_pairs={{0,1},{1,0},{2,3},{3,2},{4,5},{5,4},{6,7},{7,6},{8,9},{9,8},{10,11... | collective-permute-start | bytes 196616 | tf_op jit(solution)/shard_map/ppermute | solution.py:473
  53.6 5.3 %collective-permute-start.16 = (f32[4,40,128]{2,1,0:T(8,128)S(1)}, f32[4,40,128]{2,1,0:T(8,128)S(1)}, u32[]{:S(2)}, u32[]{:S(2)}) collective-permute-start(f32[4,40,128]{2,1,0:T(8,128)S(1)} %get-tuple-element.58), channel_id=1, source_target_pairs={{0,8},{1,9},{2,10},{3,11},{4,12},{5,13},{6,14},{7,15},{8,0},{9,1},... | collective-permute-start | bytes 245768 | tf_op jit(solution)/shard_map/ppermute | solution.py:473
  54.4 5.3 %collective-permute-start.17 = (f32[4,40,128]{2,1,0:T(8,128)S(1)}, f32[4,40,128]{2,1,0:T(8,128)S(1)}, u32[]{:S(2)}, u32[]{:S(2)}) collective-permute-start(f32[4,40,128]{2,1,0:T(8,128)S(1)} %get-tuple-element.59), channel_id=1, source_target_pairs={{0,16},{1,17},{2,18},{3,19},{4,20},{5,21},{6,22},{7,23},{8,24},{9,... | collective-permute-start | bytes 245768 | tf_op jit(solution)/shard_map/ppermute | solution.py:473
  55.7 5.3 %collective-permute-start.18 = (f32[4,40,128]{2,1,0:T(8,128)S(1)}, f32[4,40,128]{2,1,0:T(8,128)S(1)}, u32[]{:S(2)}, u32[]{:S(2)}) collective-permute-start(f32[4,40,128]{2,1,0:T(8,128)S(1)} %get-tuple-element.60), channel_id=1, source_target_pairs={{0,24},{1,25},{2,26},{3,27},{4,28},{5,29},{6,30},{7,31},{8,16},{9,... | collective-permute-start | bytes 245768 | tf_op jit(solution)/shard_map/ppermute | solution.py:473
  57.2 8.4 %collective-permute-start.14 = (f32[2,22,4,128]{3,2,1,0:T(4,128)S(1)}, f32[2,22,4,128]{3,2,1,0:T(4,128)S(1)}, u32[]{:S(2)}, u32[]{:S(2)}) collective-permute-start(f32[2,22,4,128]{3,2,1,0:T(4,128)S(1)} %get-tuple-element.54), channel_id=1, source_target_pairs={{0,1},{1,0},{2,3},{3,2},{4,5},{5,4},{6,7},{7,6},{8,9},{9,8},{10,11... | collective-permute-start | bytes 270344 | tf_op jit(solution)/shard_map/ppermute | solution.py:86
  57.2 8.4 %collective-permute-start.15 = (f32[2,22,4,128]{3,2,1,0:T(4,128)S(1)}, f32[2,22,4,128]{3,2,1,0:T(4,128)S(1)}, u32[]{:S(2)}, u32[]{:S(2)}) collective-permute-start(f32[2,22,4,128]{3,2,1,0:T(4,128)S(1)} %get-tuple-element.55), channel_id=1, source_target_pairs={{0,7},{1,2},{2,1},{3,4},{4,3},{5,6},{6,5},{7,0},{8,15},{9,10},{10,... | collective-permute-start | bytes 270344 | tf_op jit(solution)/shard_map/ppermute | solution.py:86
  61.1 9.1 %collective-permute-start.21 = (f32[1,40,128]{2,1,0:T(8,128)S(1)}, f32[1,40,128]{2,1,0:T(8,128)S(1)}, u32[]{:S(2)}, u32[]{:S(2)}) collective-permute-start(f32[1,40,128]{2,1,0:T(8,128)S(1)} %get-tuple-element.70), channel_id=1, source_target_pairs={{0,6},{1,7},{2,4},{3,5},{4,2},{5,3},{6,0},{7,1},{8,14},{9,15},{10,... | collective-permute-start | bytes 61448 | tf_op jit(solution)/shard_map/ppermute | solution.py:473
  62.7 7.5 %collective-permute-start.20 = (f32[1,40,128]{2,1,0:T(8,128)S(1)}, f32[1,40,128]{2,1,0:T(8,128)S(1)}, u32[]{:S(2)}, u32[]{:S(2)}) collective-permute-start(f32[1,40,128]{2,1,0:T(8,128)S(1)} %get-tuple-element.71), channel_id=1, source_target_pairs={{0,4},{1,5},{2,6},{3,7},{4,0},{5,1},{6,2},{7,3},{8,12},{9,13},{10,... | collective-permute-start | bytes 61448 | tf_op jit(solution)/shard_map/ppermute | solution.py:473
  63.0 7.3 %collective-permute-start.19 = (f32[1,40,128]{2,1,0:T(8,128)S(1)}, f32[1,40,128]{2,1,0:T(8,128)S(1)}, u32[]{:S(2)}, u32[]{:S(2)}) collective-permute-start(f32[1,40,128]{2,1,0:T(8,128)S(1)} %get-tuple-element.72), channel_id=1, source_target_pairs={{0,2},{1,3},{2,0},{3,1},{4,6},{5,7},{6,4},{7,5},{8,10},{9,11},{10,... | collective-permute-start | bytes 61448 | tf_op jit(solution)/shard_map/ppermute | solution.py:473
  (1 other events, 0.7 us)
